TPU v7x, 32 devices: a whole 2x2x4 slice. The times are simulated.
32 devices in a mesh: stream: 2 (over core), dp: 16 (over z, y, x).
Axes of the slice: x: 2, y: 2, z: 4, core: 2. Of those that a mesh axis runs over, the one named last changes fastest.
Arguments:
- embedded: bfloat16 [2, 16384, 768], P('stream', 'dp'), may hold values from -6 to 6
- seq_cotangent: bfloat16 [2, 16384, 768], P('stream', 'dp'), may hold values from -6 to 6
- pair_ids: int32 [256], replicated, may hold values from 0 to 108
- w_qkv: bfloat16 [768, 2304], replicated, may hold values from -0.21875 to 0.21875
- b_qv: float32 [1536], replicated, may hold values from -3 to 3
- w_out: bfloat16 [768, 768], replicated, may hold values from -1.75 to 1.75
- b_out: float32 [768], replicated, may hold values from -1.75 to 1.75
- ln1_gain: float32 [768], replicated, may hold values from 0.5 to 1.5
- ln1_bias: float32 [768], replicated, may hold values from -1.75 to 1.75
- w_in: bfloat16 [768, 3072], replicated, may hold values from -0.21875 to 0.21875
- b_in: float32 [3072], replicated, may hold values from -3 to 3
- w_down: bfloat16 [3072, 768], replicated, may hold values from -0.109375 to 0.109375
- b_down: float32 [768], replicated, may hold values from -1.75 to 1.75
- ln2_gain: float32 [768], replicated, may hold values from 0.5 to 1.5
- ln2_bias: float32 [768], replicated, may hold values from -1.75 to 1.75
- w_pool: bfloat16 [768, 768], replicated, may hold values from -0.21875 to 0.21875
- b_pool: float32 [768], replicated, may hold values from -3 to 3
Outputs:
- encoded: bfloat16 [2, 16384, 768], P('stream', 'dp')
- input_grad: bfloat16 [2, 16384, 768], P('stream', 'dp')
- grad_w_qkv: float32 [768, 2304], replicated
- grad_b_qv: float32 [1536], replicated
- grad_w_out: float32 [768, 768], replicated
- grad_b_out: float32 [768], replicated
- grad_ln1_gain: float32 [768], replicated
- grad_ln1_bias: float32 [768], replicated
- grad_w_in: float32 [768, 3072], replicated
- grad_b_in: float32 [3072], replicated
- grad_w_down: float32 [3072, 768], replicated
- grad_b_down: float32 [768], replicated
- grad_ln2_gain: float32 [768], replicated
- grad_ln2_bias: float32 [768], replicated
- grad_w_pool: float32 [768, 768], replicated
- grad_b_pool: float32 [768], replicated
All inputs are finite; a program needn't handle non-finite values.
Results may differ from a plain program's by a relative error of at most 0.029.
Values may be sent and summed in bfloat16 or wider, within the bound.
No kernel may reach another device: no remote copies, remote signals or barrier semaphores. Data moves between devices by JAX's collectives and lax.ppermute only.
A program may use at most 256 MiB of HBM per device.

v0:
```python
import math

import jax
import jax.numpy as jnp
from jax import lax
from jax.sharding import PartitionSpec as P

HEADS = 12
HEAD_DIM = 64
SEQ = 64


epsilon = 1e-06
score_scale = 10.0
margin_shift = score_scale * 0.3
root_half = 0.7071067811865476
gauss_norm = 0.3989422804014327


def from_partner(x, axis, distance):
    return lax.ppermute(x, axis, [(i, i ^ 1 << distance) for i in range(lax.axis_size(axis))])


def narrow(array):
    return array.astype(jnp.bfloat16)


def mat_mul(inputs, matrix):
    return jnp.dot(inputs, matrix, preferred_element_type=jnp.float32)


def trans_left(inputs, matrix):
    return lax.dot_general(
        inputs, matrix, (((0,), (0,)), ((), ())), preferred_element_type=jnp.float32
    )


def trans_right(inputs, matrix):
    return lax.dot_general(
        inputs, matrix, (((1,), (1,)), ((), ())), preferred_element_type=jnp.float32
    )


def norm_forward(hidden, gain_row, bias_row):
    center = hidden - jnp.mean(hidden, axis=-1, keepdims=True)
    variance = jnp.mean(center * center, axis=-1, keepdims=True)
    inv_std = lax.rsqrt(variance + epsilon)
    normed = center * inv_std
    return (normed * gain_row + bias_row, normed, inv_std)


def norm_backward(grad_out, normed, inv_std, gain_row):
    grad_norm = grad_out * gain_row
    grad_in = inv_std * (
        grad_norm
        - jnp.mean(grad_norm, axis=-1, keepdims=True)
        - normed * jnp.mean(grad_norm * normed, axis=-1, keepdims=True)
    )
    return (grad_in, jnp.sum(grad_out * normed, axis=0), jnp.sum(grad_out, axis=0))


def gelu_slope(gate_in):
    return (
        0.5 * (1.0 + lax.erf(gate_in * root_half))
        + gate_in * jnp.exp(-0.5 * gate_in * gate_in) * gauss_norm
    )


def attention_scores(queries, key_rows, head_scale):
    return (
        jnp.einsum("slhd,smhd->shlm", queries, key_rows, preferred_element_type=jnp.float32)
        * head_scale
    )


def pad_rows(vector, group_size):
    length = vector.shape[0]
    filler = jnp.zeros((-length % group_size,), jnp.float32)
    return jnp.concatenate([vector, filler]).reshape(group_size, -1)


def shards(
    embedded,
    seq_cotangent,
    pair_ids,
    w_qkv,
    b_qv,
    w_out,
    b_out,
    ln1_gain,
    ln1_bias,
    w_in,
    b_in,
    w_down,
    b_down,
    ln2_gain,
    ln2_bias,
    w_pool,
    b_pool,
):
    tokens = embedded[0]
    model_width = tokens.shape[1]
    sent_dev = tokens.shape[0] // SEQ
    ffn_width = w_in.shape[1]
    head_scale = 1.0 / math.sqrt(HEAD_DIM)
    group_size = lax.axis_size("stream") * lax.axis_size("dp")
    qkv_bias = jnp.concatenate(
        [b_qv[:model_width], jnp.zeros((model_width,), jnp.float32), b_qv[model_width:]]
    )
    projected = narrow(mat_mul(tokens, w_qkv) + qkv_bias)
    head_view = projected.reshape(sent_dev, SEQ, 3, HEADS, HEAD_DIM)
    queries = head_view[:, :, 0]
    key_rows = head_view[:, :, 1]
    value_rows = head_view[:, :, 2]
    scores = attention_scores(queries, key_rows, head_scale)
    score_max = jnp.max(scores, axis=-1, keepdims=True)
    log_total = score_max + jnp.log(jnp.sum(jnp.exp(scores - score_max), axis=-1, keepdims=True))
    probs = jnp.exp(scores - log_total)
    context = narrow(
        jnp.einsum("shlm,smhd->slhd", narrow(probs), value_rows, preferred_element_type=jnp.float32)
    )
    context = context.reshape(sent_dev * SEQ, model_width)
    attn_out = mat_mul(context, w_out) + b_out
    hidden, normed_one, inv_one = norm_forward(
        tokens.astype(jnp.float32) + attn_out, ln1_gain, ln1_bias
    )
    hidden_low = narrow(hidden)
    gate_in = mat_mul(hidden_low, w_in) + b_in
    act_low = narrow(jax.nn.gelu(gate_in, approximate=False))
    ffn_out = mat_mul(act_low, w_down) + b_down
    block_out, normed_two, inv_two = norm_forward(hidden + ffn_out, ln2_gain, ln2_bias)
    first_low = narrow(block_out.reshape(sent_dev, SEQ, model_width)[:, 0])
    pooled = jnp.tanh(mat_mul(first_low, w_pool) + b_pool)
    inv_len = lax.rsqrt(jnp.sum(pooled * pooled, axis=-1, keepdims=True) + epsilon)
    unit_rows = pooled * inv_len
    embed_low = narrow(unit_rows)
    partner = from_partner(embed_low, "stream", 0)
    opposite = lax.all_gather(partner, "dp", axis=0, tiled=True)
    total_sent = opposite.shape[0]
    own_start = lax.axis_index("dp") * sent_dev
    own_index = own_start + jnp.arange(sent_dev, dtype=jnp.int32)
    column_ids = jnp.arange(total_sent, dtype=jnp.int32)
    own_pairs = lax.dynamic_slice_in_dim(pair_ids, own_start, sent_dev)
    same_pair = own_pairs[:, None] == pair_ids[None, :]
    positive = (own_index[:, None] == column_ids[None, :]).astype(jnp.float32)
    cosine = trans_right(embed_low, opposite)
    logits = score_scale * cosine - margin_shift * positive
    masked = jnp.where(same_pair, logits, -jnp.inf)
    row_max = jnp.max(masked, axis=-1, keepdims=True)
    row_exp = jnp.exp(masked - row_max)
    row_soft = row_exp / jnp.sum(row_exp, axis=-1, keepdims=True)
    grad_cos = narrow(score_scale * (row_soft - positive))
    grad_own = mat_mul(grad_cos, opposite)
    summed_back = lax.psum_scatter(
        trans_left(grad_cos, embed_low), "dp", scatter_dimension=0, tiled=True
    )
    grad_remote = from_partner(summed_back.astype(jnp.bfloat16), "stream", 0).astype(
        summed_back.dtype
    )
    grad_embed = grad_own + grad_remote
    grad_pooled = inv_len * (
        grad_embed - unit_rows * jnp.sum(unit_rows * grad_embed, axis=-1, keepdims=True)
    )
    grad_pre = grad_pooled * (1.0 - pooled * pooled)
    grad_b_pool = jnp.sum(grad_pre, axis=0)
    pre_low = narrow(grad_pre)
    grad_w_pool = trans_left(first_low, pre_low)
    grad_first = trans_right(pre_low, w_pool)
    grad_block = seq_cotangent[0].astype(jnp.float32).reshape(sent_dev, SEQ, model_width)
    grad_block = jnp.concatenate(
        [grad_block[:, :1] + grad_first[:, None], grad_block[:, 1:]], axis=1
    )
    grad_block = grad_block.reshape(sent_dev * SEQ, model_width)
    grad_sum_two, grad_ln2_gain, grad_ln2_bias = norm_backward(
        grad_block, normed_two, inv_two, ln2_gain
    )
    grad_b_down = jnp.sum(grad_sum_two, axis=0)
    grad_ffn_low = narrow(grad_sum_two)
    grad_w_down = trans_left(act_low, grad_ffn_low)
    grad_gate = trans_right(grad_ffn_low, w_down) * gelu_slope(gate_in)
    grad_b_in = jnp.sum(grad_gate, axis=0)
    grad_gate_low = narrow(grad_gate)
    grad_w_in = trans_left(hidden_low, grad_gate_low)
    grad_hidden = grad_sum_two + trans_right(grad_gate_low, w_in)
    upper_small = pad_rows(
        jnp.concatenate([grad_b_pool, grad_ln2_gain, grad_ln2_bias, grad_b_down, grad_b_in]),
        group_size,
    )
    grad_sum_one, grad_ln1_gain, grad_ln1_bias = norm_backward(
        grad_hidden, normed_one, inv_one, ln1_gain
    )
    grad_b_out = jnp.sum(grad_sum_one, axis=0)
    grad_attn_low = narrow(grad_sum_one)
    grad_w_out = trans_left(context, grad_attn_low)
    grad_context = narrow(trans_right(grad_attn_low, w_out)).reshape(sent_dev, SEQ, HEADS, HEAD_DIM)
    again_scores = attention_scores(queries, key_rows, head_scale)
    again_probs = jnp.exp(again_scores - log_total)
    grad_probs = jnp.einsum(
        "slhd,smhd->shlm", grad_context, value_rows, preferred_element_type=jnp.float32
    )
    grad_values = jnp.einsum(
        "shlm,slhd->smhd", narrow(again_probs), grad_context, preferred_element_type=jnp.float32
    )
    grad_scores = narrow(
        again_probs * (grad_probs - jnp.sum(grad_probs * again_probs, axis=-1, keepdims=True))
    )
    grad_queries = (
        jnp.einsum("shlm,smhd->slhd", grad_scores, key_rows, preferred_element_type=jnp.float32)
        * head_scale
    )
    grad_keys = (
        jnp.einsum("shlm,slhd->smhd", grad_scores, queries, preferred_element_type=jnp.float32)
        * head_scale
    )
    grad_proj = jnp.stack([grad_queries, grad_keys, grad_values], axis=2).reshape(
        sent_dev * SEQ, 3 * model_width
    )
    bias_sums = jnp.sum(grad_proj, axis=0)
    grad_b_qv = jnp.concatenate([bias_sums[:model_width], bias_sums[2 * model_width :]])
    grad_proj_low = narrow(grad_proj)
    grad_w_qkv = trans_left(tokens, grad_proj_low)
    grad_input = grad_sum_one + trans_right(grad_proj_low, w_qkv)
    lower_small = pad_rows(
        jnp.concatenate([grad_b_qv, grad_b_out, grad_ln1_gain, grad_ln1_bias]), group_size
    )
    summed = (
        lax.psum_scatter(
            grad_w_pool.reshape(group_size, -1), ("stream", "dp"), scatter_dimension=0, tiled=True
        ),
        lax.psum_scatter(
            grad_w_down.reshape(group_size, -1), ("stream", "dp"), scatter_dimension=0, tiled=True
        ),
        lax.psum_scatter(
            grad_w_in.reshape(group_size, -1), ("stream", "dp"), scatter_dimension=0, tiled=True
        ),
        lax.psum_scatter(upper_small, ("stream", "dp"), scatter_dimension=0, tiled=True),
        lax.psum_scatter(
            grad_w_qkv.reshape(group_size, -1), ("stream", "dp"), scatter_dimension=0, tiled=True
        ),
        lax.psum_scatter(
            grad_w_out.reshape(group_size, -1), ("stream", "dp"), scatter_dimension=0, tiled=True
        ),
        lax.psum_scatter(lower_small, ("stream", "dp"), scatter_dimension=0, tiled=True),
    )
    gathered = (
        lax.all_gather(summed[0].astype(jnp.bfloat16), ("stream", "dp"), axis=0, tiled=True).astype(
            jnp.float32
        ),
        lax.all_gather(summed[1].astype(jnp.bfloat16), ("stream", "dp"), axis=0, tiled=True).astype(
            jnp.float32
        ),
        lax.all_gather(summed[2].astype(jnp.bfloat16), ("stream", "dp"), axis=0, tiled=True).astype(
            jnp.float32
        ),
        lax.all_gather(summed[3].astype(jnp.bfloat16), ("stream", "dp"), axis=0, tiled=True).astype(
            jnp.float32
        ),
        lax.all_gather(summed[4].astype(jnp.bfloat16), ("stream", "dp"), axis=0, tiled=True).astype(
            jnp.float32
        ),
        lax.all_gather(summed[5].astype(jnp.bfloat16), ("stream", "dp"), axis=0, tiled=True).astype(
            jnp.float32
        ),
        lax.all_gather(summed[6].astype(jnp.bfloat16), ("stream", "dp"), axis=0, tiled=True).astype(
            jnp.float32
        ),
    )
    out_w_pool = gathered[0].reshape(model_width, model_width)
    out_w_down = gathered[1].reshape(ffn_width, model_width)
    out_w_in = gathered[2].reshape(model_width, ffn_width)
    upper_flat = gathered[3].reshape(-1)
    out_w_qkv = gathered[4].reshape(model_width, 3 * model_width)
    out_w_out = gathered[5].reshape(model_width, model_width)
    lower_flat = gathered[6].reshape(-1)
    out_b_pool = upper_flat[0:model_width]
    out_ln2_gain = upper_flat[model_width : 2 * model_width]
    out_ln2_bias = upper_flat[2 * model_width : 3 * model_width]
    out_b_down = upper_flat[3 * model_width : 4 * model_width]
    out_b_in = upper_flat[4 * model_width : 4 * model_width + ffn_width]
    out_b_qv = lower_flat[0 : 2 * model_width]
    out_b_out = lower_flat[2 * model_width : 3 * model_width]
    out_ln1_gain = lower_flat[3 * model_width : 4 * model_width]
    out_ln1_bias = lower_flat[4 * model_width : 5 * model_width]
    return (
        narrow(block_out)[None],
        narrow(grad_input)[None],
        out_w_qkv,
        out_b_qv,
        out_w_out,
        out_b_out,
        out_ln1_gain,
        out_ln1_bias,
        out_w_in,
        out_b_in,
        out_w_down,
        out_b_down,
        out_ln2_gain,
        out_ln2_bias,
        out_w_pool,
        out_b_pool,
    )


def solution(mesh):
    placed = (
        P("stream", "dp", None),
        P("stream", "dp", None),
        P(),
        P(),
        P(),
        P(),
        P(),
        P(),
        P(),
        P(),
        P(),
        P(),
        P(),
        P(),
        P(),
        P(),
        P(),
    )
    return jax.shard_map(
        shards,
        mesh=mesh,
        in_specs=placed,
        out_specs=(
            P("stream", "dp", None),
            P("stream", "dp", None),
            P(),
            P(),
            P(),
            P(),
            P(),
            P(),
            P(),
            P(),
            P(),
            P(),
            P(),
            P(),
            P(),
            P(),
        ),
        check_vma=False,
    )
```

profile of v0, /device:TPU:0, one launch (start us, length us, event | category | flops | bytes accessed | tf_op | source)
XLA Modules:
  0.0 1421.0 jit_solution(12993525407005746180)
XLA Ops:
  9.2 7.3 add_convert_fusion
  23.1 13.1 reshape.212
  78.7 37.3 %fusion.4 = (bf16[1024,3072]{1,0:T(8,128)(2,1)S(1)}, f32[1024,3072]{1,0:T(8,128)}) fusion(f32[3072]{0:T(1024)S(1)} %copy-done.47, bf16[768,3072]{1,0:T(8,128)(2,1)} %param.26, f32[1024,768]{1,0:T(8,128)S(1)} %get-tuple-element.54, f32[768]{0:T(1024)S(1)} %copy-done.36, f32[768]{0:T(1024)S(1)} %copy-done.32, f32[1024]{0:T(1024)S(1)} %add_rsqrt_fusion.1, ...), kind=kOutput, calls=%fused_computation.7 | convolution fusion | flops 5043388416 | bytes 26765312 | tf_op jit(solution)/shard_map/dot_general | solution.py:29
  127.1 44.6 %all_gather.24 = bf16[256,768]{1,0:T(8,128)(2,1)S(1)} all-gather(bf16[16,768]{1,0:T(8,128)(2,1)} %collective-permute-done), channel_id=1, replica_groups=mesh['stream'=2,'dp'=16] {'dp'}, dimensions={0}, use_global_device_ids=true | all-gather | bytes 417792 | tf_op jit(solution)/shard_map/all_gather | solution.py:138
  180.3 114.7 %reduce-scatter.2.cloned.1.call-done = f32[16,768]{1,0:T(8,128)} async-done(((f32[256,768]{1,0:T(8,128)}), f32[16,768]{1,0:T(8,128)}) %reduce-scatter.2.cloned.1.call-update) | async-done | bytes 49168 | tf_op jit(solution)/shard_map/reduce_scatter | solution.py:154
  319.1 13.6 fusion.87
  357.2 13.5 multiply_reduce_fusion
  370.7 6.7 multiply_convert_fusion
  392.0 9.4 fusion
  406.8 10.9 fusion.26
  417.7 7.6 fusion.52
  427.3 13.4 copy.72
  440.7 13.7 convert_element_type.138
  454.4 9.6 convolution_bitcast_fusion
  464.1 8.0 copy.73
  472.0 6.6 reshape.217
  492.7 8.1 reshape.226
  508.8 8.1 reshape.230
  519.8 494.9 %all-reduce.9 = (bf16[32,55296]{1,0:T(8,128)(2,1)}, bf16[32,120]{1,0:T(8,128)(2,1)}, bf16[32,18432]{1,0:T(8,128)(2,1)}, bf16[32,73728]{1,0:T(8,128)(2,1)}, bf16[...) all-reduce(f32[32,55296]{1,0:T(8,128)} %reshape.217, ...), channel_id=3, replica_groups=mesh['stream'=2,'dp'=16] {'stream','dp'}, use_global_device_ids=true, to_apply=%region_16.17.clone | all-reduce | flops 7677696 | bytes 46066176
  1029.5 63.8 %all-gather.1 = bf16[32,1,120]{2,1,0:T(2,128)(2,1)S(1)} all-gather(bf16[1,1,120]{2,1,0:T(2,128)(2,1)S(1)} %fusion.69), channel_id=1, replica_groups=mesh['stream'=2,'dp'=16] {'stream','dp'}, dimensions={0}, use_global_device_ids=true | all-gather | bytes 7920 | tf_op jit(solution)/shard_map/all_gather | solution.py:264
  1096.0 64.9 %all-gather.4 = bf16[32,1,192]{2,1,0:T(2,128)(2,1)S(1)} all-gather(bf16[1,1,192]{2,1,0:T(2,128)(2,1)S(1)} %fusion.67), channel_id=1, replica_groups=mesh['stream'=2,'dp'=16] {'stream','dp'}, dimensions={0}, use_global_device_ids=true | all-gather | bytes 12672 | tf_op jit(solution)/shard_map/all_gather | solution.py:255
  1171.0 7.8 fusion.44
  1178.8 10.1 convert_reduce_fusion.4
  1192.1 9.8 convert_reduce_fusion.3
  1206.5 65.5 %convert_reduce_fusion.2 = f32[32,55296]{1,0:T(8,128)} fusion(bf16[32,1,55296]{2,1,0:T(2,128)(2,1)} %all-gather.13.cloned.1.call-done), kind=kLoop, calls=%fused_computation.31 | loop fusion | flops 1769472 | bytes 10616832 | tf_op jit(solution)/shard_map/reshape | solution.py:272
  1272.0 6.9 reshape.238
  1278.8 11.6 all-gather.17.cloned.1.call-done
  1290.4 32.2 %convert_reduce_fusion.1 = f32[32,73728]{1,0:T(8,128)} fusion(bf16[32,1,73728]{2,1,0:T(2,128)(2,1)} %all-gather.17.cloned.1.call-done), kind=kLoop, calls=%fused_computation.29 | loop fusion | flops 2359296 | bytes 14155776 | tf_op jit(solution)/shard_map/reshape | solution.py:270
  1322.6 8.2 reshape.244
  1330.8 43.1 %all-gather.19.cloned.1.call-done = bf16[32,1,73728]{2,1,0:T(2,128)(2,1)} async-done(((bf16[1,1,73728]{2,1,0:T(2,128)(2,1)}), bf16[32,1,73728]{2,1,0:T(2,128)(2,1)}) %all-gather.19.cloned.1.call-update) | async-done | bytes 4718608 | tf_op jit(solution)/shard_map/all_gather | solution.py:249
  1373.8 32.1 %convert_reduce_fusion = f32[32,73728]{1,0:T(8,128)} fusion(bf16[32,1,73728]{2,1,0:T(2,128)(2,1)} %all-gather.19.cloned.1.call-done), kind=kLoop, calls=%fused_computation.28 | loop fusion | flops 2359296 | bytes 14155776 | tf_op jit(solution)/shard_map/reshape | solution.py:269
  1405.9 8.0 reshape.246
  (241 shorter events, 200.9 us)
Async XLA Ops:
  7.2 287.8 %reduce-scatter.2.cloned.1.call-start = ((), (), s32[]{:S(2)}) async-start(), calls=%async_computation.1 | async-start | bytes 835584 | tf_op jit(solution)/shard_map/reduce_scatter | solution.py:154
  57.9 6.5 copy-start.1
  74.0 42.0 %slice-start.2 = ((s8[4718592]{0:T(1024)(128)(4,1)}), s8[4194304]{0:T(1024)(128)(4,1)S(1)}, s32[]{:S(2)}) async-start(s8[4718592]{0:T(1024)(128)(4,1)} %bitcast.131), calls=%async_computation.9 | async-start | bytes 8388608
  78.1 37.9 %copy-start.7 = (f32[1024,768]{1,0:T(8,128)}, f32[1024,768]{1,0:T(8,128)S(1)}, u32[]{:S(2)}) copy-start(f32[1024,768]{1,0:T(8,128)S(1)} %get-tuple-element.54) | copy-start | bytes 9437188
  78.7 37.3 %slice-start.3 = ((s8[4718592]{0:T(1024)(128)(4,1)}), s8[524288]{0:T(1024)(128)(4,1)S(1)}, s32[]{:S(2)}) async-start(s8[4718592]{0:T(1024)(128)(4,1)} %bitcast.131), calls=%async_computation.10 | async-start | bytes 1048576
  78.7 37.3 %copy-start.50 = (f32[768]{0:T(1024)S(1)}, f32[768]{0:T(1024)}, u32[]{:S(2)}) copy-start(f32[768]{0:T(1024)} %param.29) | copy-start | bytes 9220
  116.0 6.1 copy-start.29
  125.4 1.7 collective-permute-start
  176.8 1002.1 %all-gather.15.cloned.1.call-start = ((), (), s32[]{:S(2)}) async-start(), calls=%async_computation.3 | async-start | bytes 2433024 | tf_op jit(solution)/shard_map/all_gather | solution.py:261
  296.5 5.6 collective-permute-start.1
  314.3 18.5 %slice-start.4 = ((s8[4718592]{0:T(1024)(128)(4,1)}), s8[4194304]{0:T(1024)(128)(4,1)S(1)}, s32[]{:S(2)}) async-start(s8[4718592]{0:T(1024)(128)(4,1)} %bitcast.133), calls=%async_computation.11 | async-start | bytes 8388608
  319.1 13.7 copy-start.20
  319.1 13.7 copy-start.8
  319.1 13.7 copy-start.33
  319.1 13.7 slice-start.5
  332.8 6.6 copy-start.15
  351.4 19.2 %slice-start = ((s8[6291456]{0:T(1024)(128)(4,1)}), s8[4194304]{0:T(1024)(128)(4,1)S(1)}, s32[]{:S(2)}) async-start(s8[6291456]{0:T(1024)(128)(4,1)} %bitcast.125), calls=%async_computation.7 | async-start | bytes 8388608
  357.2 26.1 %copy-start.6 = (f32[16,64,1,12,64]{4,1,3,0,2:T(8,128)}, f32[16,64,1,12,64]{4,1,3,0,2:T(8,128)S(1)}, u32[]{:S(2)}) copy-start(f32[16,64,1,12,64]{4,1,3,0,2:T(8,128)S(1)} %convolution_bitcast_fusion.1) | copy-start | bytes 9437188
  357.2 13.5 slice-start.1
  401.4 16.2 %slice-start.6 = ((s8[6291456]{0:T(1024)(128)(4,1)}), s8[4194304]{0:T(1024)(128)(4,1)S(1)}, s32[]{:S(2)}) async-start(s8[6291456]{0:T(1024)(128)(4,1)} %bitcast.135), calls=%async_computation.13 | async-start | bytes 8388608
  406.7 10.9 copy-start.21
  406.8 10.9 slice-start.7
  417.7 7.7 copy-start.25
  417.7 7.7 copy-start.27
  492.7 10.8 copy-start.40
  492.7 10.8 copy-start.41
  519.8 505.4 %copy-start.31 = (f32[768]{0:T(1024)S(1)}, f32[768]{0:T(1024)}, u32[]{:S(2)}) copy-start(f32[768]{0:T(1024)} %param.30) | copy-start | bytes 9220
  519.8 505.4 %copy-start.39 = (f32[768]{0:T(1024)S(1)}, f32[768]{0:T(1024)}, u32[]{:S(2)}) copy-start(f32[768]{0:T(1024)} %param.31) | copy-start | bytes 9220
  1016.4 175.7 %all-gather.21.cloned.1.call-start = ((), (), s32[]{:S(2)}) async-start(), calls=%async_computation.6 | async-start | bytes 2433024 | tf_op jit(solution)/shard_map/all_gather | solution.py:246
  1018.1 188.4 %all-gather.13.cloned.1.call-start = ((), (), s32[]{:S(2)}) async-start(), calls=%async_computation.2 | async-start | bytes 7299072 | tf_op jit(solution)/shard_map/all_gather | solution.py:258
  1020.5 270.0 %all-gather.17.cloned.1.call-start = ((), (), s32[]{:S(2)}) async-start(), calls=%async_computation.4 | async-start | bytes 9732096 | tf_op jit(solution)/shard_map/all_gather | solution.py:252
  1022.8 351.0 %all-gather.19.cloned.1.call-start = ((), (), s32[]{:S(2)}) async-start(), calls=%async_computation.5 | async-start | bytes 9732096 | tf_op jit(solution)/shard_map/all_gather | solution.py:249
  (36 other events, 114.8 us)
Sparse Core Ops, SparseCore 0:
  176.9 118.0 reduce-scatter.1
  1016.5 55.3 all-gather.14
  1075.3 56.3 all-gather.20
  1135.0 71.4 all-gather.12
  1209.8 80.5 all-gather.16
  1293.2 80.6 all-gather.18
where the time goes:
time: 1430 us; the launch traced here: 1420 us
  blocking collectives  668 us (47%)
  local copies, waits for them, and re-layouts  205 us (14%)
  other arithmetic  202 us (14%)
  waiting for transfers between devices  171 us (12%)
  matrix products  159 us (11%)
  between operations  15.1 us (1%)
    unnamed x1, blocking collectives  495 us
    reduce_scatter x1, waiting for transfers between devices, shards(): lax.psum_scatter(trans_left(grad_cos, embed_low), 'dp', scatter_dimension...  115 us
    reshape x1, other arithmetic, shards(): out_w_qkv = gathered[4].reshape(model_width, 3 * model_width)  65.5 us
    all_gather x1, blocking collectives, shards(): lax.all_gather(summed[3].astype(jnp.bfloat16), ('stream', 'dp'), axis=0,...  64.9 us
    all_gather x1, blocking collectives, shards(): lax.all_gather(summed[6].astype(jnp.bfloat16), ('stream', 'dp'), axis=0,...  63.8 us
    dot_general x6, matrix products, mat_mul(): return jnp.dot(inputs, matrix, preferred_element_type=jnp.float32)  55.9 us
    unnamed x136, local copies, waits for them, and re-layouts  45.4 us
    all_gather x1, blocking collectives, shards(): opposite = lax.all_gather(partner, 'dp', axis=0, tiled=True)  44.6 us
  transfers between devices with their start and end apart: 8, of which 4 were waited for; matrix products, arithmetic and copies ran while one was open for 13% of the time, Pallas kernels for 0%

commit v1 on v0

v1 whole, which is shorter than its diff:
```python
import functools
import math

import jax
import jax.numpy as jnp
from jax import lax
from jax.experimental import pallas as pl
from jax.experimental.pallas import tpu as pltpu
from jax.sharding import PartitionSpec as P

HEADS = 12
HEAD_DIM = 64
SEQ = 64
GROUP = 16

epsilon = 1e-06
score_scale = 10.0
margin_shift = score_scale * 0.3
root_half = 0.7071067811865476
gauss_norm = 0.3989422804014327

low = jnp.bfloat16
wide = jnp.float32


def struct(shape, dtype):
    return jax.ShapeDtypeStruct(shape, dtype)


def whole(shape):
    return pl.BlockSpec(shape, lambda *_: (0,) * len(shape))


def call(body, grid, in_specs, out_specs, out_shape, flops=0, scratch=(), aliases=None, limit=48):
    return pl.pallas_call(
        body,
        grid=grid,
        in_specs=in_specs,
        out_specs=out_specs,
        out_shape=out_shape,
        scratch_shapes=list(scratch),
        input_output_aliases=aliases or {},
        cost_estimate=pl.CostEstimate(flops=int(flops), bytes_accessed=int(flops / 400), transcendentals=0),
        compiler_params=pltpu.CompilerParams(vmem_limit_bytes=limit << 20),
    )


def mat_mul(a, b):
    return jnp.dot(a, b, preferred_element_type=wide)


def trans_left(a, b):
    return lax.dot_general(a, b, (((0,), (0,)), ((), ())), preferred_element_type=wide)


def trans_right(a, b):
    return lax.dot_general(a, b, (((1,), (1,)), ((), ())), preferred_element_type=wide)


def normalize(h):
    center = h - jnp.mean(h, axis=-1, keepdims=True)
    inv = lax.rsqrt(jnp.mean(center * center, axis=-1, keepdims=True) + epsilon)
    return center * inv, inv


def norm_input_grad(grad, normed, inv):
    return inv * (
        grad
        - jnp.mean(grad, axis=-1, keepdims=True)
        - normed * jnp.mean(grad * normed, axis=-1, keepdims=True)
    )


def split_heads(pair, first):
    zero = jnp.zeros_like(pair)
    return jnp.concatenate([jnp.where(first, pair, zero), jnp.where(first, zero, pair)], axis=0)


def join_heads(rows, first):
    return jnp.where(first, rows[:SEQ], rows[SEQ:])


def attention_forward(x, w_qkv, qkv_bias, w_out, b_out, gain, bias):
    tokens, width = x.shape
    rows = 4 * SEQ
    pairs = width // (2 * HEAD_DIM)
    scale = 1.0 / math.sqrt(HEAD_DIM)

    def body(x_ref, wq_ref, bq_ref, wo_ref, bo_ref, g_ref, b_ref, proj_ref, prob_ref, ctx_ref, hid_ref, low_ref, inv_ref):
        x_in = x_ref[...]
        for part in range(3):
            cols = slice(part * width, (part + 1) * width)
            proj_ref[:, cols] = (mat_mul(x_in, wq_ref[:, cols]) + bq_ref[:, cols]).astype(low)
        first = lax.broadcasted_iota(jnp.int32, (SEQ, 128), 1) < HEAD_DIM
        for sent in range(4):
            r = slice(sent * SEQ, (sent + 1) * SEQ)
            for pair in range(pairs):
                c = pair * 128
                q = proj_ref[r, c : c + 128]
                k = proj_ref[r, width + c : width + c + 128]
                v = proj_ref[r, 2 * width + c : 2 * width + c + 128]
                scores = trans_right(k, split_heads(q, first)) * scale
                e = jnp.exp(scores - jnp.max(scores, axis=0, keepdims=True))
                probs = (e * (1.0 / jnp.sum(e, axis=0, keepdims=True))).astype(low)
                prob_ref[sent, pair] = probs
                ctx_ref[r, c : c + 128] = join_heads(trans_left(probs, v), first).astype(low)
        h = x_in.astype(wide) + mat_mul(ctx_ref[...], wo_ref[...]) + bo_ref[...]
        normed, inv = normalize(h)
        hidden = normed * g_ref[...] + b_ref[...]
        hid_ref[...] = hidden
        low_ref[...] = hidden.astype(low)
        inv_ref[...] = inv

    row = lambda cols: pl.BlockSpec((rows, cols), lambda i: (i, 0))
    prob_shape = (tokens // SEQ, pairs, SEQ, 128)
    return call(
        body,
        (tokens // rows,),
        [row(width), whole(w_qkv.shape), whole(qkv_bias.shape), whole(w_out.shape)] + [whole((1, width))] * 3,
        [row(3 * width), pl.BlockSpec((4,) + prob_shape[1:], lambda i: (i, 0, 0, 0)), row(width), row(width), row(width), row(1)],
        [
            struct((tokens, 3 * width), low),
            struct(prob_shape, low),
            struct((tokens, width), low),
            struct((tokens, width), wide),
            struct((tokens, width), low),
            struct((tokens, 1), wide),
        ],
        flops=2 * tokens * width * (4 * width + 4 * SEQ),
    )(x, w_qkv, qkv_bias, w_out, b_out, gain, bias)


CHUNK = 512


def ffn_forward_rows(hidden, wi_ref, bi_ref, wd_ref, bd_ref, store_act, store_slope):
    h_low = hidden.astype(low)
    ffn = wi_ref.shape[1]
    total = hidden + bd_ref[...]
    for c in range(0, ffn, CHUNK):
        u = mat_mul(h_low, wi_ref[:, c : c + CHUNK]) + bi_ref[:, c : c + CHUNK]
        phi = 0.5 + 0.5 * lax.erf(u * root_half)
        act = (u * phi).astype(low)
        store_act(c, act)
        store_slope(c, (phi + u * jnp.exp(-0.5 * u * u) * gauss_norm).astype(low))
        total = total + mat_mul(act, wd_ref[c : c + CHUNK, :])
    return normalize(total)


def ffn_backward_rows(grad_block, normed, inv, gain_ref, wd_ref, slope_of, store_gate, small_ref, bin_ref):
    grad_two = norm_input_grad(grad_block * gain_ref[...], normed, inv)
    small_ref[0:1, :] += jnp.sum(grad_block * normed, axis=0, keepdims=True)
    small_ref[1:2, :] += jnp.sum(grad_block, axis=0, keepdims=True)
    small_ref[2:3, :] += jnp.sum(grad_two, axis=0, keepdims=True)
    grad_low = grad_two.astype(low)
    for c in range(0, wd_ref.shape[0], CHUNK):
        gate = trans_right(grad_low, wd_ref[c : c + CHUNK, :]) * slope_of(c).astype(wide)
        bin_ref[:, c : c + CHUNK] += jnp.sum(gate, axis=0, keepdims=True)
        store_gate(c, gate.astype(low))
    return grad_low


def group_spec(sents, cols, index):
    return pl.BlockSpec((sents, GROUP, cols), lambda i: (0, index(i), 0))


def ffn_first(hidden, w_in, b_in, w_down, b_down, gain, bias):
    sents, _, width = hidden.shape
    ffn = w_in.shape[1]
    rows = sents * GROUP

    def body(h_ref, wi_ref, bi_ref, wd_ref, bd_ref, g_ref, b_ref, enc_ref, act_ref, slope_ref, n_ref, inv_ref, first_ref):
        def store_act(c, v):
            act_ref[:, :, c : c + CHUNK] = v.reshape(sents, GROUP, CHUNK)

        def store_slope(c, v):
            slope_ref[:, c : c + CHUNK] = v

        normed, inv = ffn_forward_rows(h_ref[...].reshape(rows, width), wi_ref, bi_ref, wd_ref, bd_ref, store_act, store_slope)
        n_ref[...] = normed
        inv_ref[...] = inv
        block = (normed * g_ref[...] + b_ref[...]).reshape(sents, GROUP, width)
        enc_ref[...] = block.astype(low)
        first_ref[...] = block[:, 0, :].astype(low)

    zero = lambda i: 0
    return call(
        body,
        (1,),
        [group_spec(sents, width, zero), whole(w_in.shape), whole((1, ffn)), whole(w_down.shape)] + [whole((1, width))] * 3,
        [
            group_spec(sents, width, zero),
            group_spec(sents, ffn, zero),
            whole((rows, ffn)),
            whole((rows, width)),
            whole((rows, 1)),
            whole((sents, width)),
        ],
        [
            struct((sents, SEQ, width), low),
            struct((sents, SEQ, ffn), low),
            struct((rows, ffn), low),
            struct((rows, width), wide),
            struct((rows, 1), wide),
            struct((sents, width), low),
        ],
        flops=4 * rows * width * ffn,
    )(hidden, w_in, b_in, w_down, b_down, gain, bias)


def ffn_rest(hidden, cot, w_in, b_in, w_down, b_down, gain, bias, encoded, act):
    sents, _, width = hidden.shape
    ffn = w_in.shape[1]
    rows = sents * GROUP
    groups = SEQ // GROUP

    def body(h_ref, cot_ref, wi_ref, bi_ref, wd_ref, bd_ref, g_ref, b_ref, _e, _a, enc_ref, act_ref, gate_ref, two_ref, small_ref, bin_ref, slope_ref):
        @pl.when(pl.program_id(0) == 0)
        def _():
            small_ref[...] = jnp.zeros_like(small_ref)
            bin_ref[...] = jnp.zeros_like(bin_ref)

        def store_act(c, v):
            act_ref[:, :, c : c + CHUNK] = v.reshape(sents, GROUP, CHUNK)

        def store_slope(c, v):
            slope_ref[:, c : c + CHUNK] = v

        def store_gate(c, v):
            gate_ref[:, :, c : c + CHUNK] = v.reshape(sents, GROUP, CHUNK)

        normed, inv = ffn_forward_rows(h_ref[...].reshape(rows, width), wi_ref, bi_ref, wd_ref, bd_ref, store_act, store_slope)
        enc_ref[...] = (normed * g_ref[...] + b_ref[...]).astype(low).reshape(sents, GROUP, width)
        grad_block = cot_ref[...].reshape(rows, width).astype(wide)
        two = ffn_backward_rows(
            grad_block, normed, inv, g_ref, wd_ref, lambda c: slope_ref[:, c : c + CHUNK], store_gate, small_ref, bin_ref
        )
        two_ref[...] = two.reshape(sents, GROUP, width)

    nxt = lambda i: i + 1
    anyspec = pl.BlockSpec(memory_space=pl.ANY)
    return call(
        body,
        (groups - 1,),
        [group_spec(sents, width, nxt)] * 2
        + [whole(w_in.shape), whole((1, ffn)), whole(w_down.shape)]
        + [whole((1, width))] * 3
        + [anyspec] * 2,
        [
            group_spec(sents, width, nxt),
            group_spec(sents, ffn, nxt),
            group_spec(sents, ffn, nxt),
            group_spec(sents, width, nxt),
            whole((8, width)),
            whole((1, ffn)),
        ],
        [
            struct((sents, SEQ, width), low),
            struct((sents, SEQ, ffn), low),
            struct((sents, SEQ, ffn), low),
            struct((sents, SEQ, width), low),
            struct((8, width), wide),
            struct((1, ffn), wide),
        ],
        flops=6 * (groups - 1) * rows * width * ffn,
        scratch=[pltpu.VMEM((rows, ffn), low)],
        aliases={8: 0, 9: 1},
    )(hidden, cot, w_in, b_in, w_down, b_down, gain, bias, encoded, act)


def ffn_first_back(cot, grad_first, normed, inv, slope, gain, w_down, gate, two, small, bin_sum):
    sents, _, width = cot.shape
    ffn = w_down.shape[0]
    rows = sents * GROUP

    def body(cot_ref, first_ref, n_ref, inv_ref, slope_ref, g_ref, wd_ref, sin_ref, bin_in_ref, _g, _t, gate_ref, two_ref, small_ref, bin_ref):
        small_ref[...] = sin_ref[...]
        bin_ref[...] = bin_in_ref[...]
        position = lax.broadcasted_iota(jnp.int32, (sents, GROUP, width), 1)
        at_first = jnp.broadcast_to(first_ref[...][:, None, :], (sents, GROUP, width))
        grad_block = cot_ref[...].astype(wide) + jnp.where(position == 0, at_first, 0.0)

        def store_gate(c, v):
            gate_ref[:, :, c : c + CHUNK] = v.reshape(sents, GROUP, CHUNK)

        got = ffn_backward_rows(
            grad_block.reshape(rows, width),
            n_ref[...],
            inv_ref[...],
            g_ref,
            wd_ref,
            lambda c: slope_ref[:, c : c + CHUNK],
            store_gate,
            small_ref,
            bin_ref,
        )
        two_ref[...] = got.reshape(sents, GROUP, width)

    zero = lambda i: 0
    anyspec = pl.BlockSpec(memory_space=pl.ANY)
    return call(
        body,
        (1,),
        [
            group_spec(sents, width, zero),
            whole((sents, width)),
            whole((rows, width)),
            whole((rows, 1)),
            whole((rows, ffn)),
            whole((1, width)),
            whole(w_down.shape),
            whole((8, width)),
            whole((1, ffn)),
            anyspec,
            anyspec,
        ],
        [group_spec(sents, ffn, zero), group_spec(sents, width, zero), whole((8, width)), whole((1, ffn))],
        [
            struct((sents, SEQ, ffn), low),
            struct((sents, SEQ, width), low),
            struct((8, width), wide),
            struct((1, ffn), wide),
        ],
        flops=2 * rows * width * ffn,
        aliases={9: 0, 10: 1},
    )(cot, grad_first, normed, inv, slope, gain, w_down, small, bin_sum, gate, two)


def lower_backward(two, gate, hidden, inv, proj, probs, w_in, w_out, gain, bias):
    tokens, width = hidden.shape
    ffn = w_in.shape[1]
    rows = 4 * SEQ
    pairs = width // (2 * HEAD_DIM)
    scale = 1.0 / math.sqrt(HEAD_DIM)

    def body(two_ref, gate_ref, hid_ref, inv_ref, proj_ref, prob_ref, wi_ref, wo_ref, g_ref, b_ref, one_ref, gp_ref, small_ref, bqv_ref, ctx_ref):
        @pl.when(pl.program_id(0) == 0)
        def _():
            small_ref[...] = jnp.zeros_like(small_ref)
            bqv_ref[...] = jnp.zeros_like(bqv_ref)

        grad_hidden = two_ref[...].astype(wide) + trans_right(gate_ref[...], wi_ref[...])
        normed = (hid_ref[...] - b_ref[...]) * (1.0 / g_ref[...])
        small_ref[0:1, :] += jnp.sum(grad_hidden * normed, axis=0, keepdims=True)
        small_ref[1:2, :] += jnp.sum(grad_hidden, axis=0, keepdims=True)
        grad_one = norm_input_grad(grad_hidden * g_ref[...], normed, inv_ref[...])
        small_ref[2:3, :] += jnp.sum(grad_one, axis=0, keepdims=True)
        one_low = grad_one.astype(low)
        one_ref[...] = one_low
        ctx_ref[...] = trans_right(one_low, wo_ref[...]).astype(low)
        first = lax.broadcasted_iota(jnp.int32, (SEQ, 128), 1) < HEAD_DIM
        for pair in range(pairs):
            c = pair * 128
            sum_q = jnp.zeros((1, 128), wide)
            sum_v = jnp.zeros((1, 128), wide)
            for sent in range(4):
                r = slice(sent * SEQ, (sent + 1) * SEQ)
                q = split_heads(proj_ref[r, c : c + 128], first)
                k = proj_ref[r, width + c : width + c + 128]
                v = proj_ref[r, 2 * width + c : 2 * width + c + 128]
                d = split_heads(ctx_ref[r, c : c + 128], first)
                p_low = prob_ref[sent, pair]
                p = p_low.astype(wide)
                grad_p = trans_right(v, d)
                grad_v = mat_mul(p_low, d)
                grad_s = (p * (grad_p - jnp.sum(grad_p * p, axis=0, keepdims=True))).astype(low)
                grad_k = mat_mul(grad_s, q) * scale
                grad_q = join_heads(trans_left(grad_s, k), first) * scale
                sum_q += jnp.sum(grad_q, axis=0, keepdims=True)
                sum_v += jnp.sum(grad_v, axis=0, keepdims=True)
                gp_ref[r, c : c + 128] = grad_q.astype(low)
                gp_ref[r, width + c : width + c + 128] = grad_k.astype(low)
                gp_ref[r, 2 * width + c : 2 * width + c + 128] = grad_v.astype(low)
            bqv_ref[0:1, c : c + 128] += sum_q
            bqv_ref[1:2, c : c + 128] += sum_v

    row = lambda cols: pl.BlockSpec((rows, cols), lambda i: (i, 0))
    return call(
        body,
        (tokens // rows,),
        [
            row(width),
            row(ffn),
            row(width),
            row(1),
            row(3 * width),
            pl.BlockSpec((4,) + probs.shape[1:], lambda i: (i, 0, 0, 0)),
            whole(w_in.shape),
            whole(w_out.shape),
            whole((1, width)),
            whole((1, width)),
        ],
        [row(width), row(3 * width), whole((8, width)), whole((8, width))],
        [struct((tokens, width), low), struct((tokens, 3 * width), low), struct((8, width), wide), struct((8, width), wide)],
        flops=2 * tokens * width * (ffn + width + 8 * SEQ),
        scratch=[pltpu.VMEM((rows, width), low)],
    )(two, gate, hidden, inv, proj, probs, w_in, w_out, gain, bias)


def input_gradient(grad_proj, w_qkv, grad_one):
    tokens, width = grad_one.shape
    rows = 4 * SEQ

    def body(gp_ref, w_ref, one_ref, out_ref):
        out_ref[...] = (one_ref[...].astype(wide) + trans_right(gp_ref[...], w_ref[...])).astype(low)

    row = lambda cols: pl.BlockSpec((rows, cols), lambda i: (i, 0))
    return call(
        body,
        (tokens // rows,),
        [row(3 * width), whole(w_qkv.shape), row(width)],
        row(width),
        struct((tokens, width), low),
        flops=6 * tokens * width * width,
    )(grad_proj, w_qkv, grad_one)


def weight_gradient(a, g, block):
    tokens, m = a.shape
    n = g.shape[1]

    def body(a_ref, g_ref, o_ref):
        o_ref[...] = trans_left(a_ref[...], g_ref[...]).astype(low)

    return call(
        body,
        (m // block,),
        [pl.BlockSpec((tokens, block), lambda i: (0, i)), whole(g.shape)],
        pl.BlockSpec((block, n), lambda i: (i, 0)),
        struct((m, n), low),
        flops=2 * tokens * m * n,
    )(a, g)


def contrastive(first, ids, w_pool, b_pool):
    total = first.shape[1]
    flat = first.reshape(2 * total, -1)
    pooled = jnp.tanh(mat_mul(flat, w_pool) + b_pool)
    inv_len = lax.rsqrt(jnp.sum(pooled * pooled, axis=-1, keepdims=True) + epsilon)
    unit = pooled * inv_len
    embed = unit.astype(low)
    zero, one = embed[:total], embed[total:]
    same = ids[:, None] == ids[None, :]
    eye = (jnp.arange(total)[:, None] == jnp.arange(total)[None, :]).astype(wide)
    logits = score_scale * trans_right(zero, one) - margin_shift * eye
    masked = jnp.where(same, logits, -jnp.inf)

    def soft(axis):
        e = jnp.exp(masked - jnp.max(masked, axis=axis, keepdims=True))
        return (score_scale * (e / jnp.sum(e, axis=axis, keepdims=True) - eye)).astype(low)

    by_row, by_col = soft(1), soft(0)
    grad_embed = jnp.concatenate(
        [mat_mul(by_row, one) + mat_mul(by_col, one), trans_left(by_row, zero) + trans_left(by_col, zero)]
    )
    grad_pre = (
        inv_len * (grad_embed - unit * jnp.sum(unit * grad_embed, axis=-1, keepdims=True)) * (1.0 - pooled * pooled)
    )
    pre_low = grad_pre.astype(low)
    return pre_low, trans_left(flat, pre_low), jnp.sum(grad_pre, axis=0)


def exchange(a, axis, mask):
    size = lax.axis_size(axis)
    return lax.ppermute(a, axis, [(i, i ^ mask) for i in range(size)])


def gather_ordered(a, axis, mask):
    got = exchange(a, axis, mask)
    bit = (lax.axis_index(axis) // mask) % 2
    n = a.shape[0]
    return lax.dynamic_slice_in_dim(jnp.concatenate([got, a, got]), (1 - bit) * n, 2 * n, 0)


def take_half(a, which, n):
    return lax.dynamic_slice_in_dim(a, which * n, n, 0)


def reduce_parts(terms, axis, mask):
    n = terms[0].shape[0] // 2
    bit = (lax.axis_index(axis) // mask) % 2
    send = sum(take_half(t, 1 - bit, n).astype(wide) for t in terms).astype(low)
    return [take_half(t, bit, n) for t in terms] + [exchange(send, axis, mask)]


def sum_all(part, steps):
    terms = [part]
    for axis, mask in steps:
        terms = reduce_parts(terms, axis, mask)
    total = sum(t.astype(wide) for t in terms).astype(low)
    return total


def spread(total, steps):
    for axis, mask in reversed(steps):
        total = gather_ordered(total, axis, mask)
    return total


def shards(
    embedded, seq_cotangent, pair_ids, w_qkv, b_qv, w_out, b_out, ln1_gain, ln1_bias, w_in, b_in, w_down, b_down,
    ln2_gain, ln2_bias, w_pool, b_pool,
):
    x = embedded[0]
    tokens, width = x.shape
    sents = tokens // SEQ
    ffn = w_in.shape[1]
    dp = lax.axis_size("dp")
    stream = lax.axis_index("stream")
    row = lambda v: v.reshape(1, -1)
    qkv_bias = row(jnp.concatenate([b_qv[:width], jnp.zeros((width,), wide), b_qv[width:]]))
    proj, probs, context, hidden, hidden_low, inv_one = attention_forward(
        x, w_qkv, qkv_bias, w_out, row(b_out), row(ln1_gain), row(ln1_bias)
    )
    hid3 = hidden.reshape(sents, SEQ, width)
    cot3 = seq_cotangent[0].reshape(sents, SEQ, width)
    upper = (w_in, row(b_in), w_down, row(b_down), row(ln2_gain), row(ln2_bias))
    enc, act, slope, normed_two, inv_two, first_low = ffn_first(hid3, *upper)
    gathered = first_low
    mask = 1
    while mask < dp:
        gathered = gather_ordered(gathered, "dp", mask)
        mask *= 2
    gathered = gather_ordered(gathered, "stream", 1)
    enc, act, gate, two, small_up, bin_sum = ffn_rest(hid3, cot3, *upper, enc, act)
    total = sents * dp
    pre_low, grad_w_pool, grad_b_pool = contrastive(gathered.reshape(2, total, width), pair_ids, w_pool, row(b_pool))
    own_pre = lax.dynamic_slice_in_dim(pre_low, stream * total + lax.axis_index("dp") * sents, sents)
    grad_first = trans_right(own_pre, w_pool)
    gate, two, small_up, bin_sum = ffn_first_back(
        cot3, grad_first, normed_two, inv_two, slope, row(ln2_gain), w_down, gate, two, small_up, bin_sum
    )
    act, gate, two = (v.reshape(tokens, -1) for v in (act, gate, two))
    grad_w_down = weight_gradient(act, two, 768)
    grad_w_in = weight_gradient(hidden_low, gate, 256)
    grad_one, grad_proj, small_low, bqv = lower_backward(
        two, gate, hidden, inv_one, proj, probs, w_in, w_out, row(ln1_gain), row(ln1_bias)
    )
    grad_w_qkv = weight_gradient(x, grad_proj, 256)
    grad_w_out = weight_gradient(context, grad_one, 256)
    grad_input = input_gradient(grad_proj, w_qkv, grad_one)

    bits = [1 << i for i in range(4)]
    tail = [1 << i for i in range(4, dp.bit_length() - 1)]
    order_a = [("stream", 1)] + [("dp", m) for m in bits]
    order_b = [("stream", 1)] + [("dp", m) for m in [bits[1], bits[0]] + bits[2:]]

    def reduce(part, order):
        s = sum_all(part, order)
        for m in tail:
            s = (s.astype(wide) + exchange(s, "dp", m).astype(wide)).astype(low)
        return spread(s, order)

    half = ffn // 2
    out_down = jnp.concatenate([reduce(grad_w_down[:half], order_a), reduce(grad_w_down[half:], order_b)], 0)
    out_in = jnp.concatenate([reduce(grad_w_in[:, :half], order_a), reduce(grad_w_in[:, half:], order_b)], 1)
    lower_rest = jnp.concatenate([grad_w_qkv[:, half:], grad_w_out], 1)
    out_qkv_a = reduce(grad_w_qkv[:, :half], order_a)
    out_rest = reduce(lower_rest, order_b)
    out_qkv = jnp.concatenate([out_qkv_a, out_rest[:, : 3 * width - half]], 1)
    out_out = out_rest[:, 3 * width - half :]
    small = jnp.concatenate([small_up[:3], bin_sum.reshape(-1, width), small_low[:3], bqv[:2]], 0)
    for axis, m in [("stream", 1)] + [("dp", m) for m in bits + tail]:
        small = small + exchange(small, axis, m)
    f32 = lambda v: v.astype(wide)
    n_in = ffn // width
    return (
        enc.reshape(1, tokens, width),
        grad_input[None],
        f32(out_qkv),
        small[6 + n_in : 8 + n_in].reshape(-1),
        f32(out_out),
        small[5 + n_in],
        small[3 + n_in],
        small[4 + n_in],
        f32(out_in),
        small[3 : 3 + n_in].reshape(-1),
        f32(out_down),
        small[2],
        small[0],
        small[1],
        grad_w_pool,
        grad_b_pool,
    )


def solution(mesh):
    sharded = P("stream", "dp", None)
    return jax.shard_map(
        shards,
        mesh=mesh,
        in_specs=(sharded, sharded) + (P(),) * 15,
        out_specs=(sharded, sharded) + (P(),) * 14,
        check_vma=False,
    )
```

time: 1430 us -> 462 us (0.32)
  blocking collectives: 668 us -> 0 us
  local copies, waits for them, and re-layouts: 205 us -> 39 us
  matrix products: 159 us -> 5.33 us
  Pallas kernels: 0 us -> 137 us
  other arithmetic: 202 us -> 90 us
  starting transfers between devices: 0.86 us -> 71.3 us
  waiting for transfers between devices: 171 us -> 109 us
    unnamed x1 -> x0, blocking collectives: 495 us -> none
    all_gather x3 -> x0, blocking collectives: 173 us -> none  [the longest x1 64.9 us: shards(): lax.all_gather(summed[3].astype(jnp.bfloat16), ('stream', 'dp'), axis=0,...]
    dot_general x24 -> x8, matrix products: 159 us -> 5.33 us  [the longest x3 3 us: trans_left(): lax.dot_general(a, b, (((0,), (0,)), ((), ())), preferred_element_type=wide)]
    reshape x6 -> x0, other arithmetic: 150 us -> none  [the longest x1 65.5 us: shards(): out_w_qkv = gathered[4].reshape(model_width, 3 * model_width)]
    pallas_call x0 -> x10, Pallas kernels: none -> 137 us  [the longest x1 32.8 us: attention_forward(): call(body, (tokens // rows,), [row(width), whole(w_qkv.shape), whole(qkv_...]
    reduce_scatter x1 -> x0, waiting for transfers between devices: 115 us -> none  [shards(): lax.psum_scatter(trans_left(grad_cos, embed_low), 'dp', scatter_dimension...]
    ppermute x2 -> x70, waiting for transfers between devices: 0.01 us -> 109 us  [exchange(): return lax.ppermute(a, axis, [(i, i ^ mask) for i in range(size)])]
    reshape x16 -> x10, local copies, waits for them, and re-layouts: 85.6 us -> 6.07 us  [the longest x7 4.15 us: shards(): row = lambda v: v.reshape(1, -1)]
  transfers between devices with their start and end apart: 8 -> 70, of which waited for: 4 -> 37; matrix products, arithmetic and copies ran while one was open for 13% -> 20% of each run, Pallas kernels for 0% -> 9%
where the time goes in v1:
time: 462 us; the launch traced here: 454 us
  Pallas kernels  137 us (30%)
  waiting for transfers between devices  109 us (24%)
  other arithmetic  90 us (19%)
  starting transfers between devices  71.3 us (15%)
  local copies, waits for them, and re-layouts  39 us (8%)
  matrix products  5.33 us (1%)
    ppermute x70, waiting for transfers between devices, exchange(): return lax.ppermute(a, axis, [(i, i ^ mask) for i in range(size)])  109 us
    ppermute x70, starting transfers between devices, exchange(): return lax.ppermute(a, axis, [(i, i ^ mask) for i in range(size)])  71.3 us
    concatenate x35, other arithmetic, gather_ordered(): jnp.concatenate([got, a, got])  46.6 us
    pallas_call x1, Pallas kernels, attention_forward(): call(body, (tokens // rows,), [row(width), whole(w_qkv.shape), whole(qkv_...  32.8 us
    pallas_call x1, Pallas kernels, lower_backward(): call(body, (tokens // rows,), [row(width), row(ffn), row(width), row(1),...  32.8 us
    pallas_call x4, Pallas kernels, weight_gradient(): call(body, (m // block,), [pl.BlockSpec((tokens, block), lambda i: (0, i)...  27.2 us
    pallas_call x1, Pallas kernels, ffn_rest(): call(body, (groups - 1,), [group_spec(sents, width, nxt)] * 2 + [whole(w_...  22.8 us
    convert_element_type x24, other arithmetic, reduce_parts(): sum((take_half(t, 1 - bit, n).astype(wide) for t in terms)).astype(low)  19.9 us
  transfers between devices with their start and end apart: 70, of which 37 were waited for; matrix products, arithmetic and copies ran while one was open for 20% of the time, Pallas kernels for 9%

profile of v1, /device:TPU:0, one launch (start us, length us, event | category | flops | bytes accessed | tf_op | source)
XLA Modules:
  0.0 453.7 jit_solution(9962434277555566302)
XLA Ops:
  6.9 32.8 %shard_map.288 = (bf16[1024,2304]{1,0:T(8,128)(2,1)}, bf16[16,6,64,128]{3,2,1,0:T(8,128)(2,1)S(1)}, bf16[1024,768]{1,0:T(8,128)(2,1)S(1)}, f32[1024,768]{1,0:T(8...) custom-call(bf16[1024,768]{1,0:T(8,128)(2,1)} %bitcast.22, bf16[768,2304]{1,0:T(8,128)(2,1)} %w_ref.1, ...), custom_call_target="tpu_custom_call" | custom-call | flops 5234491392 | bytes 13086228 | tf_op jit(solution)/shard_map/pallas_call | solution.py:116
  44.7 9.2 %shard_map.289 = (bf16[16,64,768]{2,1,0:T(8,128)(2,1)}, bf16[16,64,3072]{2,1,0:T(8,128)(2,1)}, bf16[256,3072]{1,0:T(8,128)(2,1)S(1)}, f32[256,768]{1,0:T(8,128)S...) custom-call(f32[16,64,768]{2,1,0:T(8,128)S(1)} %bitcast.15, bf16[768,3072]{1,0:T(8,128)(2,1)} %wi_ref.5, ...), custom_call_target="tpu_custom_call" | custom-call | flops 2415919104 | bytes 6039797 | tf_op jit(solution)/shard_map/pallas_call | solution.py:187
  74.9 3.0 collective-permute-start.3
  77.9 6.1 %collective-permute-done.3 = bf16[128,768]{1,0:T(8,128)(2,1)} collective-permute-done((bf16[128,768]{1,0:T(8,128)(2,1)}, bf16[128,768]{1,0:T(8,128)(2,1)}, u32[]{:S(2)}, u32[]{:S(2)}) %collective-permute-start.3) | collective-permute-done | bytes 196640 | tf_op jit(solution)/shard_map/ppermute | solution.py:465
  86.8 22.8 %shard_map.290 = (bf16[16,64,768]{2,1,0:T(8,128)(2,1)}, bf16[16,64,3072]{2,1,0:T(8,128)(2,1)}, bf16[16,64,3072]{2,1,0:T(8,128)(2,1)}, bf16[16,64,768]{2,1,0:T(8,...) custom-call(f32[16,64,768]{2,1,0:T(8,128)} %bitcast.14, ...), custom_call_target="tpu_custom_call", output_to_operand_aliasing={{0}: (8, {}), {1}: (9, {})} | custom-call | flops 10871635968 | bytes 27179088 | tf_op jit(solution)/shard_map/pallas_call | solution.py:242
  119.9 5.5 %shard_map.291 = (bf16[16,64,3072]{2,1,0:T(8,128)(2,1)}, bf16[16,64,768]{2,1,0:T(8,128)(2,1)S(1)}, f32[8,768]{1,0:T(8,128)S(1)}, f32[1,3072]{1,0:T(1,128)S(1)}) custom-call(bf16[16,64,768]{2,1,0:T(8,128)(2,1)S(1)} %bitcast.17, f32[16,768]{1,0:T(8,128)S(1)} %fusion.92.first_ref, ...), custom_call_target="tpu_custom_call", output_to_operand_aliasing={{0}: (9, {}), {1}: (10, {})} | custom-call | flops 1207959552 | bytes 3019898 | tf_op jit(solution)/shard_map/pallas_call | solution.py:301
  125.4 32.8 %shard_map.292 = (bf16[1024,768]{1,0:T(8,128)(2,1)S(1)}, bf16[1024,2304]{1,0:T(8,128)(2,1)}, f32[8,768]{1,0:T(8,128)S(1)}, f32[8,768]{1,0:T(8,128)S(1)}) custom-call(bf16[1024,768]{1,0:T(8,128)(2,1)S(1)} %bitcast.18, bf16[1024,3072]{1,0:T(8,128)(2,1)} %bitcast.24, f32[1024,768]{1,0:T(8,128)} %get-tuple-element.42.hid_ref, f32[1024,1]{1,0:T(8,128)S(1)} %copy-done.32, ...), custom_call_target="tpu_custom_call" | custom-call | flops 6845104128 | bytes 17112760 | tf_op jit(solution)/shard_map/pallas_call | solution.py:378
  158.2 6.8 %shard_map.294 = bf16[768,2304]{1,0:T(8,128)(2,1)S(1)} custom-call(bf16[1024,768]{1,0:T(8,128)(2,1)S(1)} %bitcast.23, bf16[1024,2304]{1,0:T(8,128)(2,1)} %get-tuple-element.59.gp_ref.g_ref), custom_call_target="tpu_custom_call" | custom-call | flops 3623878656 | bytes 9059696 | tf_op jit(solution)/shard_map/pallas_call | solution.py:425
  165.3 3.1 copy-done.24
  168.4 7.0 %shard_map.293 = bf16[1024,768]{1,0:T(8,128)(2,1)} custom-call(bf16[1024,2304]{1,0:T(8,128)(2,1)} %get-tuple-element.59.gp_ref.g_ref, bf16[768,2304]{1,0:T(8,128)(2,1)S(1)} %copy-done.24, bf16[1024,768]{1,0:T(8,128)(2,1)S(1)} %get-tuple-element.60.one_ref.g_ref), custom_call_target="tpu_custom_call" | custom-call | flops 3623878656 | bytes 9059696 | tf_op jit(solution)/shard_map/pallas_call | solution.py:408
  182.2 9.5 %shard_map.296 = bf16[768,3072]{1,0:T(8,128)(2,1)} custom-call(bf16[1024,768]{1,0:T(8,128)(2,1)S(1)} %copy-done.33, bf16[1024,3072]{1,0:T(8,128)(2,1)} %bitcast.25), custom_call_target="tpu_custom_call" | custom-call | flops 4831838208 | bytes 12079595 | tf_op jit(solution)/shard_map/pallas_call | solution.py:425
  197.0 8.9 %shard_map.297 = bf16[3072,768]{1,0:T(8,128)(2,1)} custom-call(bf16[1024,3072]{1,0:T(8,128)(2,1)} %bitcast.26, bf16[1024,768]{1,0:T(8,128)(2,1)S(1)} %bitcast.19), custom_call_target="tpu_custom_call" | custom-call | flops 4831838208 | bytes 12079595 | tf_op jit(solution)/shard_map/pallas_call | solution.py:425
  243.7 5.8 %collective-permute-done.16 = bf16[192,1536]{1,0:T(8,128)(2,1)S(1)} collective-permute-done((bf16[192,1536]{1,0:T(8,128)(2,1)S(1)}, bf16[192,1536]{1,0:T(8,128)(2,1)S(1)}, u32[]{:S(2)}, u32[]{:S(2)}) %collective-permute-start.16) | collective-permute-done | bytes 589856 | tf_op jit(solution)/shard_map/ppermute | solution.py:465
  254.9 7.2 %collective-permute-done.41 = bf16[192,1536]{1,0:T(8,128)(2,1)S(1)} collective-permute-done((bf16[192,1536]{1,0:T(8,128)(2,1)S(1)}, bf16[192,1536]{1,0:T(8,128)(2,1)S(1)}, u32[]{:S(2)}, u32[]{:S(2)}) %collective-permute-start.41) | collective-permute-done | bytes 589856 | tf_op jit(solution)/shard_map/ppermute | solution.py:465
  266.6 8.2 %collective-permute-done.61 = bf16[384,768]{1,0:T(8,128)(2,1)S(1)} collective-permute-done((bf16[384,768]{1,0:T(8,128)(2,1)S(1)}, bf16[384,768]{1,0:T(8,128)(2,1)S(1)}, u32[]{:S(2)}, u32[]{:S(2)}) %collective-permute-start.61) | collective-permute-done | bytes 589856 | tf_op jit(solution)/shard_map/ppermute | solution.py:465
  279.2 4.8 %collective-permute-done.17 = bf16[96,1536]{1,0:T(8,128)(2,1)S(1)} collective-permute-done((bf16[96,1536]{1,0:T(8,128)(2,1)S(1)}, bf16[96,1536]{1,0:T(8,128)(2,1)S(1)}, u32[]{:S(2)}, u32[]{:S(2)}) %collective-permute-start.17) | collective-permute-done | bytes 294944 | tf_op jit(solution)/shard_map/ppermute | solution.py:465
  300.9 3.1 collective-permute-start.19
  306.2 3.0 collective-permute-start.44
  315.5 5.0 %collective-permute-done.9 = bf16[24,1536]{1,0:T(8,128)(2,1)S(1)} collective-permute-done((bf16[24,1536]{1,0:T(8,128)(2,1)S(1)}, bf16[24,1536]{1,0:T(8,128)(2,1)S(1)}, u32[]{:S(2)}, u32[]{:S(2)}) %collective-permute-start.9) | collective-permute-done | bytes 73760 | tf_op jit(solution)/shard_map/ppermute | solution.py:465
  326.2 4.5 collective-permute-done.64
  374.7 13.7 %collective-permute-done.23 = bf16[192,1536]{1,0:T(8,128)(2,1)S(1)} collective-permute-done((bf16[192,1536]{1,0:T(8,128)(2,1)S(1)}, bf16[192,1536]{1,0:T(8,128)(2,1)S(1)}, u32[]{:S(2)}, u32[]{:S(2)}) %collective-permute-start.23) | collective-permute-done | bytes 589856 | tf_op jit(solution)/shard_map/ppermute | solution.py:465
  393.6 7.4 %collective-permute-done.48 = bf16[192,1536]{1,0:T(8,128)(2,1)S(1)} collective-permute-done((bf16[192,1536]{1,0:T(8,128)(2,1)S(1)}, bf16[192,1536]{1,0:T(8,128)(2,1)S(1)}, u32[]{:S(2)}, u32[]{:S(2)}) %collective-permute-start.48) | collective-permute-done | bytes 589856 | tf_op jit(solution)/shard_map/ppermute | solution.py:465
  405.7 6.8 %collective-permute-done.68 = bf16[384,768]{1,0:T(8,128)(2,1)S(1)} collective-permute-done((bf16[384,768]{1,0:T(8,128)(2,1)S(1)}, bf16[384,768]{1,0:T(8,128)(2,1)S(1)}, u32[]{:S(2)}, u32[]{:S(2)}) %collective-permute-start.68) | collective-permute-done | bytes 589856 | tf_op jit(solution)/shard_map/ppermute | solution.py:465
  417.2 3.1 fusion.9
  420.4 3.2 fusion.11
  423.6 3.4 fusion.5
  427.0 3.2 fusion.7
  431.8 4.2 fusion.1
  436.0 3.4 maximum_convert_fusion.2
  439.5 5.2 %maximum_convert_fusion = f32[768,3072]{1,0:T(8,128)} fusion(bf16[768,1536]{1,0:T(8,128)(2,1)S(1)} %fusion.5, bf16[768,1536]{1,0:T(8,128)(2,1)S(1)} %fusion.7), kind=kLoop, calls=%fused_computation | loop fusion | flops 9437184 | bytes 14155776 | tf_op jit(solution)/shard_map/convert_element_type | solution.py:565
  444.7 4.2 fusion.3
  448.9 4.5 maximum_convert_fusion.1
  (347 shorter events, 200.5 us)
Async XLA Ops:
  86.1 25.9 %collective-permute-start.4 = (bf16[256,768]{1,0:T(8,128)(2,1)}, bf16[256,768]{1,0:T(8,128)(2,1)}, u32[]{:S(2)}, u32[]{:S(2)}) collective-permute-start(bf16[256,768]{1,0:T(8,128)(2,1)} %fusion.43), channel_id=1, source_target_pairs={{0,16},{16,0},{1,17},{17,1},{2,18},{18,2},{3,19},{19,3},{4,20},{20... | collective-permute-start | bytes 1179656 | tf_op jit(solution)/shard_map/ppermute | solution.py:465
  178.7 51.0 %collective-permute-start.15 = (bf16[384,1536]{1,0:T(8,128)(2,1)}, bf16[384,1536]{1,0:T(8,128)(2,1)}, u32[]{:S(2)}, u32[]{:S(2)}) collective-permute-start(bf16[384,1536]{1,0:T(8,128)(2,1)} %fusion.24), channel_id=1, source_target_pairs={{0,16},{16,0},{1,17},{17,1},{2,18},{18,2},{3,19},{19,3},{4,20},{20... | collective-permute-start | bytes 3538952 | tf_op jit(solution)/shard_map/ppermute | solution.py:465
  180.3 52.9 %collective-permute-start.5 = (bf16[384,1536]{1,0:T(8,128)(2,1)}, bf16[384,1536]{1,0:T(8,128)(2,1)}, u32[]{:S(2)}, u32[]{:S(2)}) collective-permute-start(bf16[384,1536]{1,0:T(8,128)(2,1)} %constant_dynamic-slice_fusion.4), channel_id=1, source_target_pairs={{0,16},{16,0},{1,17},{17,1},{2,18},{18,2},{3,19},{19,3},{4,20},{20... | collective-permute-start | bytes 3538952 | tf_op jit(solution)/shard_map/ppermute | solution.py:465
  181.6 24.3 %collective-permute-start.25 = (f32[12,768]{1,0:T(8,128)S(1)}, f32[12,768]{1,0:T(8,128)S(1)}, u32[]{:S(2)}, u32[]{:S(2)}) collective-permute-start(f32[12,768]{1,0:T(8,128)S(1)} %pad_maximum_fusion.1), channel_id=1, source_target_pairs={{0,16},{16,0},{1,17},{17,1},{2,18},{18,2},{3,19},{19,3},{4,20},{20... | collective-permute-start | bytes 110600 | tf_op jit(solution)/shard_map/ppermute | solution.py:465
  196.9 39.2 %collective-permute-start.40 = (bf16[384,1536]{1,0:T(8,128)(2,1)}, bf16[384,1536]{1,0:T(8,128)(2,1)}, u32[]{:S(2)}, u32[]{:S(2)}) collective-permute-start(bf16[384,1536]{1,0:T(8,128)(2,1)} %constant_dynamic-slice_fusion), channel_id=1, source_target_pairs={{0,16},{16,0},{1,17},{17,1},{2,18},{18,2},{3,19},{19,3},{4,20},{20... | collective-permute-start | bytes 3538952 | tf_op jit(solution)/shard_map/ppermute | solution.py:465
  213.3 25.7 %collective-permute-start.30 = (bf16[384,1536]{1,0:T(8,128)(2,1)}, bf16[384,1536]{1,0:T(8,128)(2,1)S(1)}, u32[]{:S(2)}, u32[]{:S(2)}) collective-permute-start(bf16[384,1536]{1,0:T(8,128)(2,1)} %constant_dynamic-slice_fusion.1), channel_id=1, source_target_pairs={{0,16},{16,0},{1,17},{17,1},{2,18},{18,2},{3,19},{19,3},{4,20},{20... | collective-permute-start | bytes 3538952 | tf_op jit(solution)/shard_map/ppermute | solution.py:465
  236.1 16.3 %collective-permute-start.6 = (bf16[192,1536]{1,0:T(8,128)(2,1)S(1)}, bf16[192,1536]{1,0:T(8,128)(2,1)S(1)}, u32[]{:S(2)}, u32[]{:S(2)}) collective-permute-start(bf16[192,1536]{1,0:T(8,128)(2,1)S(1)} %add_convert_fusion.5), channel_id=1, source_target_pairs={{0,1},{1,0},{2,3},{3,2},{4,5},{5,4},{6,7},{7,6},{8,9},{9,8},{10,11... | collective-permute-start | bytes 1769480 | tf_op jit(solution)/shard_map/ppermute | solution.py:465
  239.0 23.1 %collective-permute-start.41 = (bf16[192,1536]{1,0:T(8,128)(2,1)S(1)}, bf16[192,1536]{1,0:T(8,128)(2,1)S(1)}, u32[]{:S(2)}, u32[]{:S(2)}) collective-permute-start(bf16[192,1536]{1,0:T(8,128)(2,1)S(1)} %add_convert_fusion.2), channel_id=1, source_target_pairs={{0,2},{1,3},{2,0},{3,1},{4,6},{5,7},{6,4},{7,5},{8,10},{9,11},{10,... | collective-permute-start | bytes 1769480 | tf_op jit(solution)/shard_map/ppermute | solution.py:465
  239.9 25.1 %collective-permute-start.31 = (bf16[192,1536]{1,0:T(8,128)(2,1)S(1)}, bf16[192,1536]{1,0:T(8,128)(2,1)S(1)}, u32[]{:S(2)}, u32[]{:S(2)}) collective-permute-start(bf16[192,1536]{1,0:T(8,128)(2,1)S(1)} %add_convert_fusion.3), channel_id=1, source_target_pairs={{0,1},{1,0},{2,3},{3,2},{4,5},{5,4},{6,7},{7,6},{8,9},{9,8},{10,11... | collective-permute-start | bytes 1769480 | tf_op jit(solution)/shard_map/ppermute | solution.py:465
  242.0 32.8 %collective-permute-start.61 = (bf16[384,768]{1,0:T(8,128)(2,1)S(1)}, bf16[384,768]{1,0:T(8,128)(2,1)S(1)}, u32[]{:S(2)}, u32[]{:S(2)}) collective-permute-start(bf16[384,768]{1,0:T(8,128)(2,1)S(1)} %add_convert_fusion), channel_id=1, source_target_pairs={{0,2},{1,3},{2,0},{3,1},{4,6},{5,7},{6,4},{7,5},{8,10},{9,11},{10,... | collective-permute-start | bytes 1769480 | tf_op jit(solution)/shard_map/ppermute | solution.py:465
  249.5 28.2 %collective-permute-start.51 = (bf16[384,768]{1,0:T(8,128)(2,1)S(1)}, bf16[384,768]{1,0:T(8,128)(2,1)S(1)}, u32[]{:S(2)}, u32[]{:S(2)}) collective-permute-start(bf16[384,768]{1,0:T(8,128)(2,1)S(1)} %add_convert_fusion.1), channel_id=1, source_target_pairs={{0,1},{1,0},{2,3},{3,2},{4,5},{5,4},{6,7},{7,6},{8,9},{9,8},{10,11... | collective-permute-start | bytes 1769480 | tf_op jit(solution)/shard_map/ppermute | solution.py:465
  252.4 31.6 %collective-permute-start.17 = (bf16[96,1536]{1,0:T(8,128)(2,1)S(1)}, bf16[96,1536]{1,0:T(8,128)(2,1)S(1)}, u32[]{:S(2)}, u32[]{:S(2)}) collective-permute-start(bf16[96,1536]{1,0:T(8,128)(2,1)S(1)} %add_convert_fusion.10), channel_id=1, source_target_pairs={{0,1},{1,0},{2,3},{3,2},{4,5},{5,4},{6,7},{7,6},{8,9},{9,8},{10,11... | collective-permute-start | bytes 884744 | tf_op jit(solution)/shard_map/ppermute | solution.py:465
  262.1 23.6 %collective-permute-start.7 = (bf16[96,1536]{1,0:T(8,128)(2,1)S(1)}, bf16[96,1536]{1,0:T(8,128)(2,1)S(1)}, u32[]{:S(2)}, u32[]{:S(2)}) collective-permute-start(bf16[96,1536]{1,0:T(8,128)(2,1)S(1)} %add_convert_fusion.11), channel_id=1, source_target_pairs={{0,2},{1,3},{2,0},{3,1},{4,6},{5,7},{6,4},{7,5},{8,10},{9,11},{10,... | collective-permute-start | bytes 884744 | tf_op jit(solution)/shard_map/ppermute | solution.py:465
  265.0 25.3 %collective-permute-start.42 = (bf16[96,1536]{1,0:T(8,128)(2,1)S(1)}, bf16[96,1536]{1,0:T(8,128)(2,1)S(1)}, u32[]{:S(2)}, u32[]{:S(2)}) collective-permute-start(bf16[96,1536]{1,0:T(8,128)(2,1)S(1)} %add_convert_fusion.8), channel_id=1, source_target_pairs={{0,1},{1,0},{2,3},{3,2},{4,5},{5,4},{6,7},{7,6},{8,9},{9,8},{10,11... | collective-permute-start | bytes 884744 | tf_op jit(solution)/shard_map/ppermute | solution.py:465
  274.7 17.9 %collective-permute-start.32 = (bf16[96,1536]{1,0:T(8,128)(2,1)S(1)}, bf16[96,1536]{1,0:T(8,128)(2,1)S(1)}, u32[]{:S(2)}, u32[]{:S(2)}) collective-permute-start(bf16[96,1536]{1,0:T(8,128)(2,1)S(1)} %add_convert_fusion.9), channel_id=1, source_target_pairs={{0,2},{1,3},{2,0},{3,1},{4,6},{5,7},{6,4},{7,5},{8,10},{9,11},{10,... | collective-permute-start | bytes 884744 | tf_op jit(solution)/shard_map/ppermute | solution.py:465
  277.7 17.7 %collective-permute-start.62 = (bf16[192,768]{1,0:T(8,128)(2,1)S(1)}, bf16[192,768]{1,0:T(8,128)(2,1)S(1)}, u32[]{:S(2)}, u32[]{:S(2)}) collective-permute-start(bf16[192,768]{1,0:T(8,128)(2,1)S(1)} %add_convert_fusion.6), channel_id=1, source_target_pairs={{0,1},{1,0},{2,3},{3,2},{4,5},{5,4},{6,7},{7,6},{8,9},{9,8},{10,11... | collective-permute-start | bytes 884744 | tf_op jit(solution)/shard_map/ppermute | solution.py:465
  309.2 16.3 %collective-permute-start.34 = (bf16[24,1536]{1,0:T(8,128)(2,1)S(1)}, bf16[24,1536]{1,0:T(8,128)(2,1)S(1)}, u32[]{:S(2)}, u32[]{:S(2)}) collective-permute-start(bf16[24,1536]{1,0:T(8,128)(2,1)S(1)} %add_convert_fusion.25), channel_id=1, source_target_pairs={{0,8},{1,9},{2,10},{3,11},{4,12},{5,13},{6,14},{7,15},{8,0},{9,1},... | collective-permute-start | bytes 221192 | tf_op jit(solution)/shard_map/ppermute | solution.py:465
  311.4 19.3 %collective-permute-start.64 = (bf16[48,768]{1,0:T(8,128)(2,1)S(1)}, bf16[48,768]{1,0:T(8,128)(2,1)S(1)}, u32[]{:S(2)}, u32[]{:S(2)}) collective-permute-start(bf16[48,768]{1,0:T(8,128)(2,1)S(1)} %add_convert_fusion.19), channel_id=1, source_target_pairs={{0,8},{1,9},{2,10},{3,11},{4,12},{5,13},{6,14},{7,15},{8,0},{9,1},... | collective-permute-start | bytes 221192 | tf_op jit(solution)/shard_map/ppermute | solution.py:465
  313.4 21.3 %collective-permute-start.54 = (bf16[48,768]{1,0:T(8,128)(2,1)S(1)}, bf16[48,768]{1,0:T(8,128)(2,1)S(1)}, u32[]{:S(2)}, u32[]{:S(2)}) collective-permute-start(bf16[48,768]{1,0:T(8,128)(2,1)S(1)} %add_convert_fusion.21), channel_id=1, source_target_pairs={{0,8},{1,9},{2,10},{3,11},{4,12},{5,13},{6,14},{7,15},{8,0},{9,1},... | collective-permute-start | bytes 221192 | tf_op jit(solution)/shard_map/ppermute | solution.py:465
  320.5 16.6 %collective-permute-start.20 = (bf16[24,1536]{1,0:T(8,128)(2,1)S(1)}, bf16[24,1536]{1,0:T(8,128)(2,1)S(1)}, u32[]{:S(2)}, u32[]{:S(2)}) collective-permute-start(bf16[24,1536]{1,0:T(8,128)(2,1)S(1)} %add_convert_fusion.26), channel_id=1, source_target_pairs={{0,8},{1,9},{2,10},{3,11},{4,12},{5,13},{6,14},{7,15},{8,0},{9,1},... | collective-permute-start | bytes 221192 | tf_op jit(solution)/shard_map/ppermute | solution.py:465
  322.0 16.7 %collective-permute-start.10 = (bf16[24,1536]{1,0:T(8,128)(2,1)S(1)}, bf16[24,1536]{1,0:T(8,128)(2,1)S(1)}, u32[]{:S(2)}, u32[]{:S(2)}) collective-permute-start(bf16[24,1536]{1,0:T(8,128)(2,1)S(1)} %add_convert_fusion.28), channel_id=1, source_target_pairs={{0,8},{1,9},{2,10},{3,11},{4,12},{5,13},{6,14},{7,15},{8,0},{9,1},... | collective-permute-start | bytes 221192 | tf_op jit(solution)/shard_map/ppermute | solution.py:465
  364.3 27.9 %collective-permute-start.57 = (bf16[192,768]{1,0:T(8,128)(2,1)S(1)}, bf16[192,768]{1,0:T(8,128)(2,1)S(1)}, u32[]{:S(2)}, u32[]{:S(2)}) collective-permute-start(bf16[192,768]{1,0:T(8,128)(2,1)S(1)} %fusion.56), channel_id=1, source_target_pairs={{0,2},{1,3},{2,0},{3,1},{4,6},{5,7},{6,4},{7,5},{8,10},{9,11},{10,... | collective-permute-start | bytes 884744 | tf_op jit(solution)/shard_map/ppermute | solution.py:465
  365.0 23.3 %collective-permute-start.23 = (bf16[192,1536]{1,0:T(8,128)(2,1)S(1)}, bf16[192,1536]{1,0:T(8,128)(2,1)S(1)}, u32[]{:S(2)}, u32[]{:S(2)}) collective-permute-start(bf16[192,1536]{1,0:T(8,128)(2,1)S(1)} %fusion.38), channel_id=1, source_target_pairs={{0,2},{1,3},{2,0},{3,1},{4,6},{5,7},{6,4},{7,5},{8,10},{9,11},{10,... | collective-permute-start | bytes 1769480 | tf_op jit(solution)/shard_map/ppermute | solution.py:465
  367.7 22.9 %collective-permute-start.13 = (bf16[192,1536]{1,0:T(8,128)(2,1)S(1)}, bf16[192,1536]{1,0:T(8,128)(2,1)S(1)}, u32[]{:S(2)}, u32[]{:S(2)}) collective-permute-start(bf16[192,1536]{1,0:T(8,128)(2,1)S(1)} %fusion.40), channel_id=1, source_target_pairs={{0,1},{1,0},{2,3},{3,2},{4,5},{5,4},{6,7},{7,6},{8,9},{9,8},{10,11... | collective-permute-start | bytes 1769480 | tf_op jit(solution)/shard_map/ppermute | solution.py:465
  369.3 31.6 %collective-permute-start.48 = (bf16[192,1536]{1,0:T(8,128)(2,1)S(1)}, bf16[192,1536]{1,0:T(8,128)(2,1)S(1)}, u32[]{:S(2)}, u32[]{:S(2)}) collective-permute-start(bf16[192,1536]{1,0:T(8,128)(2,1)S(1)} %fusion.34), channel_id=1, source_target_pairs={{0,2},{1,3},{2,0},{3,1},{4,6},{5,7},{6,4},{7,5},{8,10},{9,11},{10,... | collective-permute-start | bytes 1769480 | tf_op jit(solution)/shard_map/ppermute | solution.py:465
  372.4 31.3 %collective-permute-start.38 = (bf16[192,1536]{1,0:T(8,128)(2,1)S(1)}, bf16[192,1536]{1,0:T(8,128)(2,1)S(1)}, u32[]{:S(2)}, u32[]{:S(2)}) collective-permute-start(bf16[192,1536]{1,0:T(8,128)(2,1)S(1)} %fusion.36), channel_id=1, source_target_pairs={{0,1},{1,0},{2,3},{3,2},{4,5},{5,4},{6,7},{7,6},{8,9},{9,8},{10,11... | collective-permute-start | bytes 1769480 | tf_op jit(solution)/shard_map/ppermute | solution.py:465
  388.3 24.2 %collective-permute-start.68 = (bf16[384,768]{1,0:T(8,128)(2,1)S(1)}, bf16[384,768]{1,0:T(8,128)(2,1)S(1)}, u32[]{:S(2)}, u32[]{:S(2)}) collective-permute-start(bf16[384,768]{1,0:T(8,128)(2,1)S(1)} %fusion.30), channel_id=1, source_target_pairs={{0,2},{1,3},{2,0},{3,1},{4,6},{5,7},{6,4},{7,5},{8,10},{9,11},{10,... | collective-permute-start | bytes 1769480 | tf_op jit(solution)/shard_map/ppermute | solution.py:465
  390.6 26.5 %collective-permute-start.24 = (bf16[384,1536]{1,0:T(8,128)(2,1)S(1)}, bf16[384,1536]{1,0:T(8,128)(2,1)S(1)}, u32[]{:S(2)}, u32[]{:S(2)}) collective-permute-start(bf16[384,1536]{1,0:T(8,128)(2,1)S(1)} %fusion.21), channel_id=1, source_target_pairs={{0,16},{16,0},{1,17},{17,1},{2,18},{18,2},{3,19},{19,3},{4,20},{20... | collective-permute-start | bytes 3538952 | tf_op jit(solution)/shard_map/ppermute | solution.py:465
  392.1 28.2 %collective-permute-start.14 = (bf16[384,1536]{1,0:T(8,128)(2,1)S(1)}, bf16[384,1536]{1,0:T(8,128)(2,1)S(1)}, u32[]{:S(2)}, u32[]{:S(2)}) collective-permute-start(bf16[384,1536]{1,0:T(8,128)(2,1)S(1)} %fusion.23), channel_id=1, source_target_pairs={{0,16},{16,0},{1,17},{17,1},{2,18},{18,2},{3,19},{19,3},{4,20},{20... | collective-permute-start | bytes 3538952 | tf_op jit(solution)/shard_map/ppermute | solution.py:465
  403.7 19.8 %collective-permute-start.49 = (bf16[384,1536]{1,0:T(8,128)(2,1)S(1)}, bf16[384,1536]{1,0:T(8,128)(2,1)S(1)}, u32[]{:S(2)}, u32[]{:S(2)}) collective-permute-start(bf16[384,1536]{1,0:T(8,128)(2,1)S(1)} %fusion.17), channel_id=1, source_target_pairs={{0,16},{16,0},{1,17},{17,1},{2,18},{18,2},{3,19},{19,3},{4,20},{20... | collective-permute-start | bytes 3538952 | tf_op jit(solution)/shard_map/ppermute | solution.py:465
  414.6 17.3 %collective-permute-start.69 = (bf16[768,768]{1,0:T(8,128)(2,1)S(1)}, bf16[768,768]{1,0:T(8,128)(2,1)S(1)}, u32[]{:S(2)}, u32[]{:S(2)}) collective-permute-start(bf16[768,768]{1,0:T(8,128)(2,1)S(1)} %fusion.13), channel_id=1, source_target_pairs={{0,16},{16,0},{1,17},{17,1},{2,18},{18,2},{3,19},{19,3},{4,20},{20... | collective-permute-start | bytes 3538952 | tf_op jit(solution)/shard_map/ppermute | solution.py:465
  417.1 27.6 %collective-permute-start.59 = (bf16[768,768]{1,0:T(8,128)(2,1)S(1)}, bf16[768,768]{1,0:T(8,128)(2,1)S(1)}, u32[]{:S(2)}, u32[]{:S(2)}) collective-permute-start(bf16[768,768]{1,0:T(8,128)(2,1)S(1)} %fusion.15), channel_id=1, source_target_pairs={{0,16},{16,0},{1,17},{17,1},{2,18},{18,2},{3,19},{19,3},{4,20},{20... | collective-permute-start | bytes 3538952 | tf_op jit(solution)/shard_map/ppermute | solution.py:465
  (93 other events, 976.9 us)

commit v2 on v1

v2 whole, which is shorter than its diff:
```python
import math

import jax
import jax.numpy as jnp
from jax import lax
from jax.experimental import pallas as pl
from jax.experimental.pallas import tpu as pltpu
from jax.sharding import PartitionSpec as P

HEAD_DIM = 64
SEQ = 64
GROUP = 16
CHUNK = 512

epsilon = 1e-06
score_scale = 10.0
margin_shift = score_scale * 0.3
root_half = 0.7071067811865476
gauss_norm = 0.3989422804014327

low = jnp.bfloat16
wide = jnp.float32
ANY = pl.BlockSpec(memory_space=pl.ANY)


def struct(shape, dtype):
    return jax.ShapeDtypeStruct(shape, dtype)


def whole(shape):
    return pl.BlockSpec(shape, lambda *_: (0,) * len(shape))


def call(body, grid, ins, outs, bits=None, scratch=(), aliases=None, after=(), limit=60):
    n_in, n_bits = len(ins), 0 if bits is None else 1

    def wrapped(*refs):
        body(*refs[: n_bits + n_in], *refs[n_bits + n_in + len(after) :])

    return pl.pallas_call(
        wrapped,
        grid_spec=pltpu.PrefetchScalarGridSpec(
            num_scalar_prefetch=n_bits,
            grid=grid,
            in_specs=[s for s, _ in ins] + [ANY] * len(after),
            out_specs=[s for s, _ in outs],
            scratch_shapes=list(scratch),
        ),
        out_shape=[s for _, s in outs],
        input_output_aliases={n_bits + k: v for k, v in (aliases or {}).items()},
        cost_estimate=pl.CostEstimate(flops=0, bytes_accessed=0, transcendentals=0),
        compiler_params=pltpu.CompilerParams(vmem_limit_bytes=limit << 20),
    )(*([] if bits is None else [bits]), *[a for _, a in ins], *after)


def mat_mul(a, b):
    return jnp.dot(a, b, preferred_element_type=wide)


def trans_left(a, b):
    return lax.dot_general(a, b, (((0,), (0,)), ((), ())), preferred_element_type=wide)


def trans_right(a, b):
    return lax.dot_general(a, b, (((1,), (1,)), ((), ())), preferred_element_type=wide)


def normalize(h):
    center = h - jnp.mean(h, axis=-1, keepdims=True)
    inv = lax.rsqrt(jnp.mean(center * center, axis=-1, keepdims=True) + epsilon)
    return center * inv, inv


def norm_input_grad(grad, normed, inv):
    return inv * (
        grad
        - jnp.mean(grad, axis=-1, keepdims=True)
        - normed * jnp.mean(grad * normed, axis=-1, keepdims=True)
    )


def split_heads(pair, first):
    zero = jnp.zeros_like(pair)
    return jnp.concatenate([jnp.where(first, pair, zero), jnp.where(first, zero, pair)], axis=0)


def join_heads(rows, first):
    return jnp.where(first, rows[:SEQ], rows[SEQ:])


class Rows:
    def __init__(self, width, ffn):
        self.at, start = {}, 0
        for name, size in (
            ("qkv", 3 * width), ("out", width), ("gain1", width), ("bias1", width), ("in", ffn),
            ("down", width), ("gain2", width), ("bias2", width), ("pool", width),
        ):
            self.at[name] = (start, size)
            start += size
        self.size = start

    def read(self, ref, name, start=0, size=None):
        base, full = self.at[name]
        return ref[:, base + start : base + start + (full if size is None else size)]


def attention_forward(x, w_qkv, w_out, pack, rows_of):
    tokens, width = x.shape
    rows = 4 * SEQ
    pairs = width // (2 * HEAD_DIM)
    scale = 1.0 / math.sqrt(HEAD_DIM)

    def body(x_ref, wq_ref, wo_ref, pack_ref, proj_ref, prob_ref, ctx_ref, hid_ref, low_ref, inv_ref):
        x_in = x_ref[...]
        for part in range(3):
            c = slice(part * width, (part + 1) * width)
            proj_ref[:, c] = (mat_mul(x_in, wq_ref[:, c]) + rows_of.read(pack_ref, "qkv", part * width, width)).astype(low)
        first = lax.broadcasted_iota(jnp.int32, (SEQ, 128), 1) < HEAD_DIM
        cols = [slice(p * 128, (p + 1) * 128) for p in range(pairs)]
        for sent in range(4):
            r = slice(sent * SEQ, (sent + 1) * SEQ)
            q = proj_ref[r, :width]
            k = proj_ref[r, width : 2 * width]
            v = proj_ref[r, 2 * width :]
            scores = jnp.concatenate([trans_right(k[:, c], split_heads(q[:, c], first)) for c in cols], axis=1) * scale
            e = jnp.exp(scores - jnp.max(scores, axis=0, keepdims=True))
            probs = (e * (1.0 / jnp.sum(e, axis=0, keepdims=True))).astype(low)
            prob_ref[r, :] = probs
            ctx_ref[r, :] = jnp.concatenate(
                [join_heads(trans_left(probs[:, c], v[:, c]), first) for c in cols], axis=1
            ).astype(low)
        h = x_in.astype(wide) + mat_mul(ctx_ref[...], wo_ref[...]) + rows_of.read(pack_ref, "out")
        normed, inv = normalize(h)
        hidden = normed * rows_of.read(pack_ref, "gain1") + rows_of.read(pack_ref, "bias1")
        hid_ref[...] = hidden
        low_ref[...] = hidden.astype(low)
        inv_ref[...] = inv

    row = lambda cols: pl.BlockSpec((rows, cols), lambda i, *_: (i, 0))
    return call(
        body,
        (tokens // rows,),
        [(row(width), x), (whole(w_qkv.shape), w_qkv), (whole(w_out.shape), w_out), (whole(pack.shape), pack)],
        [
            (row(3 * width), struct((tokens, 3 * width), low)),
            (row(width), struct((tokens, width), low)),
            (row(width), struct((tokens, width), low)),
            (row(width), struct((tokens, width), wide)),
            (row(width), struct((tokens, width), low)),
            (row(1), struct((tokens, 1), wide)),
        ],
    )


class Streamed:
    def __init__(self, source, target, sems, axis):
        self.copies = []
        for n in range(source.shape[axis] // CHUNK):
            at = (slice(None),) * axis + (pl.ds(n * CHUNK, CHUNK),)
            self.copies.append(pltpu.make_async_copy(source.at[at], target.at[at], sems.at[n]))

    def start(self, n):
        self.copies[n].start()

    def wait(self, n):
        self.copies[n].wait()


def ffn_forward_rows(hidden, wi_ref, wd_ref, pack_ref, rows_of, wait, store_act, store_slope):
    h_low = hidden.astype(low)
    total = hidden + rows_of.read(pack_ref, "down")
    for n in range(wi_ref.shape[1] // CHUNK):
        c = n * CHUNK
        wait(n)
        u = mat_mul(h_low, wi_ref[:, c : c + CHUNK]) + rows_of.read(pack_ref, "in", c, CHUNK)
        phi = 0.5 + 0.5 * lax.erf(u * root_half)
        act = (u * phi).astype(low)
        store_act(c, act)
        store_slope(c, (phi + u * jnp.exp(-0.5 * u * u) * gauss_norm).astype(low))
        total = total + mat_mul(act, wd_ref[c : c + CHUNK, :])
    return normalize(total)


def ffn_backward_rows(grad_block, normed, inv, gain, wd_ref, wait, slope_of, store_gate, small_ref, bin_ref):
    grad_two = norm_input_grad(grad_block * gain, normed, inv)
    small_ref[0:1, :] += jnp.sum(grad_block * normed, axis=0, keepdims=True)
    small_ref[1:2, :] += jnp.sum(grad_block, axis=0, keepdims=True)
    small_ref[2:3, :] += jnp.sum(grad_two, axis=0, keepdims=True)
    grad_low = grad_two.astype(low)
    for n in range(wd_ref.shape[0] // CHUNK):
        c = n * CHUNK
        wait(n)
        gate = trans_right(grad_low, wd_ref[c : c + CHUNK, :]) * slope_of(c).astype(wide)
        bin_ref[:, c : c + CHUNK] += jnp.sum(gate, axis=0, keepdims=True)
        store_gate(c, gate.astype(low))
    return grad_low


def group_spec(sents, cols, index):
    return pl.BlockSpec((sents, GROUP, cols), lambda i, *_: (0, index, 0))


def ffn_scratch(width, ffn):
    parts = ffn // CHUNK
    return [
        pltpu.VMEM((width, ffn), low),
        pltpu.VMEM((ffn, width), low),
        pltpu.SemaphoreType.DMA((parts,)),
        pltpu.SemaphoreType.DMA((parts,)),
    ]


def start_ffn_weights(wi_hbm, wd_hbm, wi_ref, wd_ref, sem_i, sem_d):
    stream_i = Streamed(wi_hbm, wi_ref, sem_i, 1)
    stream_d = Streamed(wd_hbm, wd_ref, sem_d, 0)
    for n in range(len(stream_i.copies)):
        stream_i.start(n)
        stream_d.start(n)

    def wait(n):
        stream_i.wait(n)
        stream_d.wait(n)

    return wait


def ffn_first(hidden, w_in, w_down, pack, rows_of):
    sents, _, width = hidden.shape
    ffn = w_in.shape[1]
    rows = sents * GROUP

    def body(h_ref, wi_hbm, wd_hbm, pack_ref, enc_ref, act_ref, slope_ref, n_ref, inv_ref, first_ref, wi_ref, wd_ref, sem_i, sem_d):
        wait = start_ffn_weights(wi_hbm, wd_hbm, wi_ref, wd_ref, sem_i, sem_d)

        def store_act(c, v):
            act_ref[:, :, c : c + CHUNK] = v.reshape(sents, GROUP, CHUNK)

        def store_slope(c, v):
            slope_ref[:, c : c + CHUNK] = v

        normed, inv = ffn_forward_rows(
            h_ref[...].reshape(rows, width), wi_ref, wd_ref, pack_ref, rows_of, wait, store_act, store_slope
        )
        n_ref[...] = normed
        inv_ref[...] = inv
        block = (normed * rows_of.read(pack_ref, "gain2") + rows_of.read(pack_ref, "bias2")).reshape(sents, GROUP, width)
        enc_ref[...] = block.astype(low)
        first_ref[...] = block[:, 0, :].astype(low)

    return call(
        body,
        (1,),
        [(group_spec(sents, width, 0), hidden), (ANY, w_in), (ANY, w_down), (whole(pack.shape), pack)],
        [
            (group_spec(sents, width, 0), struct((sents, SEQ, width), low)),
            (group_spec(sents, ffn, 0), struct((sents, SEQ, ffn), low)),
            (whole((rows, ffn)), struct((rows, ffn), low)),
            (whole((rows, width)), struct((rows, width), wide)),
            (whole((rows, 1)), struct((rows, 1), wide)),
            (whole((sents, width)), struct((sents, width), low)),
        ],
        scratch=ffn_scratch(width, ffn),
    )


def ffn_group(index, hidden, cot, w_in, w_down, pack, rows_of, encoded, act, gate, two, small, bin_sum, after=()):
    sents, _, width = hidden.shape
    ffn = w_in.shape[1]
    rows = sents * GROUP
    fresh = gate is None

    def body(h_ref, cot_ref, wi_hbm, wd_hbm, pack_ref, *refs):
        refs = refs[2 if fresh else 4 :]
        if not fresh:
            sin_ref, bin_in_ref = refs[:2]
            refs = refs[2:]
        enc_ref, act_ref, gate_ref, two_ref, small_ref, bin_ref, slope_ref, wi_ref, wd_ref, sem_i, sem_d = refs
        wait = start_ffn_weights(wi_hbm, wd_hbm, wi_ref, wd_ref, sem_i, sem_d)
        small_ref[...] = jnp.zeros_like(small_ref) if fresh else sin_ref[...]
        bin_ref[...] = jnp.zeros_like(bin_ref) if fresh else bin_in_ref[...]

        def store_act(c, v):
            act_ref[:, :, c : c + CHUNK] = v.reshape(sents, GROUP, CHUNK)

        def store_slope(c, v):
            slope_ref[:, c : c + CHUNK] = v

        def store_gate(c, v):
            gate_ref[:, :, c : c + CHUNK] = v.reshape(sents, GROUP, CHUNK)

        normed, inv = ffn_forward_rows(
            h_ref[...].reshape(rows, width), wi_ref, wd_ref, pack_ref, rows_of, wait, store_act, store_slope
        )
        gain = rows_of.read(pack_ref, "gain2")
        enc_ref[...] = (normed * gain + rows_of.read(pack_ref, "bias2")).astype(low).reshape(sents, GROUP, width)
        grad_block = cot_ref[...].reshape(rows, width).astype(wide)
        got = ffn_backward_rows(
            grad_block, normed, inv, gain, wd_ref, lambda n: None, lambda c: slope_ref[:, c : c + CHUNK], store_gate,
            small_ref, bin_ref,
        )
        two_ref[...] = got.reshape(sents, GROUP, width)

    spec = lambda cols: group_spec(sents, cols, index)
    kept = [(ANY, encoded), (ANY, act)]
    aliases = {5: 0, 6: 1}
    if not fresh:
        kept += [(ANY, gate), (ANY, two), (whole(small.shape), small), (whole(bin_sum.shape), bin_sum)]
        aliases.update({7: 2, 8: 3})
    return call(
        body,
        (1,),
        [(spec(width), hidden), (spec(width), cot), (ANY, w_in), (ANY, w_down), (whole(pack.shape), pack)] + kept,
        [
            (spec(width), struct((sents, SEQ, width), low)),
            (spec(ffn), struct((sents, SEQ, ffn), low)),
            (spec(ffn), struct((sents, SEQ, ffn), low)),
            (spec(width), struct((sents, SEQ, width), low)),
            (whole((8, width)), struct((8, width), wide)),
            (whole((1, ffn)), struct((1, ffn), wide)),
        ],
        scratch=[pltpu.VMEM((rows, ffn), low)] + ffn_scratch(width, ffn),
        aliases=aliases,
        after=after,
    )


def ffn_first_back(cot, grad_first, normed, inv, slope, w_down, pack, rows_of, gate, two, small, bin_sum, after=()):
    sents, _, width = cot.shape
    ffn = w_down.shape[0]
    rows = sents * GROUP

    def body(cot_ref, first_ref, n_ref, inv_ref, slope_ref, wd_hbm, pack_ref, sin_ref, bin_in_ref, _g, _t, gate_ref, two_ref, small_ref, bin_ref, wd_ref, sem):
        stream = Streamed(wd_hbm, wd_ref, sem, 0)
        for n in range(ffn // CHUNK):
            stream.start(n)
        small_ref[...] = sin_ref[...]
        bin_ref[...] = bin_in_ref[...]
        position = lax.broadcasted_iota(jnp.int32, (sents, GROUP, width), 1)
        at_first = jnp.broadcast_to(first_ref[...][:, None, :], (sents, GROUP, width))
        grad_block = cot_ref[...].astype(wide) + jnp.where(position == 0, at_first, 0.0)

        def store_gate(c, v):
            gate_ref[:, :, c : c + CHUNK] = v.reshape(sents, GROUP, CHUNK)

        got = ffn_backward_rows(
            grad_block.reshape(rows, width), n_ref[...], inv_ref[...], rows_of.read(pack_ref, "gain2"), wd_ref, stream.wait,
            lambda c: slope_ref[:, c : c + CHUNK], store_gate, small_ref, bin_ref,
        )
        two_ref[...] = got.reshape(sents, GROUP, width)

    return call(
        body,
        (1,),
        [
            (group_spec(sents, width, 0), cot),
            (whole((sents, width)), grad_first),
            (whole((rows, width)), normed),
            (whole((rows, 1)), inv),
            (whole((rows, ffn)), slope),
            (ANY, w_down),
            (whole(pack.shape), pack),
            (whole(small.shape), small),
            (whole(bin_sum.shape), bin_sum),
            (ANY, gate),
            (ANY, two),
        ],
        [
            (group_spec(sents, ffn, 0), struct((sents, SEQ, ffn), low)),
            (group_spec(sents, width, 0), struct((sents, SEQ, width), low)),
            (whole((8, width)), struct((8, width), wide)),
            (whole((1, ffn)), struct((1, ffn), wide)),
        ],
        scratch=[pltpu.VMEM((ffn, width), low), pltpu.SemaphoreType.DMA((ffn // CHUNK,))],
        aliases={9: 0, 10: 1},
        after=after,
    )


def lower_backward(part, parts, two, gate, hidden, inv, proj, probs, w_in, w_out, pack, rows_of, before=None, after=()):
    tokens, width = hidden.shape
    ffn = w_in.shape[1]
    rows = 4 * SEQ
    steps = tokens // rows // parts
    pairs = width // (2 * HEAD_DIM)
    scale = 1.0 / math.sqrt(HEAD_DIM)
    fresh = before is None

    def body(two_ref, gate_ref, hid_ref, inv_ref, proj_ref, prob_ref, wi_hbm, wo_ref, pack_ref, *refs):
        if not fresh:
            sin_ref, bin_ref = refs[2:4]
            refs = refs[4:]
        one_ref, gp_ref, small_ref, bqv_ref, ctx_ref, wi_ref, sem = refs
        stream = Streamed(wi_hbm, wi_ref, sem, 1)

        @pl.when(pl.program_id(0) == 0)
        def _():
            for n in range(ffn // CHUNK):
                stream.start(n)
            small_ref[...] = jnp.zeros_like(small_ref) if fresh else sin_ref[...]
            bqv_ref[...] = jnp.zeros_like(bqv_ref) if fresh else bin_ref[...]
            for n in range(ffn // CHUNK):
                stream.wait(n)

        gain = rows_of.read(pack_ref, "gain1")
        grad_hidden = two_ref[...].astype(wide) + trans_right(gate_ref[...], wi_ref[...])
        normed = (hid_ref[...] - rows_of.read(pack_ref, "bias1")) * (1.0 / gain)
        small_ref[0:1, :] += jnp.sum(grad_hidden * normed, axis=0, keepdims=True)
        small_ref[1:2, :] += jnp.sum(grad_hidden, axis=0, keepdims=True)
        grad_one = norm_input_grad(grad_hidden * gain, normed, inv_ref[...])
        small_ref[2:3, :] += jnp.sum(grad_one, axis=0, keepdims=True)
        one_low = grad_one.astype(low)
        one_ref[...] = one_low
        ctx_ref[...] = trans_right(one_low, wo_ref[...]).astype(low)
        first = lax.broadcasted_iota(jnp.int32, (SEQ, 128), 1) < HEAD_DIM
        sum_q = jnp.zeros((1, width), wide)
        sum_v = jnp.zeros((1, width), wide)
        cols = [slice(p * 128, (p + 1) * 128) for p in range(pairs)]
        for sent in range(4):
            r = slice(sent * SEQ, (sent + 1) * SEQ)
            q_all = proj_ref[r, :width]
            k = proj_ref[r, width : 2 * width]
            v = proj_ref[r, 2 * width :]
            d_all = ctx_ref[r, :]
            p_low = prob_ref[r, :]
            q = [split_heads(q_all[:, c], first) for c in cols]
            d = [split_heads(d_all[:, c], first) for c in cols]
            p = p_low.astype(wide)
            grad_p = jnp.concatenate([trans_right(v[:, c], dd) for c, dd in zip(cols, d)], axis=1)
            grad_v = jnp.concatenate([mat_mul(p_low[:, c], dd) for c, dd in zip(cols, d)], axis=1)
            gp = grad_p * p
            grad_s = (gp - p * jnp.sum(gp, axis=0, keepdims=True)).astype(low)
            grad_k = jnp.concatenate([mat_mul(grad_s[:, c], qq) for c, qq in zip(cols, q)], axis=1) * scale
            grad_q = (
                jnp.concatenate([join_heads(trans_left(grad_s[:, c], k[:, c]), first) for c in cols], axis=1) * scale
            )
            sum_q += jnp.sum(grad_q, axis=0, keepdims=True)
            sum_v += jnp.sum(grad_v, axis=0, keepdims=True)
            gp_ref[r, :width] = grad_q.astype(low)
            gp_ref[r, width : 2 * width] = grad_k.astype(low)
            gp_ref[r, 2 * width :] = grad_v.astype(low)
        bqv_ref[0:1, :] += sum_q
        bqv_ref[1:2, :] += sum_v

    row = lambda cols: pl.BlockSpec((rows, cols), lambda i, *_: (i + part * steps, 0))
    ins = [
        (row(width), two),
        (row(ffn), gate),
        (row(width), hidden),
        (row(1), inv),
        (row(3 * width), proj),
        (row(width), probs),
        (ANY, w_in),
        (whole(w_out.shape), w_out),
        (whole(pack.shape), pack),
    ]
    if not fresh:
        ins += [(ANY, before[0]), (ANY, before[1]), (whole((8, width)), before[2]), (whole((8, width)), before[3])]
    return call(
        body,
        (steps,),
        ins,
        [
            (row(width), struct((tokens, width), low)),
            (row(3 * width), struct((tokens, 3 * width), low)),
            (whole((8, width)), struct((8, width), wide)),
            (whole((8, width)), struct((8, width), wide)),
        ],
        scratch=[pltpu.VMEM((rows, width), low), pltpu.VMEM((width, ffn), low), pltpu.SemaphoreType.DMA((ffn // CHUNK,))],
        aliases=None if fresh else {9: 0, 10: 1},
        after=after,
    )


def input_gradient(grad_proj, w_qkv, grad_one, after=()):
    tokens, width = grad_one.shape
    rows = 4 * SEQ

    def body(gp_ref, w_ref, one_ref, out_ref):
        out_ref[...] = (one_ref[...].astype(wide) + trans_right(gp_ref[...], w_ref[...])).astype(low)

    row = lambda cols: pl.BlockSpec((rows, cols), lambda i, *_: (i, 0))
    return call(
        body,
        (tokens // rows,),
        [(row(3 * width), grad_proj), (whole(w_qkv.shape), w_qkv), (row(width), grad_one)],
        [(row(width), struct((tokens, width), low))],
        after=after,
    )[0]


def contrastive(first, ids, w_pool, b_pool):
    total = first.shape[1]
    flat = first.reshape(2 * total, -1)
    pooled = jnp.tanh(mat_mul(flat, w_pool) + b_pool)
    inv_len = lax.rsqrt(jnp.sum(pooled * pooled, axis=-1, keepdims=True) + epsilon)
    unit = pooled * inv_len
    embed = unit.astype(low)
    zero, one = embed[:total], embed[total:]
    same = ids[:, None] == ids[None, :]
    eye = (jnp.arange(total)[:, None] == jnp.arange(total)[None, :]).astype(wide)
    logits = score_scale * trans_right(zero, one) - margin_shift * eye
    masked = jnp.where(same, logits, -jnp.inf)

    def soft(axis):
        e = jnp.exp(masked - jnp.max(masked, axis=axis, keepdims=True))
        return (score_scale * (e / jnp.sum(e, axis=axis, keepdims=True) - eye)).astype(low)

    by_row, by_col = soft(1), soft(0)
    grad_embed = jnp.concatenate(
        [mat_mul(by_row, one) + mat_mul(by_col, one), trans_left(by_row, zero) + trans_left(by_col, zero)]
    )
    grad_pre = (
        inv_len * (grad_embed - unit * jnp.sum(unit * grad_embed, axis=-1, keepdims=True)) * (1.0 - pooled * pooled)
    )
    pre_low = grad_pre.astype(low)
    return pre_low, trans_left(flat, pre_low), jnp.sum(grad_pre, axis=0)


CORE, BIT0, BIT1, BIT2 = range(4)


def exchange(a, axis, mask):
    size = lax.axis_size(axis)
    return lax.ppermute(a, axis, [(i, i ^ mask) for i in range(size)])


class Sources:
    def __init__(self, pairs):
        self.pairs = pairs
        self.m = pairs[0][0].shape[1]
        self.n = sum(g.shape[1] for _, g in pairs)
        self.tokens = pairs[0][0].shape[0]


def gradient_rows(src, bits, recv, after=()):
    m, n, tokens = src.m, src.n, src.tokens
    keep = recv is not None
    by_rows = m > n
    half = m // 2
    tile = (half // 4, n) if by_rows else (half, n // 4)
    count = len(src.pairs)
    starts = []
    at = 0
    for _, g in src.pairs:
        starts.append(at)
        at += g.shape[1] // tile[1]
    starts.append(at)

    def row_block(core, i):
        mine = core if keep else 1 - core
        return mine * (half // tile[0]) + (i if by_rows else 0)

    ins = []
    for p, (a, g) in enumerate(src.pairs):
        ins.append((pl.BlockSpec((tokens, tile[0]), lambda i, b: (0, row_block(b[CORE], i))), a))
        lo, hi = starts[p], starts[p + 1]
        ins.append(
            (
                pl.BlockSpec(
                    (tokens, tile[1]), lambda i, b, lo=lo, hi=hi: (0, 0 if by_rows else jnp.clip(i - lo, 0, hi - lo - 1))
                ),
                g,
            )
        )
    tiled = pl.BlockSpec(tile, lambda i, b: (i, 0) if by_rows else (0, i))
    if not keep:

        def body(b, *refs):
            out = refs[2 * count]
            for p in range(count):

                def run(p=p):
                    out[...] = trans_left(refs[2 * p][...], refs[2 * p + 1][...]).astype(low)

                if count == 1:
                    run()
                else:
                    pl.when((pl.program_id(0) >= starts[p]) & (pl.program_id(0) < starts[p + 1]))(run)

        return call(body, (4,), ins, [(tiled, struct((half, n), low))], bits=bits, after=after)[0]

    ins.append((tiled, recv))
    quarter = (half // 2, n // 2)

    def body(b, *refs):
        got = refs[2 * count]
        left_send, left_keep, right_send, right_keep = refs[2 * count + 1 :]
        i = pl.program_id(0)

        def put(send_ref, keep_ref, bit, rows, cols, upper, value):
            @pl.when(b[bit] == upper)
            def _():
                keep_ref[rows, cols] = value.astype(low)

            @pl.when(b[bit] != upper)
            def _():
                send_ref[rows, cols] = value.astype(low)

        for p in range(count):

            def run(p=p):
                value = trans_left(refs[2 * p][...], refs[2 * p + 1][...]) + got[...].astype(wide)
                if by_rows:
                    rows = pl.ds(pl.multiple_of((i % 2) * tile[0], tile[0]), tile[0])
                    put(left_send, left_keep, BIT0, rows, slice(None), i // 2, value[:, : n // 2])
                    put(right_send, right_keep, BIT1, rows, slice(None), i // 2, value[:, n // 2 :])
                else:
                    cols = pl.ds(pl.multiple_of((i % 2) * tile[1], tile[1]), tile[1])

                    @pl.when(i < 2)
                    def _():
                        put(left_send, left_keep, BIT0, slice(None), cols, 0, value[: half // 2])
                        put(left_send, left_keep, BIT0, slice(None), cols, 1, value[half // 2 :])

                    @pl.when(i >= 2)
                    def _():
                        put(right_send, right_keep, BIT1, slice(None), cols, 0, value[: half // 2])
                        put(right_send, right_keep, BIT1, slice(None), cols, 1, value[half // 2 :])

            if count == 1:
                run()
            else:
                pl.when((i >= starts[p]) & (i < starts[p + 1]))(run)

    return call(body, (4,), ins, [(whole(quarter), struct(quarter, low))] * 4, bits=bits, after=after)


def part_rows(ref, bit, rows):
    return ref[pl.ds(pl.multiple_of(bit * rows, rows), rows), :].astype(wide)


def whole_call(body, arrays, shapes, bits, after=()):
    return call(
        body, (1,), [(whole(a.shape), a) for a in arrays], [(whole(s), struct(s, low)) for s in shapes], bits=bits, after=after
    )


def halve_sides(left, left_got, right, right_got, bits, after=()):
    rows, cols = left.shape[0] // 2, left.shape[1]

    def body(b, l, lg, r, rg, ls, lk, rs, rk):
        for mine, got, bit, send, keep in ((l, lg, BIT1, ls, lk), (r, rg, BIT0, rs, rk)):
            send[...] = (part_rows(mine, 1 - b[bit], rows) + part_rows(got, 1 - b[bit], rows)).astype(low)
            keep[...] = (part_rows(mine, b[bit], rows) + part_rows(got, b[bit], rows)).astype(low)

    return whole_call(body, [left, left_got, right, right_got], [(rows, cols)] * 4, bits, after)


def halve_both(left, left_got, right, right_got, bits, after=()):
    rows, cols = left.shape[0] // 2, left.shape[1]

    def body(b, l, lg, r, rg, send, keep):
        for mine, got, c in ((l, lg, slice(0, cols)), (r, rg, slice(cols, 2 * cols))):
            send[:, c] = (part_rows(mine, 1 - b[BIT2], rows) + part_rows(got, 1 - b[BIT2], rows)).astype(low)
            keep[:, c] = (part_rows(mine, b[BIT2], rows) + part_rows(got, b[BIT2], rows)).astype(low)

    return whole_call(body, [left, left_got, right, right_got], [(rows, 2 * cols)] * 2, bits, after)


def add_up(mine, got, bits, after=()):
    def body(b, m, g, out):
        out[...] = (m[...].astype(wide) + g[...].astype(wide)).astype(low)

    return whole_call(body, [mine, got], [mine.shape], bits, after)[0]


def place(out, mine, got, bit, cols=slice(None)):
    rows = mine.shape[0]
    out[pl.ds(pl.multiple_of(bit * rows, rows), rows), :] = mine[:, cols]
    out[pl.ds(pl.multiple_of((1 - bit) * rows, rows), rows), :] = got[:, cols]


def join_both(mine, got, bits, after=()):
    rows, cols = mine.shape[0], mine.shape[1] // 2

    def body(b, m, g, left, right):
        place(left, m, g, b[BIT2], slice(0, cols))
        place(right, m, g, b[BIT2], slice(cols, 2 * cols))

    return whole_call(body, [mine, got], [(2 * rows, cols)] * 2, bits, after)


def join_sides(left, left_got, right, right_got, bits, after=()):
    rows, cols = left.shape

    def body(b, l, lg, r, rg, lo, ro):
        place(lo, l, lg, b[BIT1])
        place(ro, r, rg, b[BIT0])

    return whole_call(body, [left, left_got, right, right_got], [(2 * rows, cols)] * 2, bits, after)


def join_half(left, left_got, right, right_got, bits, after=()):
    rows, cols = left.shape

    def body(b, l, lg, r, rg, out):
        place(out.at[:, pl.ds(0, cols)], l, lg, b[BIT0])
        place(out.at[:, pl.ds(cols, cols)], r, rg, b[BIT1])

    return whole_call(body, [left, left_got, right, right_got], [(2 * rows, 2 * cols)], bits, after)[0]


def widen(mine, got, widths, bits, after=()):
    half, n = mine.shape
    tile = half // 4

    def body(b, m, g, *outs):
        mine_now = (pl.program_id(0) // 4) == b[CORE]
        value = jnp.where(mine_now, m[...], g[...]).astype(wide)
        at = 0
        for out, w in zip(outs, widths):
            out[...] = value[:, at : at + w]
            at += w

    def index(core_of):
        return lambda i, b: (jnp.clip(i - 4 * core_of(b), 0, 3), 0)

    return call(
        body,
        (8,),
        [(pl.BlockSpec((tile, n), index(lambda b: b[CORE])), mine), (pl.BlockSpec((tile, n), index(lambda b: 1 - b[CORE])), got)],
        [(pl.BlockSpec((tile, w), lambda i, b: (i, 0)), struct((2 * half, w), wide)) for w in widths],
        bits=bits,
        after=after,
    )


class Reduction:
    def __init__(self, src, widths, bits, clock, tail):
        self.src, self.widths, self.bits, self.clock, self.tail = src, widths, bits, clock, tail

    def step(self, fn, *args):
        out = fn(*args, after=self.clock.now())
        self.clock.set(out[0] if isinstance(out, (list, tuple)) else out)
        return out

    def core_send(self):
        send = self.step(gradient_rows, self.src, self.bits, None)
        self.got = exchange(send, "stream", 1)

    def core_sum(self):
        ls, self.l, rs, self.r = self.step(gradient_rows, self.src, self.bits, self.got)
        self.gl, self.gr = exchange(ls, "dp", 1), exchange(rs, "dp", 2)

    def first_sum(self):
        ls, self.l, rs, self.r = self.step(halve_sides, self.l, self.gl, self.r, self.gr, self.bits)
        self.gl, self.gr = exchange(ls, "dp", 2), exchange(rs, "dp", 1)

    def second_sum(self):
        send, self.v = self.step(halve_both, self.l, self.gl, self.r, self.gr, self.bits)
        self.got = exchange(send, "dp", 4)

    def third_sum(self):
        self.v = self.step(add_up, self.v, self.got, self.bits)
        self.got = exchange(self.v, "dp", self.tail[0])

    def last_sum(self):
        for mask in self.tail[1:]:
            self.v = self.step(add_up, self.v, self.got, self.bits)
            self.got = exchange(self.v, "dp", mask)
        self.v = self.step(add_up, self.v, self.got, self.bits)
        self.got = exchange(self.v, "dp", 4)

    def third_back(self):
        self.l, self.r = self.step(join_both, self.v, self.got, self.bits)
        self.gl, self.gr = exchange(self.l, "dp", 2), exchange(self.r, "dp", 1)

    def second_back(self):
        self.l, self.r = self.step(join_sides, self.l, self.gl, self.r, self.gr, self.bits)
        self.gl, self.gr = exchange(self.l, "dp", 1), exchange(self.r, "dp", 2)

    def first_back(self):
        self.v = self.step(join_half, self.l, self.gl, self.r, self.gr, self.bits)
        self.got = exchange(self.v, "stream", 1)

    def finish(self):
        return self.step(widen, self.v, self.got, self.widths, self.bits)


class Clock:
    def __init__(self, start):
        self.last = start

    def now(self):
        return (self.last,)

    def set(self, value):
        self.last = value


def gather_ordered(a, axis, mask):
    got = exchange(a, axis, mask)
    bit = (lax.axis_index(axis) // mask) % 2
    n = a.shape[0]
    return lax.dynamic_slice_in_dim(jnp.concatenate([got, a, got]), (1 - bit) * n, 2 * n, 0)


def shards(
    embedded, seq_cotangent, pair_ids, w_qkv, b_qv, w_out, b_out, ln1_gain, ln1_bias, w_in, b_in, w_down, b_down,
    ln2_gain, ln2_bias, w_pool, b_pool,
):
    x = embedded[0]
    tokens, width = x.shape
    sents = tokens // SEQ
    ffn = w_in.shape[1]
    dp = lax.axis_size("dp")
    stream, place_dp = lax.axis_index("stream"), lax.axis_index("dp")
    bits = jnp.stack([stream, place_dp % 2, (place_dp // 2) % 2, (place_dp // 4) % 2]).astype(jnp.int32)
    rows_of = Rows(width, ffn)
    pack = jnp.concatenate(
        [b_qv[:width], jnp.zeros((width,), wide), b_qv[width:], b_out, ln1_gain, ln1_bias, b_in, b_down, ln2_gain, ln2_bias, b_pool]
    ).reshape(1, -1)
    proj, probs, context, hidden, hidden_low, inv_one = attention_forward(x, w_qkv, w_out, pack, rows_of)
    hid3 = hidden.reshape(sents, SEQ, width)
    cot3 = seq_cotangent[0].reshape(sents, SEQ, width)
    enc, act, slope, normed_two, inv_two, first_low = ffn_first(hid3, w_in, w_down, pack, rows_of)
    gathered = first_low
    gate = two = small_up = bin_sum = None
    masks = [1 << i for i in range(dp.bit_length() - 1)]
    for index in range(1, SEQ // GROUP):
        enc, act, gate, two, small_up, bin_sum = ffn_group(
            index, hid3, cot3, w_in, w_down, pack, rows_of, enc, act, gate, two, small_up, bin_sum
        )
    for mask in masks:
        gathered = gather_ordered(gathered, "dp", mask)
    gathered = gather_ordered(gathered, "stream", 1)
    total = sents * dp
    pre_low, grad_w_pool, grad_b_pool = contrastive(gathered.reshape(2, total, width), pair_ids, w_pool, b_pool)
    own_pre = lax.dynamic_slice_in_dim(pre_low, stream * total + place_dp * sents, sents)
    grad_first = trans_right(own_pre, w_pool)
    gate, two, small_up, bin_sum = ffn_first_back(
        cot3, grad_first, normed_two, inv_two, slope, w_down, pack, rows_of, gate, two, small_up, bin_sum
    )
    clock = Clock(small_up)
    act, gate, two = (v.reshape(tokens, -1) for v in (act, gate, two))
    tail = masks[3:]
    down = Reduction(Sources([(act, two)]), [width], bits, clock, tail)
    into = Reduction(Sources([(hidden_low, gate)]), [ffn], bits, clock, tail)
    down.core_send()
    into.core_send()
    down.core_sum()
    state = lower_backward(0, 2, two, gate, hidden, inv_one, proj, probs, w_in, w_out, pack, rows_of, after=clock.now())
    clock.set(state[0])
    into.core_sum()
    down.first_sum()
    state = lower_backward(
        1, 2, two, gate, hidden, inv_one, proj, probs, w_in, w_out, pack, rows_of, before=state, after=clock.now()
    )
    grad_one, grad_proj, small_low, bqv = state
    clock.set(grad_one)
    down.second_sum()
    low_part = Reduction(Sources([(x, grad_proj), (context, grad_one)]), [3 * width, width], bits, clock, tail)
    low_part.core_send()
    into.first_sum()
    down.third_sum()
    small = jnp.concatenate([small_up[:3], bin_sum.reshape(-1, width), small_low[:3], bqv[:2]], 0)
    low_part.core_sum()
    down.last_sum()
    into.second_sum()
    grad_input = input_gradient(grad_proj, w_qkv, grad_one, after=clock.now())
    clock.set(grad_input)
    for axis, mask in [("stream", 1)] + [("dp", m) for m in masks]:
        small = small + exchange(small, axis, mask)
    down.third_back()
    low_part.first_sum()
    into.third_sum()
    down.second_back()
    low_part.second_sum()
    into.last_sum()
    low_part.third_sum()
    into.third_back()
    down.first_back()
    into.second_back()
    low_part.last_sum()
    (out_down,) = down.finish()
    low_part.third_back()
    into.first_back()
    low_part.second_back()
    (out_in,) = into.finish()
    low_part.first_back()
    out_qkv, out_out = low_part.finish()
    n_in = ffn // width
    return (
        enc.reshape(1, tokens, width),
        grad_input[None],
        out_qkv,
        small[6 + n_in : 8 + n_in].reshape(-1),
        out_out,
        small[5 + n_in],
        small[3 + n_in],
        small[4 + n_in],
        out_in,
        small[3 : 3 + n_in].reshape(-1),
        out_down,
        small[2],
        small[0],
        small[1],
        grad_w_pool,
        grad_b_pool,
    )


def solution(mesh):
    sharded = P("stream", "dp", None)
    return jax.shard_map(
        shards,
        mesh=mesh,
        in_specs=(sharded, sharded) + (P(),) * 15,
        out_specs=(sharded, sharded) + (P(),) * 14,
        check_vma=False,
    )
```

time: 462 us -> 421 us (0.911)
  Pallas kernels: 137 us -> 243 us
  other arithmetic: 90 us -> 6.01 us
  waiting for transfers between devices: 109 us -> 81.2 us
  starting transfers between devices: 71.3 us -> 50.7 us
  local copies, waits for them, and re-layouts: 39 us -> 27.7 us
    pallas_call x10 -> x39, Pallas kernels: 137 us -> 243 us  [call(): pl.pallas_call(wrapped, grid_spec=pltpu.PrefetchScalarGridSpec(num_scalar...]
    concatenate x35 -> x5, other arithmetic: 46.6 us -> 2.87 us  [gather_ordered(): jnp.concatenate([got, a, got])]
    convert_element_type x34 -> x0, other arithmetic: 39 us -> none  [the longest x24 19.9 us: reduce_parts(): sum((take_half(t, 1 - bit, n).astype(wide) for t in terms)).astype(low)]
    ppermute x70 -> x49, waiting for transfers between devices: 109 us -> 81.2 us  [exchange(): return lax.ppermute(a, axis, [(i, i ^ mask) for i in range(size)])]
    ppermute x70 -> x49, starting transfers between devices: 71.3 us -> 50.7 us  [exchange(): return lax.ppermute(a, axis, [(i, i ^ mask) for i in range(size)])]
    unnamed x110 -> x102, local copies, waits for them, and re-layouts: 16.8 us -> 23.2 us
    slice x5 -> x0, local copies, waits for them, and re-layouts: 6.42 us -> none  [the longest x1 2.68 us: shards(): grad_w_in[:, :half]]
    dynamic_slice x5 -> x0, local copies, waits for them, and re-layouts: 5.65 us -> none  [take_half(): return lax.dynamic_slice_in_dim(a, which * n, n, 0)]
  transfers between devices with their start and end apart: 70 -> 49, of which waited for: 37 -> 24; matrix products, arithmetic and copies ran while one was open for 20% -> 2% of each run, Pallas kernels for 9% -> 40%
where the time goes in v2:
time: 421 us; the launch traced here: 416 us
  Pallas kernels  243 us (58%)
  waiting for transfers between devices  81.2 us (19%)
  starting transfers between devices  50.7 us (12%)
  local copies, waits for them, and re-layouts  27.7 us (7%)
  matrix products  6.17 us (1%)
  other arithmetic  6.01 us (1%)
    pallas_call x39, Pallas kernels, call(): pl.pallas_call(wrapped, grid_spec=pltpu.PrefetchScalarGridSpec(num_scalar...  243 us
    ppermute x49, waiting for transfers between devices, exchange(): return lax.ppermute(a, axis, [(i, i ^ mask) for i in range(size)])  81.2 us
    ppermute x49, starting transfers between devices, exchange(): return lax.ppermute(a, axis, [(i, i ^ mask) for i in range(size)])  50.7 us
    unnamed x102, local copies, waits for them, and re-layouts  23.2 us
  transfers between devices with their start and end apart: 49, of which 24 were waited for; matrix products, arithmetic and copies ran while one was open for 2% of the time, Pallas kernels for 40%

profile of v2, /device:TPU:0, one launch (start us, length us, event | category | flops | bytes accessed | tf_op | source)
XLA Modules:
  0.0 416.1 jit_solution(3242072929207532450)
XLA Ops:
  8.4 17.1 %shard_map.288 = (bf16[1024,2304]{1,0:T(8,128)(2,1)}, bf16[1024,768]{1,0:T(8,128)(2,1)}, bf16[1024,768]{1,0:T(8,128)(2,1)}, f32[1024,768]{1,0:T(8,128)}, bf16[1024,768]{1,0:T(8,128)(2,1)}, /*index=5*/f32[1024,1]{1,0:T(8,128)}) custom-call(bf16[1024,768]{1,0:T(8,128)(2,1)} %bitcast.36, bf16[768,2304]{1,0:T(8,128)(2,1)} %refs_1_.5, bf16[768,768]{1,0:T(8,128)(2,1)} %refs_7_.3, ...), custom_call_target="tpu_custom_call" | custom-call | tf_op jit(solution)/shard_map/pallas_call | solution.py:40
  25.5 9.6 %shard_map.289 = (bf16[16,64,768]{2,1,0:T(8,128)(2,1)}, bf16[16,64,3072]{2,1,0:T(8,128)(2,1)}, bf16[256,3072]{1,0:T(8,128)(2,1)}, f32[256,768]{1,0:T(8,128)}, f32[256,1]{1,0:T(8,128)}, /*index=5*/bf16[16,768]{1,0:T(8,128)(2,1)}) custom-call(f32[16,64,768]{2,1,0:T(8,128)} %bitcast.23, bf16[768,3072]{1,0:T(8,128)(2,1)} %refs_6_.3, bf16[3072,768]{1,0:T(8,128)(2,1)} %refs_5_.1, ...), custom_call_target="tpu_custom_call" | custom-call | tf_op jit(solution)/shard_map/pallas_call | solution.py:40
  50.2 4.0 collective-permute-start.3
  54.1 5.8 %collective-permute-done.3 = bf16[128,768]{1,0:T(8,128)(2,1)S(1)} collective-permute-done((bf16[128,768]{1,0:T(8,128)(2,1)S(1)}, bf16[128,768]{1,0:T(8,128)(2,1)S(1)}, u32[]{:S(2)}, u32[]{:S(2)}) %collective-permute-start.3) | collective-permute-done | bytes 196640 | tf_op jit(solution)/shard_map/ppermute | solution.py:524
  60.5 11.2 %shard_map.290 = (bf16[16,64,768]{2,1,0:T(8,128)(2,1)}, bf16[16,64,3072]{2,1,0:T(8,128)(2,1)}, bf16[16,64,3072]{2,1,0:T(8,128)(2,1)}, bf16[16,64,768]{2,1,0:T(8,...) custom-call(f32[16,64,768]{2,1,0:T(8,128)} %bitcast.24, ...), custom_call_target="tpu_custom_call", output_to_operand_aliasing={{0}: (5, {}), {1}: (6, {})} | custom-call | tf_op jit(solution)/shard_map/pallas_call | solution.py:40
  71.7 11.3 %shard_map.291 = (bf16[16,64,768]{2,1,0:T(8,128)(2,1)}, bf16[16,64,3072]{2,1,0:T(8,128)(2,1)}, bf16[16,64,3072]{2,1,0:T(8,128)(2,1)}, bf16[16,64,768]{2,1,0:T(8,...) custom-call(f32[16,64,768]{2,1,0:T(8,128)} %bitcast.25, ...), custom_call_target="tpu_custom_call", output_to_operand_aliasing={{0}: (5, {}), {1}: (6, {}), {2}: (7, {}), {3}: (8, {})} | custom-call | tf_op jit(solution)/shard_map/pallas_call | solution.py:40
  83.1 11.1 %shard_map.292 = (bf16[16,64,768]{2,1,0:T(8,128)(2,1)}, bf16[16,64,3072]{2,1,0:T(8,128)(2,1)}, bf16[16,64,3072]{2,1,0:T(8,128)(2,1)}, bf16[16,64,768]{2,1,0:T(8,...) custom-call(f32[16,64,768]{2,1,0:T(8,128)} %bitcast.26, ...), custom_call_target="tpu_custom_call", output_to_operand_aliasing={{0}: (5, {}), {1}: (6, {}), {2}: (7, {}), {3}: (8, {})} | custom-call | tf_op jit(solution)/shard_map/pallas_call | solution.py:40
  102.4 6.9 %shard_map.293 = (bf16[16,64,3072]{2,1,0:T(8,128)(2,1)}, bf16[16,64,768]{2,1,0:T(8,128)(2,1)}, f32[8,768]{1,0:T(8,128)}, f32[1,3072]{1,0:T(1,128)}) custom-call(bf16[16,64,768]{2,1,0:T(8,128)(2,1)} %bitcast.34, f32[16,768]{1,0:T(8,128)} %fusion.26.refs_1_, f32[256,768]{1,0:T(8,128)} %get-tuple-element.119.refs_2_, ...), custom_call_target="tpu_custom_call", output_to_operand_aliasing={{0}: (9, {}), {1}: (10, {})} | custom-call | tf_op jit(solution)/shard_map/pallas_call | solution.py:40
  109.4 7.1 %shard_map.294.refs_3_ = bf16[1536,768]{1,0:T(8,128)(2,1)} custom-call(s32[4]{0:T(128)} %pad_add_fusion.refs_0_, bf16[1024,3072]{1,0:T(8,128)(2,1)} %bitcast.21, bf16[1024,768]{1,0:T(8,128)(2,1)} %bitcast.27, f32[8,768]{1,0:T(8,128)} %get-tuple-element.132.refs_3_), custom_call_target="tpu_custom_call" | custom-call | tf_op jit(solution)/shard_map/pallas_call | solution.py:40
  116.9 7.4 %shard_map.295.refs_4_ = bf16[384,3072]{1,0:T(8,128)(2,1)} custom-call(s32[4]{0:T(128)} %pad_add_fusion.refs_0_, bf16[1024,768]{1,0:T(8,128)(2,1)} %get-tuple-element.133.refs_1_, bf16[1024,3072]{1,0:T(8,128)(2,1)} %bitcast.17, bf16[1536,768]{1,0:T(8,128)(2,1)} %shard_map.294.refs_3_), custom_call_target="tpu_custom_call" | custom-call | tf_op jit(solution)/shard_map/pallas_call | solution.py:40
  124.3 8.1 %shard_map.296 = (bf16[768,384]{1,0:T(8,128)(2,1)}, bf16[768,384]{1,0:T(8,128)(2,1)}, bf16[768,384]{1,0:T(8,128)(2,1)}, bf16[768,384]{1,0:T(8,128)(2,1)}) custom-call(s32[4]{0:T(128)} %pad_add_fusion.refs_0_, bf16[1024,3072]{1,0:T(8,128)(2,1)} %bitcast.22, bf16[1024,768]{1,0:T(8,128)(2,1)} %bitcast.28, bf16[1536,768]{1,0:T(8,128)(2,1)} %collective-permute-done.5.refs_3_, ...), custom_call_target="tpu_custom_call" | custom-call | tf_op jit(solution)/shard_map/pallas_call | solution.py:40
  135.5 14.9 %shard_map.297 = (bf16[1024,768]{1,0:T(8,128)(2,1)}, bf16[1024,2304]{1,0:T(8,128)(2,1)}, f32[8,768]{1,0:T(8,128)}, f32[8,768]{1,0:T(8,128)}) custom-call(bf16[1024,768]{1,0:T(8,128)(2,1)} %bitcast.29, bf16[1024,3072]{1,0:T(8,128)(2,1)} %bitcast.18, f32[1024,768]{1,0:T(8,128)} %get-tuple-element.102.refs_2_, f32[1024,1]{1,0:T(8,128)} %get-tuple-element.128.refs_3_, ...), custom_call_target="tpu_custom_call" | custom-call | tf_op jit(solution)/shard_map/pallas_call | solution.py:40
  150.4 8.5 %shard_map.298 = (bf16[192,1536]{1,0:T(8,128)(2,1)}, bf16[192,1536]{1,0:T(8,128)(2,1)}, bf16[192,1536]{1,0:T(8,128)(2,1)}, bf16[192,1536]{1,0:T(8,128)(2,1)}) custom-call(s32[4]{0:T(128)} %pad_add_fusion.refs_0_, bf16[1024,768]{1,0:T(8,128)(2,1)} %get-tuple-element.133.refs_1_, bf16[1024,3072]{1,0:T(8,128)(2,1)} %bitcast.19, ...), custom_call_target="tpu_custom_call" | custom-call | tf_op jit(solution)/shard_map/pallas_call | solution.py:40
  159.9 3.4 shard_map.299
  164.3 15.4 %shard_map.300 = (bf16[1024,768]{1,0:T(8,128)(2,1)}, bf16[1024,2304]{1,0:T(8,128)(2,1)}, f32[8,768]{1,0:T(8,128)}, f32[8,768]{1,0:T(8,128)}) custom-call(bf16[1024,768]{1,0:T(8,128)(2,1)} %bitcast.30, bf16[1024,3072]{1,0:T(8,128)(2,1)} %bitcast.20, f32[1024,768]{1,0:T(8,128)} %get-tuple-element.102.refs_2_, ...), custom_call_target="tpu_custom_call", output_to_operand_aliasing={{0}: (9, {}), {1}: (10, {})} | custom-call | tf_op jit(solution)/shard_map/pallas_call | solution.py:40
  183.4 8.1 %shard_map.302.refs_5_ = bf16[384,3072]{1,0:T(8,128)(2,1)} custom-call(s32[4]{0:T(128)} %pad_add_fusion.refs_0_, bf16[1024,768]{1,0:T(8,128)(2,1)} %bitcast.37, bf16[1024,2304]{1,0:T(8,128)(2,1)} %get-tuple-element.144.refs_2_.refs_0_, bf16[1024,768]{1,0:T(8,128)(2,1)} %get-tuple-element.149.refs_3_, ...), custom_call_target="tpu_custom_call" | custom-call | tf_op jit(solution)/shard_map/pallas_call | solution.py:40
  194.9 12.4 %collective-permute-done.9.refs_2_ = bf16[192,1536]{1,0:T(8,128)(2,1)S(1)} collective-permute-done((bf16[192,1536]{1,0:T(8,128)(2,1)S(1)}, bf16[192,1536]{1,0:T(8,128)(2,1)S(1)}, u32[]{:S(2)}, u32[]{:S(2)}) %collective-permute-start.9) | collective-permute-done | bytes 589856 | tf_op jit(solution)/shard_map/ppermute | solution.py:524
  209.5 3.5 shard_map.303
  217.9 8.9 %shard_map.305 = (bf16[192,1536]{1,0:T(8,128)(2,1)}, bf16[192,1536]{1,0:T(8,128)(2,1)}, bf16[192,1536]{1,0:T(8,128)(2,1)}, bf16[192,1536]{1,0:T(8,128)(2,1)}) custom-call(s32[4]{0:T(128)} %pad_add_fusion.refs_0_, bf16[1024,768]{1,0:T(8,128)(2,1)} %bitcast.38, bf16[1024,2304]{1,0:T(8,128)(2,1)} %get-tuple-element.144.refs_2_.refs_0_, ...), custom_call_target="tpu_custom_call" | custom-call | tf_op jit(solution)/shard_map/pallas_call | solution.py:40
  235.4 12.1 %collective-permute-done.14.refs_4_ = bf16[96,1536]{1,0:T(8,128)(2,1)S(1)} collective-permute-done((bf16[96,1536]{1,0:T(8,128)(2,1)}, bf16[96,1536]{1,0:T(8,128)(2,1)S(1)}, u32[]{:S(2)}, u32[]{:S(2)}) %collective-permute-start.14) | collective-permute-done | bytes 294944 | tf_op jit(solution)/shard_map/ppermute | solution.py:524
  251.0 8.8 %shard_map.308.refs_3_ = bf16[1024,768]{1,0:T(8,128)(2,1)} custom-call(bf16[1024,2304]{1,0:T(8,128)(2,1)} %get-tuple-element.144.refs_2_.refs_0_, bf16[768,2304]{1,0:T(8,128)(2,1)} %refs_1_.5, bf16[1024,768]{1,0:T(8,128)(2,1)} %get-tuple-element.145.refs_5_.refs_4_.refs_2_, bf16[48,3072]{1,0:T(8,128)(2,1)} %get-tuple-element.160.refs_3_), custom_call_target="tpu_custom_call" | custom-call | tf_op jit(solution)/shard_map/pallas_call | solution.py:40
  267.9 3.6 shard_map.310
  293.5 3.1 collective-permute-done.26.refs_2_
  307.1 4.0 shard_map.317.refs_5_.refs_1_
  313.6 7.0 %collective-permute-done.30.refs_2_ = bf16[96,1536]{1,0:T(8,128)(2,1)S(1)} collective-permute-done((bf16[96,1536]{1,0:T(8,128)(2,1)S(1)}, bf16[96,1536]{1,0:T(8,128)(2,1)S(1)}, u32[]{:S(2)}, u32[]{:S(2)}) %collective-permute-start.30) | collective-permute-done | bytes 294944 | tf_op jit(solution)/shard_map/ppermute | solution.py:524
  330.7 8.7 %shard_map.320.refs_3_ = f32[3072,768]{1,0:T(8,128)} custom-call(s32[4]{0:T(128)} %pad_add_fusion.refs_0_, bf16[1536,768]{1,0:T(8,128)(2,1)} %shard_map.317.refs_5_.refs_1_, bf16[1536,768]{1,0:T(8,128)(2,1)} %collective-permute-done.35.refs_2_, bf16[48,3072]{1,0:T(8,128)(2,1)} %shard_map.319.refs_3_.refs_1_), custom_call_target="tpu_custom_call" | custom-call | tf_op jit(solution)/shard_map/pallas_call | solution.py:40
  344.2 4.0 shard_map.322.refs_5_.refs_1_
  351.0 6.5 %collective-permute-done.36.refs_2_ = bf16[96,1536]{1,0:T(8,128)(2,1)S(1)} collective-permute-done((bf16[96,1536]{1,0:T(8,128)(2,1)S(1)}, bf16[96,1536]{1,0:T(8,128)(2,1)S(1)}, u32[]{:S(2)}, u32[]{:S(2)}) %collective-permute-start.36) | collective-permute-done | bytes 294944 | tf_op jit(solution)/shard_map/ppermute | solution.py:524
  364.8 8.7 %shard_map.324.refs_5_ = f32[768,3072]{1,0:T(8,128)} custom-call(s32[4]{0:T(128)} %pad_add_fusion.refs_0_, bf16[384,3072]{1,0:T(8,128)(2,1)} %shard_map.322.refs_5_.refs_1_, bf16[384,3072]{1,0:T(8,128)(2,1)} %collective-permute-done.42.refs_2_, bf16[192,1536]{1,0:T(8,128)(2,1)} %get-tuple-element.181.refs_3_.refs_1_), custom_call_target="tpu_custom_call" | custom-call | tf_op jit(solution)/shard_map/pallas_call | solution.py:40
  373.5 3.8 collective-permute-done.40.refs_2_
  379.2 3.8 shard_map.325.refs_1_.refs_3_
  407.1 8.8 %shard_map.326 = (f32[768,2304]{1,0:T(8,128)}, f32[768,768]{1,0:T(8,128)}) custom-call(s32[4]{0:T(128)} %pad_add_fusion.refs_0_, bf16[384,3072]{1,0:T(8,128)(2,1)} %shard_map.325.refs_1_.refs_3_, bf16[384,3072]{1,0:T(8,128)(2,1)} %collective-permute-done.43.refs_2_, bf16[384,3072]{1,0:T(8,128)(2,1)} %shard_map.325.refs_1_.refs_3_), custom_call_target="tpu_custom_call" | custom-call | tf_op jit(solution)/shard_map/pallas_call | solution.py:40
  (246 shorter events, 157.3 us)
Async XLA Ops:
  60.4 34.4 %collective-permute-start.4 = (bf16[256,768]{1,0:T(8,128)(2,1)S(1)}, bf16[256,768]{1,0:T(8,128)(2,1)S(1)}, u32[]{:S(2)}, u32[]{:S(2)}) collective-permute-start(bf16[256,768]{1,0:T(8,128)(2,1)S(1)} %fusion.5), channel_id=1, source_target_pairs={{0,16},{16,0},{1,17},{17,1},{2,18},{18,2},{3,19},{19,3},{4,20},{20... | collective-permute-start | bytes 1179656 | tf_op jit(solution)/shard_map/ppermute | solution.py:524
  124.3 26.1 %collective-permute-start.8 = (bf16[384,3072]{1,0:T(8,128)(2,1)}, bf16[384,3072]{1,0:T(8,128)(2,1)}, u32[]{:S(2)}, u32[]{:S(2)}) collective-permute-start(bf16[384,3072]{1,0:T(8,128)(2,1)} %shard_map.295.refs_4_), channel_id=1, source_target_pairs={{0,16},{16,0},{1,17},{17,1},{2,18},{18,2},{3,19},{19,3},{4,20},{20... | collective-permute-start | bytes 7077896 | tf_op jit(solution)/shard_map/ppermute | solution.py:524
  132.4 26.5 %collective-permute-start.6 = (bf16[768,384]{1,0:T(8,128)(2,1)}, bf16[768,384]{1,0:T(8,128)(2,1)S(1)}, u32[]{:S(2)}, u32[]{:S(2)}) collective-permute-start(bf16[768,384]{1,0:T(8,128)(2,1)} %get-tuple-element.134.refs_9_), channel_id=1, source_target_pairs={{0,1},{1,0},{2,3},{3,2},{4,5},{5,4},{6,7},{7,6},{8,9},{9,8},{10,11... | collective-permute-start | bytes 1769480 | tf_op jit(solution)/shard_map/ppermute | solution.py:524
  134.0 25.0 %collective-permute-start.7 = (bf16[768,384]{1,0:T(8,128)(2,1)}, bf16[768,384]{1,0:T(8,128)(2,1)S(1)}, u32[]{:S(2)}, u32[]{:S(2)}) collective-permute-start(bf16[768,384]{1,0:T(8,128)(2,1)} %get-tuple-element.141), channel_id=1, source_target_pairs={{0,2},{1,3},{2,0},{3,1},{4,6},{5,7},{6,4},{7,5},{8,10},{9,11},{10,... | collective-permute-start | bytes 1769480 | tf_op jit(solution)/shard_map/ppermute | solution.py:524
  163.3 16.4 %collective-permute-start.11 = (bf16[384,384]{1,0:T(8,128)(2,1)}, bf16[384,384]{1,0:T(8,128)(2,1)S(1)}, u32[]{:S(2)}, u32[]{:S(2)}) collective-permute-start(bf16[384,384]{1,0:T(8,128)(2,1)} %get-tuple-element.143.refs_13_), channel_id=1, source_target_pairs={{0,2},{1,3},{2,0},{3,1},{4,6},{5,7},{6,4},{7,5},{8,10},{9,11},{10,... | collective-permute-start | bytes 884744 | tf_op jit(solution)/shard_map/ppermute | solution.py:524
  163.8 15.9 %collective-permute-start.12 = (bf16[384,384]{1,0:T(8,128)(2,1)}, bf16[384,384]{1,0:T(8,128)(2,1)S(1)}, u32[]{:S(2)}, u32[]{:S(2)}) collective-permute-start(bf16[384,384]{1,0:T(8,128)(2,1)} %get-tuple-element.152), channel_id=1, source_target_pairs={{0,1},{1,0},{2,3},{3,2},{4,5},{5,4},{6,7},{7,6},{8,9},{9,8},{10,11... | collective-permute-start | bytes 884744 | tf_op jit(solution)/shard_map/ppermute | solution.py:524
  191.5 26.5 %collective-permute-start.17 = (bf16[384,3072]{1,0:T(8,128)(2,1)}, bf16[384,3072]{1,0:T(8,128)(2,1)}, u32[]{:S(2)}, u32[]{:S(2)}) collective-permute-start(bf16[384,3072]{1,0:T(8,128)(2,1)} %shard_map.302.refs_5_), channel_id=1, source_target_pairs={{0,16},{16,0},{1,17},{17,1},{2,18},{18,2},{3,19},{19,3},{4,20},{20... | collective-permute-start | bytes 7077896 | tf_op jit(solution)/shard_map/ppermute | solution.py:524
  191.5 15.7 %collective-permute-start.9 = (bf16[192,1536]{1,0:T(8,128)(2,1)S(1)}, bf16[192,1536]{1,0:T(8,128)(2,1)S(1)}, u32[]{:S(2)}, u32[]{:S(2)}) collective-permute-start(bf16[192,1536]{1,0:T(8,128)(2,1)S(1)} %copy-done.9), channel_id=1, source_target_pairs={{0,1},{1,0},{2,3},{3,2},{4,5},{5,4},{6,7},{7,6},{8,9},{9,8},{10,11... | collective-permute-start | bytes 1769480 | tf_op jit(solution)/shard_map/ppermute | solution.py:524
  193.1 15.6 %collective-permute-start.10 = (bf16[192,1536]{1,0:T(8,128)(2,1)}, bf16[192,1536]{1,0:T(8,128)(2,1)S(1)}, u32[]{:S(2)}, u32[]{:S(2)}) collective-permute-start(bf16[192,1536]{1,0:T(8,128)(2,1)} %get-tuple-element.148), channel_id=1, source_target_pairs={{0,2},{1,3},{2,0},{3,1},{4,6},{5,7},{6,4},{7,5},{8,10},{9,11},{10,... | collective-permute-start | bytes 1769480 | tf_op jit(solution)/shard_map/ppermute | solution.py:524
  194.6 18.4 %collective-permute-start.15 = (bf16[192,768]{1,0:T(8,128)(2,1)S(1)}, bf16[192,768]{1,0:T(8,128)(2,1)}, u32[]{:S(2)}, u32[]{:S(2)}) collective-permute-start(bf16[192,768]{1,0:T(8,128)(2,1)S(1)} %copy-done.19), channel_id=1, source_target_pairs={{0,4},{1,5},{2,6},{3,7},{4,0},{5,1},{6,2},{7,3},{8,12},{9,13},{10,... | collective-permute-start | bytes 884744 | tf_op jit(solution)/shard_map/ppermute | solution.py:524
  215.5 15.7 %collective-permute-start.16 = (bf16[192,768]{1,0:T(8,128)(2,1)}, bf16[192,768]{1,0:T(8,128)(2,1)S(1)}, u32[]{:S(2)}, u32[]{:S(2)}) collective-permute-start(bf16[192,768]{1,0:T(8,128)(2,1)} %shard_map.304.refs_6_.refs_1_), channel_id=1, source_target_pairs={{0,8},{1,9},{2,10},{3,11},{4,12},{5,13},{6,14},{7,15},{8,0},{9,1},... | collective-permute-start | bytes 884744 | tf_op jit(solution)/shard_map/ppermute | solution.py:524
  216.4 18.9 %collective-permute-start.13 = (bf16[96,1536]{1,0:T(8,128)(2,1)}, bf16[96,1536]{1,0:T(8,128)(2,1)S(1)}, u32[]{:S(2)}, u32[]{:S(2)}) collective-permute-start(bf16[96,1536]{1,0:T(8,128)(2,1)} %get-tuple-element.155.refs_3_), channel_id=1, source_target_pairs={{0,2},{1,3},{2,0},{3,1},{4,6},{5,7},{6,4},{7,5},{8,10},{9,11},{10,... | collective-permute-start | bytes 884744 | tf_op jit(solution)/shard_map/ppermute | solution.py:524
  226.9 40.0 %collective-permute-start.18 = (bf16[192,1536]{1,0:T(8,128)(2,1)}, bf16[192,1536]{1,0:T(8,128)(2,1)S(1)}, u32[]{:S(2)}, u32[]{:S(2)}) collective-permute-start(bf16[192,1536]{1,0:T(8,128)(2,1)} %get-tuple-element.159.refs_3_), channel_id=1, source_target_pairs={{0,1},{1,0},{2,3},{3,2},{4,5},{5,4},{6,7},{7,6},{8,9},{9,8},{10,11... | collective-permute-start | bytes 1769480 | tf_op jit(solution)/shard_map/ppermute | solution.py:524
  227.4 39.5 %collective-permute-start.19 = (bf16[192,1536]{1,0:T(8,128)(2,1)}, bf16[192,1536]{1,0:T(8,128)(2,1)S(1)}, u32[]{:S(2)}, u32[]{:S(2)}) collective-permute-start(bf16[192,1536]{1,0:T(8,128)(2,1)} %get-tuple-element.163), channel_id=1, source_target_pairs={{0,2},{1,3},{2,0},{3,1},{4,6},{5,7},{6,4},{7,5},{8,10},{9,11},{10,... | collective-permute-start | bytes 1769480 | tf_op jit(solution)/shard_map/ppermute | solution.py:524
  227.9 19.5 %collective-permute-start.14 = (bf16[96,1536]{1,0:T(8,128)(2,1)}, bf16[96,1536]{1,0:T(8,128)(2,1)S(1)}, u32[]{:S(2)}, u32[]{:S(2)}) collective-permute-start(bf16[96,1536]{1,0:T(8,128)(2,1)} %get-tuple-element.157), channel_id=1, source_target_pairs={{0,1},{1,0},{2,3},{3,2},{4,5},{5,4},{6,7},{7,6},{8,9},{9,8},{10,11... | collective-permute-start | bytes 884744 | tf_op jit(solution)/shard_map/ppermute | solution.py:524
  234.4 28.1 %collective-permute-start.20 = (bf16[192,768]{1,0:T(8,128)(2,1)}, bf16[192,768]{1,0:T(8,128)(2,1)S(1)}, u32[]{:S(2)}, u32[]{:S(2)}) collective-permute-start(bf16[192,768]{1,0:T(8,128)(2,1)} %shard_map.306.refs_5_.refs_1_), channel_id=1, source_target_pairs={{0,4},{1,5},{2,6},{3,7},{4,0},{5,1},{6,2},{7,3},{8,12},{9,13},{10,... | collective-permute-start | bytes 884744 | tf_op jit(solution)/shard_map/ppermute | solution.py:524
  259.7 14.7 %collective-permute-start.25 = (bf16[48,3072]{1,0:T(8,128)(2,1)S(1)}, bf16[48,3072]{1,0:T(8,128)(2,1)S(1)}, u32[]{:S(2)}, u32[]{:S(2)}) collective-permute-start(bf16[48,3072]{1,0:T(8,128)(2,1)S(1)} %copy-done.18), channel_id=1, source_target_pairs={{0,4},{1,5},{2,6},{3,7},{4,0},{5,1},{6,2},{7,3},{8,12},{9,13},{10,... | collective-permute-start | bytes 884744 | tf_op jit(solution)/shard_map/ppermute | solution.py:524
  265.8 12.1 %collective-permute-start.23 = (bf16[384,384]{1,0:T(8,128)(2,1)}, bf16[384,384]{1,0:T(8,128)(2,1)S(1)}, u32[]{:S(2)}, u32[]{:S(2)}) collective-permute-start(bf16[384,384]{1,0:T(8,128)(2,1)} %get-tuple-element.164.refs_5_.refs_1_), channel_id=1, source_target_pairs={{0,2},{1,3},{2,0},{3,1},{4,6},{5,7},{6,4},{7,5},{8,10},{9,11},{10,... | collective-permute-start | bytes 884744 | tf_op jit(solution)/shard_map/ppermute | solution.py:524
  266.3 11.6 %collective-permute-start.24 = (bf16[384,384]{1,0:T(8,128)(2,1)}, bf16[384,384]{1,0:T(8,128)(2,1)}, u32[]{:S(2)}, u32[]{:S(2)}) collective-permute-start(bf16[384,384]{1,0:T(8,128)(2,1)} %get-tuple-element.169.refs_3_), channel_id=1, source_target_pairs={{0,1},{1,0},{2,3},{3,2},{4,5},{5,4},{6,7},{7,6},{8,9},{9,8},{10,11... | collective-permute-start | bytes 884744 | tf_op jit(solution)/shard_map/ppermute | solution.py:524
  271.5 11.3 %collective-permute-start.21 = (bf16[96,1536]{1,0:T(8,128)(2,1)}, bf16[96,1536]{1,0:T(8,128)(2,1)S(1)}, u32[]{:S(2)}, u32[]{:S(2)}) collective-permute-start(bf16[96,1536]{1,0:T(8,128)(2,1)} %get-tuple-element.166.refs_3_), channel_id=1, source_target_pairs={{0,2},{1,3},{2,0},{3,1},{4,6},{5,7},{6,4},{7,5},{8,10},{9,11},{10,... | collective-permute-start | bytes 884744 | tf_op jit(solution)/shard_map/ppermute | solution.py:524
  277.7 12.6 %collective-permute-start.27 = (bf16[48,3072]{1,0:T(8,128)(2,1)}, bf16[48,3072]{1,0:T(8,128)(2,1)S(1)}, u32[]{:S(2)}, u32[]{:S(2)}) collective-permute-start(bf16[48,3072]{1,0:T(8,128)(2,1)} %shard_map.311.refs_5_.refs_1_), channel_id=1, source_target_pairs={{0,8},{1,9},{2,10},{3,11},{4,12},{5,13},{6,14},{7,15},{8,0},{9,1},... | collective-permute-start | bytes 884744 | tf_op jit(solution)/shard_map/ppermute | solution.py:524
  281.6 24.5 %collective-permute-start.32 = (bf16[768,384]{1,0:T(8,128)(2,1)}, bf16[768,384]{1,0:T(8,128)(2,1)S(1)}, u32[]{:S(2)}, u32[]{:S(2)}) collective-permute-start(bf16[768,384]{1,0:T(8,128)(2,1)} %get-tuple-element.171.refs_5_.refs_1_), channel_id=1, source_target_pairs={{0,1},{1,0},{2,3},{3,2},{4,5},{5,4},{6,7},{7,6},{8,9},{9,8},{10,11... | collective-permute-start | bytes 1769480 | tf_op jit(solution)/shard_map/ppermute | solution.py:524
  282.2 23.9 %collective-permute-start.33 = (bf16[768,384]{1,0:T(8,128)(2,1)}, bf16[768,384]{1,0:T(8,128)(2,1)S(1)}, u32[]{:S(2)}, u32[]{:S(2)}) collective-permute-start(bf16[768,384]{1,0:T(8,128)(2,1)} %get-tuple-element.176.refs_3_), channel_id=1, source_target_pairs={{0,2},{1,3},{2,0},{3,1},{4,6},{5,7},{6,4},{7,5},{8,10},{9,11},{10,... | collective-permute-start | bytes 1769480 | tf_op jit(solution)/shard_map/ppermute | solution.py:524
  286.4 10.2 %collective-permute-start.26 = (bf16[48,3072]{1,0:T(8,128)(2,1)}, bf16[48,3072]{1,0:T(8,128)(2,1)S(1)}, u32[]{:S(2)}, u32[]{:S(2)}) collective-permute-start(bf16[48,3072]{1,0:T(8,128)(2,1)} %get-tuple-element.173.refs_3_), channel_id=1, source_target_pairs={{0,4},{1,5},{2,6},{3,7},{4,0},{5,1},{6,2},{7,3},{8,12},{9,13},{10,... | collective-permute-start | bytes 884744 | tf_op jit(solution)/shard_map/ppermute | solution.py:524
  311.2 19.5 %collective-permute-start.35 = (bf16[1536,768]{1,0:T(8,128)(2,1)}, bf16[1536,768]{1,0:T(8,128)(2,1)}, u32[]{:S(2)}, u32[]{:S(2)}) collective-permute-start(bf16[1536,768]{1,0:T(8,128)(2,1)} %shard_map.317.refs_5_.refs_1_), channel_id=1, source_target_pairs={{0,16},{16,0},{1,17},{17,1},{2,18},{18,2},{3,19},{19,3},{4,20},{20... | collective-permute-start | bytes 7077896 | tf_op jit(solution)/shard_map/ppermute | solution.py:524
  312.3 15.2 %collective-permute-start.28 = (bf16[48,3072]{1,0:T(8,128)(2,1)S(1)}, bf16[48,3072]{1,0:T(8,128)(2,1)S(1)}, u32[]{:S(2)}, u32[]{:S(2)}) collective-permute-start(bf16[48,3072]{1,0:T(8,128)(2,1)S(1)} %copy-done.2), channel_id=1, source_target_pairs={{0,8},{1,9},{2,10},{3,11},{4,12},{5,13},{6,14},{7,15},{8,0},{9,1},... | collective-permute-start | bytes 884744 | tf_op jit(solution)/shard_map/ppermute | solution.py:524
  325.0 18.2 %collective-permute-start.38 = (bf16[192,1536]{1,0:T(8,128)(2,1)}, bf16[192,1536]{1,0:T(8,128)(2,1)S(1)}, u32[]{:S(2)}, u32[]{:S(2)}) collective-permute-start(bf16[192,1536]{1,0:T(8,128)(2,1)} %get-tuple-element.177.refs_3_.refs_1_), channel_id=1, source_target_pairs={{0,1},{1,0},{2,3},{3,2},{4,5},{5,4},{6,7},{7,6},{8,9},{9,8},{10,11... | collective-permute-start | bytes 1769480 | tf_op jit(solution)/shard_map/ppermute | solution.py:524
  325.6 17.5 %collective-permute-start.39 = (bf16[192,1536]{1,0:T(8,128)(2,1)}, bf16[192,1536]{1,0:T(8,128)(2,1)S(1)}, u32[]{:S(2)}, u32[]{:S(2)}) collective-permute-start(bf16[192,1536]{1,0:T(8,128)(2,1)} %get-tuple-element.180.refs_3_), channel_id=1, source_target_pairs={{0,2},{1,3},{2,0},{3,1},{4,6},{5,7},{6,4},{7,5},{8,10},{9,11},{10,... | collective-permute-start | bytes 1769480 | tf_op jit(solution)/shard_map/ppermute | solution.py:524
  348.1 16.7 %collective-permute-start.42 = (bf16[384,3072]{1,0:T(8,128)(2,1)}, bf16[384,3072]{1,0:T(8,128)(2,1)}, u32[]{:S(2)}, u32[]{:S(2)}) collective-permute-start(bf16[384,3072]{1,0:T(8,128)(2,1)} %shard_map.322.refs_5_.refs_1_), channel_id=1, source_target_pairs={{0,16},{16,0},{1,17},{17,1},{2,18},{18,2},{3,19},{19,3},{4,20},{20... | collective-permute-start | bytes 7077896 | tf_op jit(solution)/shard_map/ppermute | solution.py:524
  362.5 14.9 %collective-permute-start.40 = (bf16[192,1536]{1,0:T(8,128)(2,1)}, bf16[192,1536]{1,0:T(8,128)(2,1)S(1)}, u32[]{:S(2)}, u32[]{:S(2)}) collective-permute-start(bf16[192,1536]{1,0:T(8,128)(2,1)} %get-tuple-element.181.refs_3_.refs_1_), channel_id=1, source_target_pairs={{0,1},{1,0},{2,3},{3,2},{4,5},{5,4},{6,7},{7,6},{8,9},{9,8},{10,11... | collective-permute-start | bytes 1769480 | tf_op jit(solution)/shard_map/ppermute | solution.py:524
  363.8 14.6 %collective-permute-start.41 = (bf16[192,1536]{1,0:T(8,128)(2,1)}, bf16[192,1536]{1,0:T(8,128)(2,1)S(1)}, u32[]{:S(2)}, u32[]{:S(2)}) collective-permute-start(bf16[192,1536]{1,0:T(8,128)(2,1)} %get-tuple-element.182.refs_3_), channel_id=1, source_target_pairs={{0,2},{1,3},{2,0},{3,1},{4,6},{5,7},{6,4},{7,5},{8,10},{9,11},{10,... | collective-permute-start | bytes 1769480 | tf_op jit(solution)/shard_map/ppermute | solution.py:524
  383.1 24.1 %collective-permute-start.43 = (bf16[384,3072]{1,0:T(8,128)(2,1)}, bf16[384,3072]{1,0:T(8,128)(2,1)}, u32[]{:S(2)}, u32[]{:S(2)}) collective-permute-start(bf16[384,3072]{1,0:T(8,128)(2,1)} %shard_map.325.refs_1_.refs_3_), channel_id=1, source_target_pairs={{0,16},{16,0},{1,17},{17,1},{2,18},{18,2},{3,19},{19,3},{4,20},{20... | collective-permute-start | bytes 7077896 | tf_op jit(solution)/shard_map/ppermute | solution.py:524
  (63 other events, 343.4 us)

commit v3 on v1

v3 whole, which is shorter than its diff:
```python
import functools
import math

import jax
import jax.numpy as jnp
from jax import lax
from jax.experimental import pallas as pl
from jax.experimental.pallas import tpu as pltpu
from jax.sharding import PartitionSpec as P

HEAD_DIM = 64
SEQ = 64
GROUP = 16
CHUNK = 512

epsilon = 1e-06
score_scale = 10.0
margin_shift = score_scale * 0.3
root_half = 0.7071067811865476
gauss_norm = 0.3989422804014327

low = jnp.bfloat16
wide = jnp.float32
ANY = pl.BlockSpec(memory_space=pl.ANY)
VMEM = pl.BlockSpec(memory_space=pltpu.VMEM)
SMEM = pl.BlockSpec(memory_space=pltpu.SMEM)
HBM = pl.BlockSpec(memory_space=pltpu.HBM)
MIB = 1 << 20


def struct(shape, dtype):
    return jax.ShapeDtypeStruct(shape, dtype)


def call(body, ins, outs, bits=None, scratch=(), aliases=None, after=(), limit=10, far=(), far_out=(), hand_out=(), cost=460):
    first = 0 if bits is None else 1
    ins = [pltpu.with_memory_space_constraint(a, pltpu.HBM) if i in far else a for i, a in enumerate(ins)]

    def wrapped(*refs):
        body(*refs[: first + len(ins)], *refs[first + len(ins) + len(after) :])

    return pl.pallas_call(
        wrapped,
        in_specs=[SMEM] * first + [HBM if i in far else VMEM for i in range(len(ins))] + [ANY] * len(after),
        out_specs=[HBM if i in hand_out else VMEM for i in range(len(outs))],
        out_shape=[(pltpu.HBM if i in far_out or i in hand_out else pltpu.VMEM)(o.shape, o.dtype) for i, o in enumerate(outs)],
        scratch_shapes=list(scratch),
        input_output_aliases={first + k: v for k, v in (aliases or {}).items()},
        cost_estimate=pl.CostEstimate(flops=cost * 2 * 10**8, bytes_accessed=0, transcendentals=0),
        compiler_params=pltpu.CompilerParams(vmem_limit_bytes=limit * MIB),
    )(*([] if bits is None else [bits]), *ins, *after)


def row_of(ref, start=0, size=None):
    return ref[pl.ds(start, ref.shape[0] if size is None else size)].reshape(1, -1)


def mat_mul(a, b):
    return jnp.dot(a, b, preferred_element_type=wide)


def trans_left(a, b):
    return lax.dot_general(a, b, (((0,), (0,)), ((), ())), preferred_element_type=wide)


def trans_right(a, b):
    return lax.dot_general(a, b, (((1,), (1,)), ((), ())), preferred_element_type=wide)


def normalize(h):
    center = h - jnp.mean(h, axis=-1, keepdims=True)
    inv = lax.rsqrt(jnp.mean(center * center, axis=-1, keepdims=True) + epsilon)
    return center * inv, inv


def norm_input_grad(grad, normed, inv):
    return inv * (
        grad
        - jnp.mean(grad, axis=-1, keepdims=True)
        - normed * jnp.mean(grad * normed, axis=-1, keepdims=True)
    )


def split_heads(pair, first):
    zero = jnp.zeros_like(pair)
    return jnp.concatenate([jnp.where(first, pair, zero), jnp.where(first, zero, pair)], axis=0)


def join_heads(rows, first):
    return jnp.where(first, rows[:SEQ], rows[SEQ:])


def attention_forward(bits, x, w_qkv, b_qv, w_out, b_out, gain, bias, later):
    tokens, width = x.shape
    rows = 4 * SEQ
    pairs = width // (2 * HEAD_DIM)
    scale = 1.0 / math.sqrt(HEAD_DIM)

    def body(_bits, *refs):
        n = len(later)
        far, far_later, outs, near_later, near, sems = (
            refs[:7], refs[7 : 7 + n], refs[7 + n : 13 + n], refs[13 + n : 13 + 2 * n], refs[13 + 2 * n : -1], refs[-1]
        )
        proj_ref, prob_ref, ctx_ref, hid_ref, low_ref, inv_ref = outs
        x_ref, wq_ref, bqv_ref, wo_ref, bo_ref, g_ref, b_ref = near
        pairs_of = zip(far + far_later, near + near_later)
        copies = [pltpu.make_async_copy(f, near_f, sems.at[i]) for i, (f, near_f) in enumerate(pairs_of)]
        for copy in copies:
            copy.start()
        for copy in copies[:3]:
            copy.wait()
        first = lax.broadcasted_iota(jnp.int32, (SEQ, 128), 1) < HEAD_DIM
        cols = [slice(p * 128, (p + 1) * 128) for p in range(pairs)]

        @pl.loop(0, tokens // rows)
        def _(step):
            base = pl.multiple_of(step * rows, rows)
            block = pl.ds(base, rows)
            x_in = x_ref[block, :]
            for part in range(3):
                c = slice(part * width, (part + 1) * width)
                value = mat_mul(x_in, wq_ref[:, c])
                if part != 1:
                    value = value + row_of(bqv_ref, (part // 2) * width, width)
                proj_ref[block, c] = value.astype(low)
            for sent in range(4):
                r = pl.ds(pl.multiple_of(base + sent * SEQ, SEQ), SEQ)
                q = proj_ref[r, :width]
                k = proj_ref[r, width : 2 * width]
                v = proj_ref[r, 2 * width :]
                scores = (
                    jnp.concatenate([trans_right(k[:, c], split_heads(q[:, c], first)) for c in cols], axis=1) * scale
                )
                e = jnp.exp(scores - jnp.max(scores, axis=0, keepdims=True))
                probs = (e * (1.0 / jnp.sum(e, axis=0, keepdims=True))).astype(low)
                prob_ref[r, :] = probs
                ctx_ref[r, :] = jnp.concatenate(
                    [join_heads(trans_left(probs[:, c], v[:, c]), first) for c in cols], axis=1
                ).astype(low)

            @pl.when(step == 0)
            def _():
                for copy in copies[3:7]:
                    copy.wait()

            h = x_in.astype(wide) + mat_mul(ctx_ref[block, :], wo_ref[...]) + row_of(bo_ref)
            normed, inv = normalize(h)
            hidden = normed * row_of(g_ref) + row_of(b_ref)
            hid_ref[block, :] = hidden
            low_ref[block, :] = hidden.astype(low)
            inv_ref[block, :] = inv

        for copy in copies[7:]:
            copy.wait()

    return call(
        body,
        [x, w_qkv, b_qv, w_out, b_out, gain, bias] + later,
        [
            struct((tokens, 3 * width), low),
            struct((tokens, width), low),
            struct((tokens, width), low),
            struct((tokens, width), wide),
            struct((tokens, width), low),
            struct((tokens, 1), wide),
        ]
        + [struct(v.shape, v.dtype) for v in later],
        scratch=[pltpu.VMEM(v.shape, v.dtype) for v in (x, w_qkv, b_qv, w_out, b_out, gain, bias)]
        + [pltpu.SemaphoreType.DMA((7 + len(later),))],
        bits=bits,
        far=range(7 + len(later)),
        limit=14,
    )


def ffn_forward_rows(hidden, wi_ref, bi_ref, wd_ref, bd_ref, store_act, store_slope):
    h_low = hidden.astype(low)
    total = hidden + row_of(bd_ref)
    for c in range(0, wi_ref.shape[1], CHUNK):
        u = mat_mul(h_low, wi_ref[:, c : c + CHUNK]) + row_of(bi_ref, c, CHUNK)
        phi = 0.5 + 0.5 * lax.erf(u * root_half)
        act = (u * phi).astype(low)
        store_act(c, act)
        store_slope(c, (phi + u * jnp.exp(-0.5 * u * u) * gauss_norm).astype(low))
        total = total + mat_mul(act, wd_ref[c : c + CHUNK, :])
    return normalize(total)


def ffn_backward_rows(grad_block, normed, inv, gain, wd_ref, slope_of, store_gate, small_ref, bin_ref):
    grad_two = norm_input_grad(grad_block * gain, normed, inv)
    small_ref[0:1, :] += jnp.sum(grad_block * normed, axis=0, keepdims=True)
    small_ref[1:2, :] += jnp.sum(grad_block, axis=0, keepdims=True)
    small_ref[2:3, :] += jnp.sum(grad_two, axis=0, keepdims=True)
    grad_low = grad_two.astype(low)
    for c in range(0, wd_ref.shape[0], CHUNK):
        gate = trans_right(grad_low, wd_ref[c : c + CHUNK, :]) * slope_of(c).astype(wide)
        bin_ref[:, c : c + CHUNK] += jnp.sum(gate, axis=0, keepdims=True)
        store_gate(c, gate.astype(low))
    return grad_low


def ffn_group(index, hidden, cot, upper, state, after=()):
    w_in, b_in, w_down, b_down, gain, bias = upper
    sents, _, width = hidden.shape
    ffn = w_in.shape[1]
    rows = sents * GROUP
    at = slice(index * GROUP, (index + 1) * GROUP)
    first = index == 0
    second = index == 1

    def stores(act_ref, slope_ref):
        def store_act(c, v):
            act_ref[:, at, c : c + CHUNK] = v.reshape(sents, GROUP, CHUNK)

        def store_slope(c, v):
            slope_ref[:, c : c + CHUNK] = v

        return store_act, store_slope

    def forward(h_ref, wi_ref, bi_ref, wd_ref, bd_ref, act_ref, slope_ref):
        return ffn_forward_rows(
            h_ref[:, at, :].reshape(rows, width), wi_ref, bi_ref, wd_ref, bd_ref, *stores(act_ref, slope_ref)
        )

    def body_first(h_ref, wi_ref, bi_ref, wd_ref, bd_ref, g_ref, b_ref, enc_hbm, act_ref, slope_ref, n_ref, inv_ref, first_ref, enc_ref, sem):
        normed, inv = forward(h_ref, wi_ref, bi_ref, wd_ref, bd_ref, act_ref, slope_ref)
        n_ref[...] = normed
        inv_ref[...] = inv
        block = (normed * row_of(g_ref) + row_of(b_ref)).reshape(sents, GROUP, width)
        enc_ref[...] = block.astype(low)
        copy = pltpu.make_async_copy(enc_ref, enc_hbm.at[:, pl.ds(index * GROUP, GROUP), :], sem)
        copy.start()
        first_ref[...] = block[:, 0, :].astype(low)
        copy.wait()

    enc_shape = struct((sents, SEQ, width), low)
    enc_scratch = [pltpu.VMEM((sents, GROUP, width), low), pltpu.SemaphoreType.DMA]
    act_shape = struct((sents, SEQ, ffn), low)
    if first:
        return call(
            body_first,
            [hidden, w_in, b_in, w_down, b_down, gain, bias],
            [
                enc_shape,
                act_shape,
                struct((rows, ffn), low),
                struct((rows, width), wide),
                struct((rows, 1), wide),
                struct((sents, width), low),
            ],
            scratch=enc_scratch,
            hand_out=[0],
        )

    def body(h_ref, cot_ref, wi_ref, bi_ref, wd_ref, bd_ref, g_ref, b_ref, *refs):
        refs = refs[2 if second else 4 :]
        if not second:
            sin_ref, bin_in_ref = refs[:2]
            refs = refs[2:]
        enc_hbm, act_ref, gate_ref, two_ref, small_ref, bin_ref, slope_ref, enc_ref, sem = refs
        small_ref[...] = jnp.zeros_like(small_ref) if second else sin_ref[...]
        bin_ref[...] = jnp.zeros_like(bin_ref) if second else bin_in_ref[...]

        def store_gate(c, v):
            gate_ref[:, at, c : c + CHUNK] = v.reshape(sents, GROUP, CHUNK)

        normed, inv = forward(h_ref, wi_ref, bi_ref, wd_ref, bd_ref, act_ref, slope_ref)
        gain_row = row_of(g_ref)
        enc_ref[...] = (normed * gain_row + row_of(b_ref)).astype(low).reshape(sents, GROUP, width)
        copy = pltpu.make_async_copy(enc_ref, enc_hbm.at[:, pl.ds(index * GROUP, GROUP), :], sem)
        copy.start()
        grad_block = cot_ref[:, at, :].reshape(rows, width).astype(wide)
        got = ffn_backward_rows(
            grad_block, normed, inv, gain_row, wd_ref, lambda c: slope_ref[:, c : c + CHUNK], store_gate, small_ref, bin_ref
        )
        two_ref[:, at, :] = got.reshape(sents, GROUP, width)
        copy.wait()

    aliases = {8: 0, 9: 1}
    if not second:
        aliases.update({10: 2, 11: 3})
    return call(
        body,
        [hidden, cot, w_in, b_in, w_down, b_down, gain, bias] + list(state),
        [enc_shape, act_shape, act_shape, enc_shape, struct((8, width), wide), struct((1, ffn), wide)],
        scratch=[pltpu.VMEM((rows, ffn), low)] + enc_scratch,
        aliases=aliases,
        after=after,
        far=[8],
        hand_out=[0],
    )


def ffn_first_back(cot, grad_first, normed, inv, slope, gain, w_down, gate, two, small, bin_sum):
    sents, _, width = cot.shape
    ffn = w_down.shape[0]
    rows = sents * GROUP
    at = slice(0, GROUP)

    def body(cot_ref, first_ref, n_ref, inv_ref, slope_ref, g_ref, wd_ref, sin_ref, bin_in_ref, _g, _t, gate_ref, two_ref, small_ref, bin_ref):
        small_ref[...] = sin_ref[...]
        bin_ref[...] = bin_in_ref[...]
        position = lax.broadcasted_iota(jnp.int32, (sents, GROUP, width), 1)
        at_first = jnp.broadcast_to(first_ref[...][:, None, :], (sents, GROUP, width))
        grad_block = cot_ref[:, at, :].astype(wide) + jnp.where(position == 0, at_first, 0.0)

        def store_gate(c, v):
            gate_ref[:, at, c : c + CHUNK] = v.reshape(sents, GROUP, CHUNK)

        got = ffn_backward_rows(
            grad_block.reshape(rows, width), n_ref[...], inv_ref[...], row_of(g_ref), wd_ref,
            lambda c: slope_ref[:, c : c + CHUNK], store_gate, small_ref, bin_ref,
        )
        two_ref[:, at, :] = got.reshape(sents, GROUP, width)

    return call(
        body,
        [cot, grad_first, normed, inv, slope, gain, w_down, small, bin_sum, gate, two],
        [struct((sents, SEQ, ffn), low), struct((sents, SEQ, width), low), struct((8, width), wide), struct((1, ffn), wide)],
        aliases={9: 0, 10: 1},
    )


def lower_backward(part, parts, two, gate, hidden, inv, proj, probs, w_in, w_out, gain, bias, before=None, after=()):
    tokens, width = hidden.shape
    ffn = w_in.shape[1]
    rows = 4 * SEQ
    steps = tokens // rows // parts
    pairs = width // (2 * HEAD_DIM)
    scale = 1.0 / math.sqrt(HEAD_DIM)
    fresh = before is None

    def body(two_ref, gate_ref, hid_ref, inv_ref, proj_ref, prob_ref, wi_ref, wo_ref, g_ref, b_ref, *refs):
        if not fresh:
            sin_ref, bin_ref = refs[2:4]
            refs = refs[4:]
        one_ref, gp_ref, small_ref, bqv_ref, ctx_ref = refs
        small_ref[...] = jnp.zeros_like(small_ref) if fresh else sin_ref[...]
        bqv_ref[...] = jnp.zeros_like(bqv_ref) if fresh else bin_ref[...]
        first = lax.broadcasted_iota(jnp.int32, (SEQ, 128), 1) < HEAD_DIM
        cols = [slice(p * 128, (p + 1) * 128) for p in range(pairs)]

        @pl.loop(0, steps)
        def _(step):
            base = pl.multiple_of((step + part * steps) * rows, rows)
            block = pl.ds(base, rows)
            gain_row = row_of(g_ref)
            grad_hidden = two_ref[block, :].astype(wide) + trans_right(gate_ref[block, :], wi_ref[...])
            normed = (hid_ref[block, :] - row_of(b_ref)) * (1.0 / gain_row)
            small_ref[0:1, :] += jnp.sum(grad_hidden * normed, axis=0, keepdims=True)
            small_ref[1:2, :] += jnp.sum(grad_hidden, axis=0, keepdims=True)
            grad_one = norm_input_grad(grad_hidden * gain_row, normed, inv_ref[block, :])
            small_ref[2:3, :] += jnp.sum(grad_one, axis=0, keepdims=True)
            one_low = grad_one.astype(low)
            one_ref[block, :] = one_low
            ctx_ref[...] = trans_right(one_low, wo_ref[...]).astype(low)
            sum_q = jnp.zeros((1, width), wide)
            sum_v = jnp.zeros((1, width), wide)
            for sent in range(4):
                r = pl.ds(pl.multiple_of(base + sent * SEQ, SEQ), SEQ)
                q_all = proj_ref[r, :width]
                k = proj_ref[r, width : 2 * width]
                v = proj_ref[r, 2 * width :]
                d_all = ctx_ref[sent * SEQ : (sent + 1) * SEQ, :]
                p_low = prob_ref[r, :]
                q = [split_heads(q_all[:, c], first) for c in cols]
                d = [split_heads(d_all[:, c], first) for c in cols]
                p = p_low.astype(wide)
                grad_p = jnp.concatenate([trans_right(v[:, c], dd) for c, dd in zip(cols, d)], axis=1)
                grad_v = jnp.concatenate([mat_mul(p_low[:, c], dd) for c, dd in zip(cols, d)], axis=1)
                gp = grad_p * p
                grad_s = (gp - p * jnp.sum(gp, axis=0, keepdims=True)).astype(low)
                grad_k = jnp.concatenate([mat_mul(grad_s[:, c], qq) for c, qq in zip(cols, q)], axis=1) * scale
                grad_q = (
                    jnp.concatenate([join_heads(trans_left(grad_s[:, c], k[:, c]), first) for c in cols], axis=1) * scale
                )
                sum_q += jnp.sum(grad_q, axis=0, keepdims=True)
                sum_v += jnp.sum(grad_v, axis=0, keepdims=True)
                gp_ref[r, :width] = grad_q.astype(low)
                gp_ref[r, width : 2 * width] = grad_k.astype(low)
                gp_ref[r, 2 * width :] = grad_v.astype(low)
            bqv_ref[0:1, :] += sum_q
            bqv_ref[1:2, :] += sum_v

    return call(
        body,
        [two, gate, hidden, inv, proj, probs, w_in, w_out, gain, bias] + ([] if fresh else list(before)),
        [struct((tokens, width), low), struct((tokens, 3 * width), low), struct((8, width), wide), struct((8, width), wide)],
        scratch=[pltpu.VMEM((rows, width), low)],
        aliases=None if fresh else {10: 0, 11: 1},
        after=after,
    )


def input_gradient(grad_proj, w_qkv, grad_one, after=()):
    tokens, width = grad_one.shape
    rows = 4 * SEQ

    def body(gp_ref, w_ref, one_ref, out_ref, token):
        token[...] = jnp.zeros_like(token)

        @pl.loop(0, tokens // rows)
        def _(step):
            block = pl.ds(pl.multiple_of(step * rows, rows), rows)
            out_ref[block, :] = (one_ref[block, :].astype(wide) + trans_right(gp_ref[block, :], w_ref[...])).astype(low)

    return call(
        body, [grad_proj, w_qkv, grad_one], [struct((tokens, width), low), struct((8, 128), wide)], after=after, far_out=[0]
    )


def pooler_gradients(flat, id_column, id_row, w_pool, b_pool):
    total = flat.shape[0] // 2
    pooled = jnp.tanh(mat_mul(flat, w_pool) + b_pool)
    inv_len = lax.rsqrt(jnp.sum(pooled * pooled, axis=-1, keepdims=True) + epsilon)
    unit = pooled * inv_len
    embed = unit.astype(low)
    zero, one = embed[:total], embed[total:]
    square = (total, total)
    eye = (lax.broadcasted_iota(jnp.int32, square, 0) == lax.broadcasted_iota(jnp.int32, square, 1)).astype(wide)
    logits = score_scale * trans_right(zero, one) - margin_shift * eye
    masked = jnp.where(id_column == id_row, logits, -jnp.inf)

    def soft(axis):
        e = jnp.exp(masked - jnp.max(masked, axis=axis, keepdims=True))
        return (score_scale * (e / jnp.sum(e, axis=axis, keepdims=True) - eye)).astype(low)

    by_row, by_col = soft(1), soft(0)
    grad_embed = jnp.concatenate(
        [mat_mul(by_row, one) + mat_mul(by_col, one), trans_left(by_row, zero) + trans_left(by_col, zero)], axis=0
    )
    grad_pre = (
        inv_len * (grad_embed - unit * jnp.sum(unit * grad_embed, axis=-1, keepdims=True)) * (1.0 - pooled * pooled)
    )
    pre_low = grad_pre.astype(low)
    return pre_low, trans_left(flat, pre_low), jnp.sum(grad_pre, axis=0, keepdims=True)


def contrastive(own, got, bits, sents, id_column, id_row, w_pool, b_pool, after):
    total, width = own.shape
    if total > 512:
        start = bits[CORE] * total + bits[PLACE] * sents
        flat = jnp.where(bits[CORE] == 0, jnp.concatenate([own, got]), jnp.concatenate([got, own]))
        pre_low, grad_w, grad_b = pooler_gradients(flat, id_column, id_row, w_pool, b_pool.reshape(1, -1))
        return trans_right(lax.dynamic_slice_in_dim(pre_low, start, sents), w_pool), grad_w, grad_b.reshape(-1)

    def body(b, own_ref, got_ref, col_ref, row_ref, w_ref, b_ref, first_ref, gw_ref, gb_ref, flat_ref, pre_ref):
        flat_ref[pl.ds(pl.multiple_of(b[CORE] * total, total), total), :] = own_ref[...]
        flat_ref[pl.ds(pl.multiple_of((1 - b[CORE]) * total, total), total), :] = got_ref[...]
        pre_low, grad_w, grad_b = pooler_gradients(flat_ref[...], col_ref[...], row_ref[...], w_ref[...], row_of(b_ref))
        pre_ref[...] = pre_low
        gw_ref[...] = grad_w
        gb_ref[...] = grad_b.reshape(-1)
        first_ref[...] = trans_right(pre_ref[pl.ds(pl.multiple_of(b[CORE] * total + b[PLACE] * sents, sents), sents), :], w_ref[...])

    return call(
        body,
        [own, got, id_column, id_row, w_pool, b_pool],
        [struct((sents, width), wide), struct((width, width), wide), struct((width,), wide)],
        bits=bits,
        scratch=[pltpu.VMEM((2 * total, width), low)] * 2,
        after=after,
        far_out=[1, 2],
    )


def put_in_order(blocks, bits, low_bit, after):
    rows, width = blocks[0].shape

    def body(b, *refs):
        me = (b[PLACE] >> low_bit) & (len(blocks) - 1)
        for i, ref in enumerate(refs[:-1]):
            at = pl.multiple_of((me ^ i) * rows, rows)
            refs[-1][pl.ds(at, rows), :] = ref[...]

    return call(
        body, blocks, [struct((rows * len(blocks), width), low)], bits=bits, after=after, limit=8, cost=115
    )[0]


CORE, BIT0, BIT1, BIT2, PLACE = range(5)
SMALL = 16


def exchange(a, axis, mask):
    size = lax.axis_size(axis)
    return lax.ppermute(a, axis, [(i, i ^ mask) for i in range(size)])


class Sources:
    def __init__(self, pairs, small=None):
        self.pairs = pairs
        self.small = small
        self.m = pairs[0][0].shape[1]
        self.n = sum(g.shape[1] for _, g in pairs)
        self.flat = [a for pair in pairs for a in pair]


def gradient_rows(src, bits, recv, after=()):
    m, n = src.m, src.n
    half, quarter = m // 2, m // 4
    count = len(src.flat)
    edge = n // 2

    small = src.small or []
    extra = SMALL if small else 0

    if recv is None:

        def body(b, *refs):
            out = refs[count + len(small)]
            rows = pl.ds(pl.multiple_of((1 - b[CORE]) * half, 128), half)
            at = 0
            for a, g in zip(refs[:count:2], refs[1:count:2]):
                out[:half, at : at + g.shape[1]] = trans_left(a[:, rows], g[...]).astype(low)
                at += g.shape[1]
            if small:
                up, bin_sum, down, bqv = refs[count : count + 4]
                kept = refs[-1]
                width = up.shape[1]
                parts = [up[:3]] + [bin_sum[:, c : c + width] for c in range(0, bin_sum.shape[1], width)] + [down[:3], bqv[:2]]
                parts.append(jnp.zeros((SMALL - sum(p.shape[0] for p in parts), width), wide))
                kept[...] = jnp.concatenate(parts, axis=0).astype(low)
                out[half:, :] = jnp.zeros((SMALL, n), low)
                out[half:, :width] = kept[...]

        shapes = [struct((half + extra, n), low)] + ([struct((SMALL, small[0].shape[1]), low)] if small else [])
        return call(body, src.flat + small, shapes, bits=bits, after=after)

    def body(b, *refs):
        got, left_send, left_keep, right_send, right_keep = refs[-5:]
        rows = pl.ds(pl.multiple_of(b[CORE] * half, 128), half)
        if extra:
            total = (refs[count][...].astype(wide) + got[half:, : refs[count].shape[1]].astype(wide)).astype(low)
            for ref in (left_send, left_keep):
                ref[quarter:, :] = jnp.zeros((SMALL, edge), low)
                ref[quarter:, : total.shape[1]] = total
        for side, bit, send, keep in ((0, BIT0, left_send, left_keep), (1, BIT1, right_send, right_keep)):
            at = 0
            for a, g in zip(refs[:count:2], refs[1:count:2]):
                lo, hi = max(at, side * edge), min(at + g.shape[1], (side + 1) * edge)
                if lo < hi:
                    c = slice(lo - side * edge, hi - side * edge)
                    value = (trans_left(a[:, rows], g[:, lo - at : hi - at]) + got[:half, lo:hi].astype(wide)).astype(low)

                    def put(kept, c=c, value=value, send=send, keep=keep):
                        keep[:quarter, c] = value[kept * quarter : (kept + 1) * quarter]
                        send[:quarter, c] = value[(1 - kept) * quarter : (2 - kept) * quarter]

                    pl.when(b[bit] == 0)(functools.partial(put, 0))
                    pl.when(b[bit] != 0)(functools.partial(put, 1))
                at += g.shape[1]

    shapes = [struct((quarter + e, edge), low) for e in (extra, extra, 0, 0)]
    return call(body, src.flat + ([src.kept] if small else []) + [recv], shapes, bits=bits, after=after)


def part_rows(ref, bit, rows):
    return ref[pl.ds(pl.multiple_of(bit * rows, rows), rows), :].astype(wide)


def whole_call(body, arrays, shapes, bits, after=()):
    return call(body, arrays, [struct(s, low) for s in shapes], bits=bits, after=after, limit=8, cost=115)


def halve_sides(left, left_got, right, right_got, bits, after=()):
    rows, cols = right.shape[0] // 2, right.shape[1]
    extra = left.shape[0] - right.shape[0]

    def body(b, l, lg, r, rg, ls, lk, rs, rk):
        for mine, got, bit, send, keep in ((l, lg, BIT1, ls, lk), (r, rg, BIT0, rs, rk)):
            send[:rows, :] = (part_rows(mine, 1 - b[bit], rows) + part_rows(got, 1 - b[bit], rows)).astype(low)
            keep[:rows, :] = (part_rows(mine, b[bit], rows) + part_rows(got, b[bit], rows)).astype(low)
        if extra:
            total = (l[2 * rows :, :].astype(wide) + lg[2 * rows :, :].astype(wide)).astype(low)
            ls[rows:, :] = total
            lk[rows:, :] = total

    shapes = [(rows + e, cols) for e in (extra, extra, 0, 0)]
    return whole_call(body, [left, left_got, right, right_got], shapes, bits, after)


def halve_both(left, left_got, right, right_got, bits, after=()):
    rows, cols = right.shape[0] // 2, right.shape[1]
    extra = left.shape[0] - right.shape[0]

    def body(b, l, lg, r, rg, send, keep):
        for mine, got, c in ((l, lg, slice(0, cols)), (r, rg, slice(cols, 2 * cols))):
            send[:rows, c] = (part_rows(mine, 1 - b[BIT2], rows) + part_rows(got, 1 - b[BIT2], rows)).astype(low)
            keep[:rows, c] = (part_rows(mine, b[BIT2], rows) + part_rows(got, b[BIT2], rows)).astype(low)
        if extra:
            total = (l[2 * rows :, :].astype(wide) + lg[2 * rows :, :].astype(wide)).astype(low)
            for ref in (send, keep):
                ref[rows:, :cols] = total
                ref[rows:, cols:] = jnp.zeros_like(total)

    return whole_call(body, [left, left_got, right, right_got], [(rows + extra, 2 * cols)] * 2, bits, after)


def add_up(mine, got, bits, after=()):
    def body(b, m, g, out):
        out[...] = (m[...].astype(wide) + g[...].astype(wide)).astype(low)

    return whole_call(body, [mine, got], [mine.shape], bits, after)[0]


def place(out, mine, got, bit, cols=slice(None), rows=None):
    rows = mine.shape[0] if rows is None else rows
    out[pl.ds(pl.multiple_of(bit * rows, rows), rows), :] = mine[:rows, cols]
    out[pl.ds(pl.multiple_of((1 - bit) * rows, rows), rows), :] = got[:rows, cols]


def join_both(mine, got, rows, vectors, bits, after=()):
    cols = mine.shape[1] // 2
    width = vectors[1]

    def body(b, m, g, *refs):
        *outs, left, right = refs
        place(left, m, g, b[BIT2], slice(0, cols), rows)
        place(right, m, g, b[BIT2], slice(cols, 2 * cols), rows)
        at = rows
        for out in outs:
            for c in range(0, out.shape[0], width):
                out[pl.ds(c, width)] = m[at : at + 1, :width].astype(wide).reshape(-1)
                at += 1

    shapes = [struct((v,), wide) for v in vectors[0]] + [struct((2 * rows, cols), low)] * 2
    return call(body, [mine, got], shapes, bits=bits, after=after, limit=8, cost=115, far_out=range(len(vectors[0])))


def join_sides(left, left_got, right, right_got, bits, after=()):
    rows, cols = left.shape

    def body(b, l, lg, r, rg, lo, ro):
        place(lo, l, lg, b[BIT1])
        place(ro, r, rg, b[BIT0])

    return whole_call(body, [left, left_got, right, right_got], [(2 * rows, cols)] * 2, bits, after)


def join_half(left, left_got, right, right_got, bits, after=()):
    rows, cols = left.shape

    def body(b, l, lg, r, rg, out):
        place(out.at[:, pl.ds(0, cols)], l, lg, b[BIT0])
        place(out.at[:, pl.ds(cols, cols)], r, rg, b[BIT1])

    return whole_call(body, [left, left_got, right, right_got], [(2 * rows, 2 * cols)], bits, after)[0]


def widen(source, which, before, widths, bits, after=()):
    half, n = source.shape
    parts = 4
    tile = half // parts

    def body(b, src, *refs):
        refs = refs[0 if before is None else len(before) :]
        outs, token, bufs, sems = refs[: len(widths)], refs[len(widths)], refs[len(widths) + 1 : -1], refs[-1]
        token[...] = jnp.zeros_like(token)
        start = (1 - b[CORE] if which else b[CORE]) * half
        copies = []
        for t in range(parts):
            at = 0
            for out, buf, w in zip(outs, bufs, widths):
                buf[t] = src[t * tile : (t + 1) * tile, at : at + w].astype(wide)
                rows = pl.ds(pl.multiple_of(start + t * tile, tile), tile)
                copies.append(pltpu.make_async_copy(buf.at[t], out.at[rows, :], sems.at[len(copies)]))
                copies[-1].start()
                at += w
        for copy in copies:
            copy.wait()

    return call(
        body,
        [source] + list(before or []),
        [struct((2 * half, w), wide) for w in widths] + [struct((8, 128), wide)],
        bits=bits,
        scratch=[pltpu.VMEM((parts, tile, w), wide) for w in widths] + [pltpu.SemaphoreType.DMA((parts * len(widths),))],
        aliases={1 + i: i for i in range(len(widths))} if before else None,
        after=after,
        far=range(1, 1 + len(widths)) if before else (),
        hand_out=range(len(widths)),
        limit=12,
        cost=115,
    )


class Reduction:
    def __init__(self, src, widths, bits, clock, tail, vectors=()):
        self.vectors = vectors
        self.src, self.widths, self.bits, self.clock, self.tail = src, widths, bits, clock, tail

    def step(self, fn, *args):
        out = fn(*args, after=self.clock.now())
        self.clock.set(out[-1] if isinstance(out, (list, tuple)) else out)
        return out

    def core_send(self):
        send, *kept = self.step(gradient_rows, self.src, self.bits, None)
        if kept:
            self.src.kept = kept[0]
        self.got = exchange(send, "stream", 1)

    def core_sum(self):
        ls, self.l, rs, self.r = self.step(gradient_rows, self.src, self.bits, self.got)
        self.gl, self.gr = exchange(ls, "dp", 1), exchange(rs, "dp", 2)

    def first_sum(self):
        ls, self.l, rs, self.r = self.step(halve_sides, self.l, self.gl, self.r, self.gr, self.bits)
        self.gl, self.gr = exchange(ls, "dp", 2), exchange(rs, "dp", 1)

    def second_sum(self):
        send, self.v = self.step(halve_both, self.l, self.gl, self.r, self.gr, self.bits)
        self.got = exchange(send, "dp", 4)

    def third_sum(self):
        self.v = self.step(add_up, self.v, self.got, self.bits)
        self.got = exchange(self.v, "dp", self.tail[0])

    def last_sum(self):
        for mask in self.tail[1:]:
            self.v = self.step(add_up, self.v, self.got, self.bits)
            self.got = exchange(self.v, "dp", mask)
        self.v = self.step(add_up, self.v, self.got, self.bits)
        self.got = exchange(self.v, "dp", 4)

    def third_back(self):
        vectors = self.vectors, self.src.small[0].shape[1] if self.src.small else None
        *self.sums, self.l, self.r = self.step(join_both, self.v, self.got, self.src.m // 16, vectors, self.bits)
        self.gl, self.gr = exchange(self.l, "dp", 2), exchange(self.r, "dp", 1)

    def second_back(self):
        self.l, self.r = self.step(join_sides, self.l, self.gl, self.r, self.gr, self.bits)
        self.gl, self.gr = exchange(self.l, "dp", 1), exchange(self.r, "dp", 2)

    def first_back(self):
        self.v = self.step(join_half, self.l, self.gl, self.r, self.gr, self.bits)
        self.got = exchange(self.v, "stream", 1)

    def finish_own(self):
        self.out = self.step(widen, self.v, 0, None, self.widths, self.bits)[:-1]

    def finish(self):
        return self.step(widen, self.got, 1, self.out, self.widths, self.bits)[:-1]


class Clock:
    def __init__(self, start):
        self.last = start

    def now(self):
        return (self.last,)

    def set(self, value):
        self.last = value


def shards(
    embedded, seq_cotangent, pair_ids, w_qkv, b_qv, w_out, b_out, ln1_gain, ln1_bias, w_in, b_in, w_down, b_down,
    ln2_gain, ln2_bias, w_pool, b_pool,
):
    x = embedded[0]
    tokens, width = x.shape
    sents = tokens // SEQ
    ffn = w_in.shape[1]
    dp = lax.axis_size("dp")
    stream, place_dp = lax.axis_index("stream"), lax.axis_index("dp")
    bits = jnp.stack([stream, place_dp & 1, (place_dp >> 1) & 1, (place_dp >> 2) & 1, place_dp]).astype(jnp.int32)
    later = [
        w_in, w_down, seq_cotangent[0], w_pool, b_in, b_down, ln2_gain, ln2_bias, b_pool, pair_ids[:, None], pair_ids[None, :]
    ]
    proj, probs, context, hidden, hidden_low, inv_one, *later = attention_forward(
        bits, x, w_qkv, b_qv, w_out, b_out, ln1_gain, ln1_bias, later
    )
    w_in, w_down, cotangent, w_pool, b_in, b_down, ln2_gain, ln2_bias, b_pool, id_column, id_row = later
    hid3 = hidden.reshape(sents, SEQ, width)
    cot3 = cotangent.reshape(sents, SEQ, width)
    upper = (w_in, b_in, w_down, b_down, ln2_gain, ln2_bias)
    enc, act, slope, normed_two, inv_two, first_low = ffn_group(0, hid3, cot3, upper, ())
    masks = [1 << i for i in range(dp.bit_length() - 1)]
    state = [enc, act]
    gathered = first_low
    group = 1
    order = [inv_two]
    for low_bit in range(0, len(masks), 2):
        span = 4 if low_bit + 1 < len(masks) else 2
        blocks = [gathered] + [exchange(gathered, "dp", i << low_bit) for i in range(1, span)]
        if group < SEQ // GROUP:
            state = ffn_group(group, hid3, cot3, upper, state, after=order)
            group += 1
            order = [state[-1]]
        gathered = put_in_order(blocks, bits, low_bit, order)
        order = [gathered]
    other = exchange(gathered, "stream", 1)
    while group < SEQ // GROUP:
        state = ffn_group(group, hid3, cot3, upper, state, after=order)
        group += 1
        order = [state[-1]]
    enc, act, gate, two, small_up, bin_sum = state
    grad_first, grad_w_pool, grad_b_pool = contrastive(
        gathered, other, bits, sents, id_column, id_row, w_pool, b_pool, order
    )
    gate, two, small_up, bin_sum = ffn_first_back(
        cot3, grad_first, normed_two, inv_two, slope, ln2_gain, w_down, gate, two, small_up, bin_sum
    )
    clock = Clock(small_up)
    act, gate, two = (v.reshape(tokens, -1) for v in (act, gate, two))
    tail = masks[3:]
    down = Reduction(Sources([(act, two)]), [width], bits, clock, tail)
    into = Reduction(Sources([(hidden_low, gate)]), [ffn], bits, clock, tail)
    down.core_send()
    into.core_send()
    down.core_sum()
    lower = (two, gate, hidden, inv_one, proj, probs, w_in, w_out, ln1_gain, ln1_bias)
    state = lower_backward(0, 2, *lower, after=clock.now())
    clock.set(state[-1])
    state = lower_backward(1, 2, *lower, before=state, after=clock.now())
    grad_one, grad_proj, small_low, bqv = state
    clock.set(bqv)
    down.first_sum()
    into.core_sum()
    low_part = Reduction(
        Sources([(x, grad_proj), (context, grad_one)], [small_up, bin_sum, small_low, bqv]),
        [3 * width, width],
        bits,
        clock,
        tail,
        (width, width, width, ffn, width, width, width, 2 * width),
    )
    down.second_sum()
    low_part.core_send()
    down.third_sum()
    into.first_sum()
    low_part.core_sum()
    into.second_sum()
    down.last_sum()
    grad_input, token = input_gradient(grad_proj, w_qkv, grad_one, after=clock.now())
    clock.set(token)
    low_part.first_sum()
    into.third_sum()
    down.third_back()
    low_part.second_sum()
    down.second_back()
    into.last_sum()
    low_part.third_sum()
    into.third_back()
    down.first_back()
    down.finish_own()
    into.second_back()
    low_part.last_sum()
    (out_down,) = down.finish()
    low_part.third_back()
    into.first_back()
    into.finish_own()
    low_part.second_back()
    (out_in,) = into.finish()
    low_part.first_back()
    low_part.finish_own()
    out_qkv, out_out = low_part.finish()
    g_ln2_gain, g_ln2_bias, g_b_down, g_b_in, g_ln1_gain, g_ln1_bias, g_b_out, g_b_qv = low_part.sums
    return (
        enc.reshape(1, tokens, width),
        grad_input[None],
        out_qkv,
        g_b_qv,
        out_out,
        g_b_out,
        g_ln1_gain,
        g_ln1_bias,
        out_in,
        g_b_in,
        out_down,
        g_b_down,
        g_ln2_gain,
        g_ln2_bias,
        grad_w_pool,
        grad_b_pool,
    )


def solution(mesh):
    sharded = P("stream", "dp", None)
    return jax.shard_map(
        shards,
        mesh=mesh,
        in_specs=(sharded, sharded) + (P(),) * 15,
        out_specs=(sharded, sharded) + (P(),) * 14,
        check_vma=False,
    )
```

time: 462 us -> 244 us (0.53); the launches traced: 454 us -> 241 us
  other arithmetic: 90 us -> 0 us
  waiting for transfers between devices: 109 us -> 60.5 us
  local copies, waits for them, and re-layouts: 39 us -> 3.58 us
  starting transfers between devices: 71.3 us -> 44.8 us
  Pallas kernels: 137 us -> 131 us
  matrix products: 5.33 us -> 0 us
    ppermute x70 -> x46, waiting for transfers between devices: 109 us -> 60.5 us  [exchange(): return lax.ppermute(a, axis, [(i, i ^ mask) for i in range(size)])]
    concatenate x38 -> x0, other arithmetic: 47.8 us -> none  [the longest x35 46.6 us: gather_ordered(): jnp.concatenate([got, a, got])]
    convert_element_type x35 -> x0, other arithmetic: 39.1 us -> none  [the longest x24 19.9 us: reduce_parts(): sum((take_half(t, 1 - bit, n).astype(wide) for t in terms)).astype(low)]
    ppermute x70 -> x46, starting transfers between devices: 71.3 us -> 44.8 us  [exchange(): return lax.ppermute(a, axis, [(i, i ^ mask) for i in range(size)])]
    unnamed x110 -> x22, local copies, waits for them, and re-layouts: 16.8 us -> 2.02 us
    slice x11 -> x0, local copies, waits for them, and re-layouts: 10.1 us -> none  [the longest x1 2.68 us: shards(): grad_w_in[:, :half]]
    pallas_call x10 -> x45, Pallas kernels: 137 us -> 131 us  [call(): pl.pallas_call(wrapped, in_specs=[SMEM] * first + [HBM if i in far else V...]
    reshape x10 -> x0, local copies, waits for them, and re-layouts: 6.07 us -> none  [the longest x7 4.15 us: shards(): row = lambda v: v.reshape(1, -1)]
  transfers between devices with their start and end apart: 70 -> 46, of which waited for: 37 -> 20; matrix products, arithmetic and copies ran while one was open for 20% -> 0% of each run, Pallas kernels for 9% -> 38%
where the time goes in v3:
time: 244 us; the launch traced here: 241 us
  Pallas kernels  131 us (54%)
  waiting for transfers between devices  60.5 us (25%)
  starting transfers between devices  44.8 us (18%)
  local copies, waits for them, and re-layouts  3.58 us (1%)
    pallas_call x45, Pallas kernels, call(): pl.pallas_call(wrapped, in_specs=[SMEM] * first + [HBM if i in far else V...  131 us
    ppermute x46, waiting for transfers between devices, exchange(): return lax.ppermute(a, axis, [(i, i ^ mask) for i in range(size)])  60.5 us
    ppermute x46, starting transfers between devices, exchange(): return lax.ppermute(a, axis, [(i, i ^ mask) for i in range(size)])  44.8 us
  transfers between devices with their start and end apart: 46, of which 20 were waited for; matrix products, arithmetic and copies ran while one was open for 0% of the time, Pallas kernels for 38%

profile of v3, /device:TPU:0, one launch (start us, length us, event | category | flops | bytes accessed | tf_op | source)
XLA Modules:
  0.0 241.0 jit_solution(6422057489832668640)
XLA Ops:
  2.2 16.8 %shard_map.288 = (bf16[1024,2304]{1,0:T(8,128)(2,1)S(1)}, bf16[1024,768]{1,0:T(8,128)(2,1)S(1)}, bf16[1024,768]{1,0:T(8,128)(2,1)S(1)}, f32[1024,768]{1,0:T(8,12...) custom-call(s32[5]{0:T(128)S(1)} %stack.23.refs_0_, ...), custom_call_target="tpu_custom_call" | custom-call | flops 92000002048 | tf_op jit(solution)/shard_map/pallas_call | solution.py:42
  19.0 4.9 %shard_map.289 = (bf16[16,64,768]{2,1,0:T(8,128)(2,1)}, bf16[16,64,3072]{2,1,0:T(8,128)(2,1)S(1)}, bf16[256,3072]{1,0:T(8,128)(2,1)S(1)}, f32[256,768]{1,0:T(8,1...) custom-call(f32[16,64,768]{2,1,0:T(8,128)S(1)} %bitcast.25, ...), custom_call_target="tpu_custom_call" | custom-call | flops 92000002048 | tf_op jit(solution)/shard_map/pallas_call | solution.py:42
  24.0 4.0 %collective-permute-start.2 = (bf16[16,768]{1,0:T(8,128)(2,1)S(1)}, bf16[16,768]{1,0:T(8,128)(2,1)S(1)}, u32[]{:S(2)}, u32[]{:S(2)}) collective-permute-start(bf16[16,768]{1,0:T(8,128)(2,1)S(1)} %get-tuple-element.156.refs_1_), channel_id=1, source_target_pairs={{0,3},{1,2},{2,1},{3,0},{4,7},{5,6},{6,5},{7,4},{8,11},{9,10},{10,... | collective-permute-start | bytes 73736 | tf_op jit(solution)/shard_map/ppermute | solution.py:487
  28.6 5.8 %shard_map.290 = (bf16[16,64,768]{2,1,0:T(8,128)(2,1)}, bf16[16,64,3072]{2,1,0:T(8,128)(2,1)S(1)}, bf16[16,64,3072]{2,1,0:T(8,128)(2,1)S(1)}, bf16[16,64,768]{2,...) custom-call(f32[16,64,768]{2,1,0:T(8,128)S(1)} %bitcast.26, ...), custom_call_target="tpu_custom_call", output_to_operand_aliasing={{0}: (8, {}), {1}: (9, {})} | custom-call | flops 92000002048 | tf_op jit(solution)/shard_map/pallas_call | solution.py:42
  34.9 4.1 %collective-permute-start.5 = (bf16[64,768]{1,0:T(8,128)(2,1)S(1)}, bf16[64,768]{1,0:T(8,128)(2,1)S(1)}, u32[]{:S(2)}, u32[]{:S(2)}) collective-permute-start(bf16[64,768]{1,0:T(8,128)(2,1)S(1)} %shard_map.291.refs_14_.refs_1_), channel_id=1, source_target_pairs={{0,12},{1,13},{2,14},{3,15},{4,8},{5,9},{6,10},{7,11},{8,4},{9,5},... | collective-permute-start | bytes 294920 | tf_op jit(solution)/shard_map/ppermute | solution.py:487
  39.7 6.4 %shard_map.292 = (bf16[16,64,768]{2,1,0:T(8,128)(2,1)}, bf16[16,64,3072]{2,1,0:T(8,128)(2,1)S(1)}, bf16[16,64,3072]{2,1,0:T(8,128)(2,1)S(1)}, bf16[16,64,768]{2,...) custom-call(f32[16,64,768]{2,1,0:T(8,128)S(1)} %bitcast.27, ...), custom_call_target="tpu_custom_call", output_to_operand_aliasing={{0}: (8, {}), {1}: (9, {}), {2}: (10, {}), {3}: (11, {})} | custom-call | flops 92000002048 | tf_op jit(solution)/shard_map/pallas_call | solution.py:42
  47.1 6.2 %shard_map.294 = (bf16[16,64,768]{2,1,0:T(8,128)(2,1)}, bf16[16,64,3072]{2,1,0:T(8,128)(2,1)S(1)}, bf16[16,64,3072]{2,1,0:T(8,128)(2,1)S(1)}, bf16[16,64,768]{2,...) custom-call(f32[16,64,768]{2,1,0:T(8,128)S(1)} %bitcast.28, ...), custom_call_target="tpu_custom_call", output_to_operand_aliasing={{0}: (8, {}), {1}: (9, {}), {2}: (10, {}), {3}: (11, {})} | custom-call | flops 92000002048 | tf_op jit(solution)/shard_map/pallas_call | solution.py:42
  53.3 5.3 %shard_map.295 = (f32[16,768]{1,0:T(8,128)S(1)}, f32[768,768]{1,0:T(8,128)}, f32[768]{0:T(1024)}) custom-call(s32[5]{0:T(128)S(1)} %stack.23.refs_0_, bf16[256,768]{1,0:T(8,128)(2,1)S(1)} %shard_map.293.refs_14_.refs_1_, bf16[256,768]{1,0:T(8,128)(2,1)S(1)} %collective-permute-done.6.refs_2_, s32[256,1]{1,0:T(8,128)S(1)} %get-tuple-element.164.refs_3_, ...), custom_call_target="tpu_custom_call" | custom-call | flops 92000002048 | tf_op jit(solution)/shard_map/pallas_call | solution.py:42
  60.6 3.7 %shard_map.297.refs_3_ = bf16[1536,768]{1,0:T(8,128)(2,1)S(1)} custom-call(s32[5]{0:T(128)S(1)} %stack.23.refs_0_, bf16[1024,3072]{1,0:T(8,128)(2,1)S(1)} %bitcast.23, bf16[1024,768]{1,0:T(8,128)(2,1)S(1)} %bitcast.33, f32[8,768]{1,0:T(8,128)S(1)} %get-tuple-element.181.refs_3_.refs_5_), custom_call_target="tpu_custom_call" | custom-call | flops 92000002048 | tf_op jit(solution)/shard_map/pallas_call | solution.py:42
  65.4 4.6 %shard_map.298.refs_4_ = bf16[384,3072]{1,0:T(8,128)(2,1)} custom-call(s32[5]{0:T(128)S(1)} %stack.23.refs_0_, bf16[1024,768]{1,0:T(8,128)(2,1)S(1)} %get-tuple-element.182.refs_1_, bf16[1024,3072]{1,0:T(8,128)(2,1)S(1)} %bitcast.19, bf16[1536,768]{1,0:T(8,128)(2,1)S(1)} %shard_map.297.refs_3_), custom_call_target="tpu_custom_call" | custom-call | flops 92000002048 | tf_op jit(solution)/shard_map/pallas_call | solution.py:42
  70.2 5.6 %shard_map.299 = (bf16[768,384]{1,0:T(8,128)(2,1)}, bf16[768,384]{1,0:T(8,128)(2,1)S(1)}, bf16[768,384]{1,0:T(8,128)(2,1)}, bf16[768,384]{1,0:T(8,128)(2,1)S(1)}) custom-call(s32[5]{0:T(128)S(1)} %stack.23.refs_0_, bf16[1024,3072]{1,0:T(8,128)(2,1)S(1)} %bitcast.24, bf16[1024,768]{1,0:T(8,128)(2,1)S(1)} %bitcast.34, ...), custom_call_target="tpu_custom_call" | custom-call | flops 92000002048 | tf_op jit(solution)/shard_map/pallas_call | solution.py:42
  78.8 8.5 %shard_map.300 = (bf16[1024,768]{1,0:T(8,128)(2,1)S(1)}, bf16[1024,2304]{1,0:T(8,128)(2,1)S(1)}, f32[8,768]{1,0:T(8,128)S(1)}, f32[8,768]{1,0:T(8,128)S(1)}) custom-call(bf16[1024,768]{1,0:T(8,128)(2,1)S(1)} %bitcast.35, bf16[1024,3072]{1,0:T(8,128)(2,1)S(1)} %bitcast.20, f32[1024,768]{1,0:T(8,128)S(1)} %get-tuple-element.139.refs_2_, ...), custom_call_target="tpu_custom_call" | custom-call | flops 92000002048 | tf_op jit(solution)/shard_map/pallas_call | solution.py:42
  87.3 8.4 %shard_map.301 = (bf16[1024,768]{1,0:T(8,128)(2,1)S(1)}, bf16[1024,2304]{1,0:T(8,128)(2,1)S(1)}, f32[8,768]{1,0:T(8,128)S(1)}, f32[8,768]{1,0:T(8,128)S(1)}) custom-call(bf16[1024,768]{1,0:T(8,128)(2,1)S(1)} %bitcast.36, bf16[1024,3072]{1,0:T(8,128)(2,1)S(1)} %bitcast.21, ...), custom_call_target="tpu_custom_call", output_to_operand_aliasing={{0}: (10, {}), {1}: (11, {})} | custom-call | flops 92000002048 | tf_op jit(solution)/shard_map/pallas_call | solution.py:42
  98.4 5.0 %shard_map.303 = (bf16[192,1536]{1,0:T(8,128)(2,1)S(1)}, bf16[192,1536]{1,0:T(8,128)(2,1)S(1)}, bf16[192,1536]{1,0:T(8,128)(2,1)S(1)}, bf16[192,1536]{1,0:T(8,128)(2,1)S(1)}) custom-call(s32[5]{0:T(128)S(1)} %stack.23.refs_0_, bf16[1024,768]{1,0:T(8,128)(2,1)S(1)} %get-tuple-element.182.refs_1_, bf16[1024,3072]{1,0:T(8,128)(2,1)S(1)} %bitcast.22, ...), custom_call_target="tpu_custom_call" | custom-call | flops 92000002048 | tf_op jit(solution)/shard_map/pallas_call | solution.py:42
  109.1 3.2 %shard_map.305 = (bf16[400,3072]{1,0:T(8,128)(2,1)S(1)}, bf16[16,768]{1,0:T(8,128)(2,1)S(1)}) custom-call(s32[5]{0:T(128)S(1)} %stack.23.refs_0_, bf16[1024,768]{1,0:T(8,128)(2,1)S(1)} %bitcast.17, bf16[1024,2304]{1,0:T(8,128)(2,1)S(1)} %get-tuple-element.188.refs_2_.refs_0_, bf16[1024,768]{1,0:T(8,128)(2,1)S(1)} %get-tuple-element.201.refs_3_, ...), custom_call_target="tpu_custom_call" | custom-call | flops 92000002048 | tf_op jit(solution)/shard_map/pallas_call | solution.py:42
  112.4 2.4 %collective-permute-done.13.refs_2_ = bf16[192,768]{1,0:T(8,128)(2,1)S(1)} collective-permute-done((bf16[192,768]{1,0:T(8,128)(2,1)S(1)}, bf16[192,768]{1,0:T(8,128)(2,1)S(1)}, u32[]{:S(2)}, u32[]{:S(2)}) %collective-permute-start.13) | collective-permute-done | bytes 294944 | tf_op jit(solution)/shard_map/ppermute | solution.py:487
  122.2 4.5 %shard_map.308 = (bf16[208,1536]{1,0:T(8,128)(2,1)S(1)}, bf16[208,1536]{1,0:T(8,128)(2,1)S(1)}, bf16[192,1536]{1,0:T(8,128)(2,1)S(1)}, bf16[192,1536]{1,0:T(8,128)(2,1)S(1)}) custom-call(s32[5]{0:T(128)S(1)} %stack.23.refs_0_, bf16[1024,768]{1,0:T(8,128)(2,1)S(1)} %bitcast.18, bf16[1024,2304]{1,0:T(8,128)(2,1)S(1)} %get-tuple-element.188.refs_2_.refs_0_, ...), custom_call_target="tpu_custom_call" | custom-call | flops 92000002048 | tf_op jit(solution)/shard_map/pallas_call | solution.py:42
  133.5 5.6 %shard_map.311 = (bf16[1024,768]{1,0:T(8,128)(2,1)}, f32[8,128]{1,0:T(8,128)S(1)}) custom-call(bf16[1024,2304]{1,0:T(8,128)(2,1)S(1)} %get-tuple-element.188.refs_2_.refs_0_, bf16[768,2304]{1,0:T(8,128)(2,1)S(1)} %copy-done, bf16[1024,768]{1,0:T(8,128)(2,1)S(1)} %get-tuple-element.189.refs_4_.refs_2_, bf16[192,768]{1,0:T(8,128)(2,1)S(1)} %shard_map.310.refs_3_.refs_1_), custom_call_target="tpu_custom_call" | custom-call | flops 92000002048 | tf_op jit(solution)/shard_map/pallas_call | solution.py:42
  144.1 8.6 %collective-permute-done.25.refs_2_ = bf16[48,3072]{1,0:T(8,128)(2,1)S(1)} collective-permute-done((bf16[48,3072]{1,0:T(8,128)(2,1)S(1)}, bf16[48,3072]{1,0:T(8,128)(2,1)S(1)}, u32[]{:S(2)}, u32[]{:S(2)}) %collective-permute-start.25) | collective-permute-done | bytes 294944 | tf_op jit(solution)/shard_map/ppermute | solution.py:487
  158.6 6.6 %collective-permute-done.22.refs_2_ = bf16[112,1536]{1,0:T(8,128)(2,1)S(1)} collective-permute-done((bf16[112,1536]{1,0:T(8,128)(2,1)S(1)}, bf16[112,1536]{1,0:T(8,128)(2,1)S(1)}, u32[]{:S(2)}, u32[]{:S(2)}) %collective-permute-start.22) | collective-permute-done | bytes 344096 | tf_op jit(solution)/shard_map/ppermute | solution.py:487
  172.8 2.6 %collective-permute-start.34 = (bf16[768,384]{1,0:T(8,128)(2,1)S(1)}, bf16[768,384]{1,0:T(8,128)(2,1)S(1)}, u32[]{:S(2)}, u32[]{:S(2)}) collective-permute-start(bf16[768,384]{1,0:T(8,128)(2,1)S(1)} %get-tuple-element.232.refs_1_), channel_id=1, source_target_pairs={{0,1},{1,0},{2,3},{3,2},{4,5},{5,4},{6,7},{7,6},{8,9},{9,8},{10,11... | collective-permute-start | bytes 1769480 | tf_op jit(solution)/shard_map/ppermute | solution.py:487
  175.4 6.0 %collective-permute-done.26.refs_2_ = bf16[64,3072]{1,0:T(8,128)(2,1)S(1)} collective-permute-done((bf16[64,3072]{1,0:T(8,128)(2,1)S(1)}, bf16[64,3072]{1,0:T(8,128)(2,1)S(1)}, u32[]{:S(2)}, u32[]{:S(2)}) %collective-permute-start.26) | collective-permute-done | bytes 393248 | tf_op jit(solution)/shard_map/ppermute | solution.py:487
  182.1 2.9 %collective-permute-done.31.refs_2_ = bf16[48,3072]{1,0:T(8,128)(2,1)S(1)} collective-permute-done((bf16[48,3072]{1,0:T(8,128)(2,1)S(1)}, bf16[48,3072]{1,0:T(8,128)(2,1)S(1)}, u32[]{:S(2)}, u32[]{:S(2)}) %collective-permute-start.31) | collective-permute-done | bytes 294944 | tf_op jit(solution)/shard_map/ppermute | solution.py:487
  185.6 2.6 %collective-permute-start.32 = (bf16[96,1536]{1,0:T(8,128)(2,1)S(1)}, bf16[96,1536]{1,0:T(8,128)(2,1)S(1)}, u32[]{:S(2)}, u32[]{:S(2)}) collective-permute-start(bf16[96,1536]{1,0:T(8,128)(2,1)S(1)} %get-tuple-element.230.refs_1_), channel_id=1, source_target_pairs={{0,2},{1,3},{2,0},{3,1},{4,6},{5,7},{6,4},{7,5},{8,10},{9,11},{10,... | collective-permute-start | bytes 884744 | tf_op jit(solution)/shard_map/ppermute | solution.py:487
  189.0 2.8 %shard_map.321 = (f32[3072,768]{1,0:T(8,128)}, f32[8,128]{1,0:T(8,128)S(1)}) custom-call(s32[5]{0:T(128)S(1)} %stack.23.refs_0_, bf16[1536,768]{1,0:T(8,128)(2,1)S(1)} %shard_map.320.refs_1_.refs_2_, bf16[1536,768]{1,0:T(8,128)(2,1)S(1)} %shard_map.320.refs_1_.refs_2_), custom_call_target="tpu_custom_call" | custom-call | flops 23000000512 | tf_op jit(solution)/shard_map/pallas_call | solution.py:42
  196.8 2.8 %shard_map.324 = (f32[3072,768]{1,0:T(8,128)}, f32[8,128]{1,0:T(8,128)S(1)}) custom-call(s32[5]{0:T(128)S(1)} %stack.23.refs_0_, bf16[1536,768]{1,0:T(8,128)(2,1)S(1)} %collective-permute-done.37.refs_1_, f32[3072,768]{1,0:T(8,128)} %get-tuple-element.235.refs_2_, bf16[64,3072]{1,0:T(8,128)(2,1)S(1)} %shard_map.323.refs_3_.refs_1_), custom_call_target="tpu_custom_call", output_to_operand_aliasing={{0}: (2, {})} | custom-call | flops 23000000512 | tf_op jit(solution)/shard_map/pallas_call | solution.py:42
  199.6 6.9 %collective-permute-done.36.refs_2_ = bf16[64,3072]{1,0:T(8,128)(2,1)S(1)} collective-permute-done((bf16[64,3072]{1,0:T(8,128)(2,1)S(1)}, bf16[64,3072]{1,0:T(8,128)(2,1)S(1)}, u32[]{:S(2)}, u32[]{:S(2)}) %collective-permute-start.36) | collective-permute-done | bytes 393248 | tf_op jit(solution)/shard_map/ppermute | solution.py:487
  212.4 2.8 %shard_map.327 = (f32[768,3072]{1,0:T(8,128)}, f32[8,128]{1,0:T(8,128)S(1)}) custom-call(s32[5]{0:T(128)S(1)} %stack.23.refs_0_, bf16[384,3072]{1,0:T(8,128)(2,1)S(1)} %shard_map.326.refs_1_.refs_2_, bf16[384,3072]{1,0:T(8,128)(2,1)S(1)} %shard_map.326.refs_1_.refs_2_), custom_call_target="tpu_custom_call" | custom-call | flops 23000000512 | tf_op jit(solution)/shard_map/pallas_call | solution.py:42
  217.7 2.8 %shard_map.329 = (f32[768,3072]{1,0:T(8,128)}, f32[8,128]{1,0:T(8,128)S(1)}) custom-call(s32[5]{0:T(128)S(1)} %stack.23.refs_0_, bf16[384,3072]{1,0:T(8,128)(2,1)S(1)} %collective-permute-done.44.refs_1_, f32[768,3072]{1,0:T(8,128)} %get-tuple-element.243.refs_2_, bf16[192,1536]{1,0:T(8,128)(2,1)S(1)} %get-tuple-element.242.refs_3_), custom_call_target="tpu_custom_call", output_to_operand_aliasing={{0}: (2, {})} | custom-call | flops 23000000512 | tf_op jit(solution)/shard_map/pallas_call | solution.py:42
  220.6 11.1 %collective-permute-done.42.refs_2_ = bf16[192,1536]{1,0:T(8,128)(2,1)S(1)} collective-permute-done((bf16[192,1536]{1,0:T(8,128)(2,1)S(1)}, bf16[192,1536]{1,0:T(8,128)(2,1)S(1)}, u32[]{:S(2)}, u32[]{:S(2)}) %collective-permute-start.42) | collective-permute-done | bytes 589856 | tf_op jit(solution)/shard_map/ppermute | solution.py:487
  232.8 2.8 %shard_map.331 = (f32[768,2304]{1,0:T(8,128)}, f32[768,768]{1,0:T(8,128)}, f32[8,128]{1,0:T(8,128)S(1)}) custom-call(s32[5]{0:T(128)S(1)} %stack.23.refs_0_, bf16[384,3072]{1,0:T(8,128)(2,1)S(1)} %shard_map.330.refs_1_.refs_2_, bf16[384,3072]{1,0:T(8,128)(2,1)S(1)} %shard_map.330.refs_1_.refs_2_), custom_call_target="tpu_custom_call" | custom-call | flops 23000000512 | tf_op jit(solution)/shard_map/pallas_call | solution.py:42
  237.3 3.4 %shard_map.332 = (f32[768,2304]{1,0:T(8,128)}, f32[768,768]{1,0:T(8,128)}, f32[8,128]{1,0:T(8,128)}) custom-call(s32[5]{0:T(128)S(1)} %stack.23.refs_0_, bf16[384,3072]{1,0:T(8,128)(2,1)S(1)} %collective-permute-done.45.refs_1_, f32[768,2304]{1,0:T(8,128)} %get-tuple-element.245.refs_2_, ...), custom_call_target="tpu_custom_call", output_to_operand_aliasing={{0}: (2, {}), {1}: (3, {})} | custom-call | flops 23000000512 | tf_op jit(solution)/shard_map/pallas_call | solution.py:42
  (129 shorter events, 69.7 us)
Async XLA Ops:
  24.0 10.4 %collective-permute-start.2 = (bf16[16,768]{1,0:T(8,128)(2,1)S(1)}, bf16[16,768]{1,0:T(8,128)(2,1)S(1)}, u32[]{:S(2)}, u32[]{:S(2)}) collective-permute-start(bf16[16,768]{1,0:T(8,128)(2,1)S(1)} %get-tuple-element.156.refs_1_), channel_id=1, source_target_pairs={{0,3},{1,2},{2,1},{3,0},{4,7},{5,6},{6,5},{7,4},{8,11},{9,10},{10,... | collective-permute-start | bytes 73736 | tf_op jit(solution)/shard_map/ppermute | solution.py:487
  34.9 11.1 %collective-permute-start.5 = (bf16[64,768]{1,0:T(8,128)(2,1)S(1)}, bf16[64,768]{1,0:T(8,128)(2,1)S(1)}, u32[]{:S(2)}, u32[]{:S(2)}) collective-permute-start(bf16[64,768]{1,0:T(8,128)(2,1)S(1)} %shard_map.291.refs_14_.refs_1_), channel_id=1, source_target_pairs={{0,12},{1,13},{2,14},{3,15},{4,8},{5,9},{6,10},{7,11},{8,4},{9,5},... | collective-permute-start | bytes 294920 | tf_op jit(solution)/shard_map/ppermute | solution.py:487
  70.1 28.3 %collective-permute-start.12 = (bf16[384,3072]{1,0:T(8,128)(2,1)}, bf16[384,3072]{1,0:T(8,128)(2,1)}, u32[]{:S(2)}, u32[]{:S(2)}) collective-permute-start(bf16[384,3072]{1,0:T(8,128)(2,1)} %shard_map.298.refs_4_), channel_id=1, source_target_pairs={{0,16},{16,0},{1,17},{17,1},{2,18},{18,2},{3,19},{19,3},{4,20},{20... | collective-permute-start | bytes 7077896 | tf_op jit(solution)/shard_map/ppermute | solution.py:487
  75.8 19.9 %collective-permute-start.8 = (bf16[768,384]{1,0:T(8,128)(2,1)}, bf16[768,384]{1,0:T(8,128)(2,1)}, u32[]{:S(2)}, u32[]{:S(2)}) collective-permute-start(bf16[768,384]{1,0:T(8,128)(2,1)} %get-tuple-element.191), channel_id=1, source_target_pairs={{0,1},{1,0},{2,3},{3,2},{4,5},{5,4},{6,7},{7,6},{8,9},{9,8},{10,11... | collective-permute-start | bytes 1769480 | tf_op jit(solution)/shard_map/ppermute | solution.py:487
  77.3 18.4 %collective-permute-start.9 = (bf16[768,384]{1,0:T(8,128)(2,1)}, bf16[768,384]{1,0:T(8,128)(2,1)}, u32[]{:S(2)}, u32[]{:S(2)}) collective-permute-start(bf16[768,384]{1,0:T(8,128)(2,1)} %get-tuple-element.192), channel_id=1, source_target_pairs={{0,2},{1,3},{2,0},{3,1},{4,6},{5,7},{6,4},{7,5},{8,10},{9,11},{10,... | collective-permute-start | bytes 1769480 | tf_op jit(solution)/shard_map/ppermute | solution.py:487
  97.3 9.2 %collective-permute-start.10 = (bf16[384,384]{1,0:T(8,128)(2,1)S(1)}, bf16[384,384]{1,0:T(8,128)(2,1)S(1)}, u32[]{:S(2)}, u32[]{:S(2)}) collective-permute-start(bf16[384,384]{1,0:T(8,128)(2,1)S(1)} %get-tuple-element.195), channel_id=1, source_target_pairs={{0,2},{1,3},{2,0},{3,1},{4,6},{5,7},{6,4},{7,5},{8,10},{9,11},{10,... | collective-permute-start | bytes 884744 | tf_op jit(solution)/shard_map/ppermute | solution.py:487
  97.8 9.5 %collective-permute-start.11 = (bf16[384,384]{1,0:T(8,128)(2,1)S(1)}, bf16[384,384]{1,0:T(8,128)(2,1)S(1)}, u32[]{:S(2)}, u32[]{:S(2)}) collective-permute-start(bf16[384,384]{1,0:T(8,128)(2,1)S(1)} %get-tuple-element.197), channel_id=1, source_target_pairs={{0,1},{1,0},{2,3},{3,2},{4,5},{5,4},{6,7},{7,6},{8,9},{9,8},{10,11... | collective-permute-start | bytes 884744 | tf_op jit(solution)/shard_map/ppermute | solution.py:487
  103.3 15.7 %collective-permute-start.15 = (bf16[192,1536]{1,0:T(8,128)(2,1)S(1)}, bf16[192,1536]{1,0:T(8,128)(2,1)S(1)}, u32[]{:S(2)}, u32[]{:S(2)}) collective-permute-start(bf16[192,1536]{1,0:T(8,128)(2,1)S(1)} %get-tuple-element.206), channel_id=1, source_target_pairs={{0,1},{1,0},{2,3},{3,2},{4,5},{5,4},{6,7},{7,6},{8,9},{9,8},{10,11... | collective-permute-start | bytes 1769480 | tf_op jit(solution)/shard_map/ppermute | solution.py:487
  104.9 14.3 %collective-permute-start.16 = (bf16[192,1536]{1,0:T(8,128)(2,1)S(1)}, bf16[192,1536]{1,0:T(8,128)(2,1)S(1)}, u32[]{:S(2)}, u32[]{:S(2)}) collective-permute-start(bf16[192,1536]{1,0:T(8,128)(2,1)S(1)} %get-tuple-element.207), channel_id=1, source_target_pairs={{0,2},{1,3},{2,0},{3,1},{4,6},{5,7},{6,4},{7,5},{8,10},{9,11},{10,... | collective-permute-start | bytes 1769480 | tf_op jit(solution)/shard_map/ppermute | solution.py:487
  112.4 9.8 %collective-permute-start.19 = (bf16[400,3072]{1,0:T(8,128)(2,1)S(1)}, bf16[400,3072]{1,0:T(8,128)(2,1)S(1)}, u32[]{:S(2)}, u32[]{:S(2)}) collective-permute-start(bf16[400,3072]{1,0:T(8,128)(2,1)S(1)} %get-tuple-element.212), channel_id=1, source_target_pairs={{0,16},{16,0},{1,17},{17,1},{2,18},{18,2},{3,19},{19,3},{4,20},{20... | collective-permute-start | bytes 7372808 | tf_op jit(solution)/shard_map/ppermute | solution.py:487
  115.5 15.9 %collective-permute-start.14 = (bf16[192,768]{1,0:T(8,128)(2,1)S(1)}, bf16[192,768]{1,0:T(8,128)(2,1)S(1)}, u32[]{:S(2)}, u32[]{:S(2)}) collective-permute-start(bf16[192,768]{1,0:T(8,128)(2,1)S(1)} %shard_map.306.refs_5_.refs_1_), channel_id=1, source_target_pairs={{0,8},{1,9},{2,10},{3,11},{4,12},{5,13},{6,14},{7,15},{8,0},{9,1},... | collective-permute-start | bytes 884744 | tf_op jit(solution)/shard_map/ppermute | solution.py:487
  120.1 8.7 %collective-permute-start.17 = (bf16[96,1536]{1,0:T(8,128)(2,1)S(1)}, bf16[96,1536]{1,0:T(8,128)(2,1)S(1)}, u32[]{:S(2)}, u32[]{:S(2)}) collective-permute-start(bf16[96,1536]{1,0:T(8,128)(2,1)S(1)} %get-tuple-element.209), channel_id=1, source_target_pairs={{0,2},{1,3},{2,0},{3,1},{4,6},{5,7},{6,4},{7,5},{8,10},{9,11},{10,... | collective-permute-start | bytes 884744 | tf_op jit(solution)/shard_map/ppermute | solution.py:487
  121.6 9.1 %collective-permute-start.18 = (bf16[96,1536]{1,0:T(8,128)(2,1)S(1)}, bf16[96,1536]{1,0:T(8,128)(2,1)S(1)}, u32[]{:S(2)}, u32[]{:S(2)}) collective-permute-start(bf16[96,1536]{1,0:T(8,128)(2,1)S(1)} %get-tuple-element.211), channel_id=1, source_target_pairs={{0,1},{1,0},{2,3},{3,2},{4,5},{5,4},{6,7},{7,6},{8,9},{9,8},{10,11... | collective-permute-start | bytes 884744 | tf_op jit(solution)/shard_map/ppermute | solution.py:487
  126.7 14.5 %collective-permute-start.21 = (bf16[192,1536]{1,0:T(8,128)(2,1)S(1)}, bf16[192,1536]{1,0:T(8,128)(2,1)S(1)}, u32[]{:S(2)}, u32[]{:S(2)}) collective-permute-start(bf16[192,1536]{1,0:T(8,128)(2,1)S(1)} %get-tuple-element.218), channel_id=1, source_target_pairs={{0,2},{1,3},{2,0},{3,1},{4,6},{5,7},{6,4},{7,5},{8,10},{9,11},{10,... | collective-permute-start | bytes 1769480 | tf_op jit(solution)/shard_map/ppermute | solution.py:487
  127.2 15.7 %collective-permute-start.20 = (bf16[208,1536]{1,0:T(8,128)(2,1)S(1)}, bf16[208,1536]{1,0:T(8,128)(2,1)S(1)}, u32[]{:S(2)}, u32[]{:S(2)}) collective-permute-start(bf16[208,1536]{1,0:T(8,128)(2,1)S(1)} %get-tuple-element.217), channel_id=1, source_target_pairs={{0,1},{1,0},{2,3},{3,2},{4,5},{5,4},{6,7},{7,6},{8,9},{9,8},{10,11... | collective-permute-start | bytes 1916936 | tf_op jit(solution)/shard_map/ppermute | solution.py:487
  139.1 16.7 %collective-permute-start.24 = (bf16[192,768]{1,0:T(8,128)(2,1)S(1)}, bf16[192,768]{1,0:T(8,128)(2,1)S(1)}, u32[]{:S(2)}, u32[]{:S(2)}) collective-permute-start(bf16[192,768]{1,0:T(8,128)(2,1)S(1)} %shard_map.310.refs_3_.refs_1_), channel_id=1, source_target_pairs={{0,4},{1,5},{2,6},{3,7},{4,0},{5,1},{6,2},{7,3},{8,12},{9,13},{10,... | collective-permute-start | bytes 884744 | tf_op jit(solution)/shard_map/ppermute | solution.py:487
  140.1 12.6 %collective-permute-start.25 = (bf16[48,3072]{1,0:T(8,128)(2,1)S(1)}, bf16[48,3072]{1,0:T(8,128)(2,1)S(1)}, u32[]{:S(2)}, u32[]{:S(2)}) collective-permute-start(bf16[48,3072]{1,0:T(8,128)(2,1)S(1)} %get-tuple-element.224), channel_id=1, source_target_pairs={{0,4},{1,5},{2,6},{3,7},{4,0},{5,1},{6,2},{7,3},{8,12},{9,13},{10,... | collective-permute-start | bytes 884744 | tf_op jit(solution)/shard_map/ppermute | solution.py:487
  143.8 14.8 %collective-permute-start.23 = (bf16[96,1536]{1,0:T(8,128)(2,1)S(1)}, bf16[96,1536]{1,0:T(8,128)(2,1)S(1)}, u32[]{:S(2)}, u32[]{:S(2)}) collective-permute-start(bf16[96,1536]{1,0:T(8,128)(2,1)S(1)} %get-tuple-element.223), channel_id=1, source_target_pairs={{0,1},{1,0},{2,3},{3,2},{4,5},{5,4},{6,7},{7,6},{8,9},{9,8},{10,11... | collective-permute-start | bytes 884744 | tf_op jit(solution)/shard_map/ppermute | solution.py:487
  153.3 17.7 %collective-permute-start.27 = (bf16[48,3072]{1,0:T(8,128)(2,1)S(1)}, bf16[48,3072]{1,0:T(8,128)(2,1)S(1)}, u32[]{:S(2)}, u32[]{:S(2)}) collective-permute-start(bf16[48,3072]{1,0:T(8,128)(2,1)S(1)} %shard_map.313.refs_3_.refs_1_), channel_id=1, source_target_pairs={{0,8},{1,9},{2,10},{3,11},{4,12},{5,13},{6,14},{7,15},{8,0},{9,1},... | collective-permute-start | bytes 884744 | tf_op jit(solution)/shard_map/ppermute | solution.py:487
  154.2 11.0 %collective-permute-start.22 = (bf16[112,1536]{1,0:T(8,128)(2,1)S(1)}, bf16[112,1536]{1,0:T(8,128)(2,1)S(1)}, u32[]{:S(2)}, u32[]{:S(2)}) collective-permute-start(bf16[112,1536]{1,0:T(8,128)(2,1)S(1)} %get-tuple-element.221), channel_id=1, source_target_pairs={{0,2},{1,3},{2,0},{3,1},{4,6},{5,7},{6,4},{7,5},{8,10},{9,11},{10,... | collective-permute-start | bytes 1032200 | tf_op jit(solution)/shard_map/ppermute | solution.py:487
  156.4 12.2 %collective-permute-start.28 = (bf16[384,384]{1,0:T(8,128)(2,1)S(1)}, bf16[384,384]{1,0:T(8,128)(2,1)S(1)}, u32[]{:S(2)}, u32[]{:S(2)}) collective-permute-start(bf16[384,384]{1,0:T(8,128)(2,1)S(1)} %get-tuple-element.228.refs_1_), channel_id=1, source_target_pairs={{0,2},{1,3},{2,0},{3,1},{4,6},{5,7},{6,4},{7,5},{8,10},{9,11},{10,... | collective-permute-start | bytes 884744 | tf_op jit(solution)/shard_map/ppermute | solution.py:487
  156.9 11.6 %collective-permute-start.29 = (bf16[384,384]{1,0:T(8,128)(2,1)S(1)}, bf16[384,384]{1,0:T(8,128)(2,1)S(1)}, u32[]{:S(2)}, u32[]{:S(2)}) collective-permute-start(bf16[384,384]{1,0:T(8,128)(2,1)S(1)} %get-tuple-element.225.refs_5_.refs_3_), channel_id=1, source_target_pairs={{0,1},{1,0},{2,3},{3,2},{4,5},{5,4},{6,7},{7,6},{8,9},{9,8},{10,11... | collective-permute-start | bytes 884744 | tf_op jit(solution)/shard_map/ppermute | solution.py:487
  165.9 15.5 %collective-permute-start.26 = (bf16[64,3072]{1,0:T(8,128)(2,1)S(1)}, bf16[64,3072]{1,0:T(8,128)(2,1)S(1)}, u32[]{:S(2)}, u32[]{:S(2)}) collective-permute-start(bf16[64,3072]{1,0:T(8,128)(2,1)S(1)} %get-tuple-element.227), channel_id=1, source_target_pairs={{0,4},{1,5},{2,6},{3,7},{4,0},{5,1},{6,2},{7,3},{8,12},{9,13},{10,... | collective-permute-start | bytes 1179656 | tf_op jit(solution)/shard_map/ppermute | solution.py:487
  169.2 19.0 %collective-permute-start.35 = (bf16[768,384]{1,0:T(8,128)(2,1)S(1)}, bf16[768,384]{1,0:T(8,128)(2,1)S(1)}, u32[]{:S(2)}, u32[]{:S(2)}) collective-permute-start(bf16[768,384]{1,0:T(8,128)(2,1)S(1)} %get-tuple-element.229.refs_3_), channel_id=1, source_target_pairs={{0,2},{1,3},{2,0},{3,1},{4,6},{5,7},{6,4},{7,5},{8,10},{9,11},{10,... | collective-permute-start | bytes 1769480 | tf_op jit(solution)/shard_map/ppermute | solution.py:487
  171.6 13.3 %collective-permute-start.31 = (bf16[48,3072]{1,0:T(8,128)(2,1)S(1)}, bf16[48,3072]{1,0:T(8,128)(2,1)S(1)}, u32[]{:S(2)}, u32[]{:S(2)}) collective-permute-start(bf16[48,3072]{1,0:T(8,128)(2,1)S(1)} %shard_map.317.refs_3_.refs_1_), channel_id=1, source_target_pairs={{0,4},{1,5},{2,6},{3,7},{4,0},{5,1},{6,2},{7,3},{8,12},{9,13},{10,... | collective-permute-start | bytes 884744 | tf_op jit(solution)/shard_map/ppermute | solution.py:487
  172.8 15.4 %collective-permute-start.34 = (bf16[768,384]{1,0:T(8,128)(2,1)S(1)}, bf16[768,384]{1,0:T(8,128)(2,1)S(1)}, u32[]{:S(2)}, u32[]{:S(2)}) collective-permute-start(bf16[768,384]{1,0:T(8,128)(2,1)S(1)} %get-tuple-element.232.refs_1_), channel_id=1, source_target_pairs={{0,1},{1,0},{2,3},{3,2},{4,5},{5,4},{6,7},{7,6},{8,9},{9,8},{10,11... | collective-permute-start | bytes 1769480 | tf_op jit(solution)/shard_map/ppermute | solution.py:487
  182.0 13.8 %collective-permute-start.30 = (bf16[64,3072]{1,0:T(8,128)(2,1)S(1)}, bf16[64,3072]{1,0:T(8,128)(2,1)S(1)}, u32[]{:S(2)}, u32[]{:S(2)}) collective-permute-start(bf16[64,3072]{1,0:T(8,128)(2,1)S(1)} %shard_map.318.refs_3_.refs_1_), channel_id=1, source_target_pairs={{0,8},{1,9},{2,10},{3,11},{4,12},{5,13},{6,14},{7,15},{8,0},{9,1},... | collective-permute-start | bytes 1179656 | tf_op jit(solution)/shard_map/ppermute | solution.py:487
  195.5 14.6 %collective-permute-start.40 = (bf16[192,1536]{1,0:T(8,128)(2,1)S(1)}, bf16[192,1536]{1,0:T(8,128)(2,1)S(1)}, u32[]{:S(2)}, u32[]{:S(2)}) collective-permute-start(bf16[192,1536]{1,0:T(8,128)(2,1)S(1)} %get-tuple-element.239.refs_1_), channel_id=1, source_target_pairs={{0,1},{1,0},{2,3},{3,2},{4,5},{5,4},{6,7},{7,6},{8,9},{9,8},{10,11... | collective-permute-start | bytes 1769480 | tf_op jit(solution)/shard_map/ppermute | solution.py:487
  195.6 16.0 %collective-permute-start.41 = (bf16[192,1536]{1,0:T(8,128)(2,1)S(1)}, bf16[192,1536]{1,0:T(8,128)(2,1)S(1)}, u32[]{:S(2)}, u32[]{:S(2)}) collective-permute-start(bf16[192,1536]{1,0:T(8,128)(2,1)S(1)} %get-tuple-element.234.refs_3_), channel_id=1, source_target_pairs={{0,2},{1,3},{2,0},{3,1},{4,6},{5,7},{6,4},{7,5},{8,10},{9,11},{10,... | collective-permute-start | bytes 1769480 | tf_op jit(solution)/shard_map/ppermute | solution.py:487
  196.5 10.1 %collective-permute-start.36 = (bf16[64,3072]{1,0:T(8,128)(2,1)S(1)}, bf16[64,3072]{1,0:T(8,128)(2,1)S(1)}, u32[]{:S(2)}, u32[]{:S(2)}) collective-permute-start(bf16[64,3072]{1,0:T(8,128)(2,1)S(1)} %shard_map.323.refs_3_.refs_1_), channel_id=1, source_target_pairs={{0,4},{1,5},{2,6},{3,7},{4,0},{5,1},{6,2},{7,3},{8,12},{9,13},{10,... | collective-permute-start | bytes 1179656 | tf_op jit(solution)/shard_map/ppermute | solution.py:487
  217.0 14.7 %collective-permute-start.42 = (bf16[192,1536]{1,0:T(8,128)(2,1)S(1)}, bf16[192,1536]{1,0:T(8,128)(2,1)S(1)}, u32[]{:S(2)}, u32[]{:S(2)}) collective-permute-start(bf16[192,1536]{1,0:T(8,128)(2,1)S(1)} %get-tuple-element.241.refs_1_), channel_id=1, source_target_pairs={{0,1},{1,0},{2,3},{3,2},{4,5},{5,4},{6,7},{7,6},{8,9},{9,8},{10,11... | collective-permute-start | bytes 1769480 | tf_op jit(solution)/shard_map/ppermute | solution.py:487
  217.5 14.5 %collective-permute-start.43 = (bf16[192,1536]{1,0:T(8,128)(2,1)S(1)}, bf16[192,1536]{1,0:T(8,128)(2,1)S(1)}, u32[]{:S(2)}, u32[]{:S(2)}) collective-permute-start(bf16[192,1536]{1,0:T(8,128)(2,1)S(1)} %get-tuple-element.242.refs_3_), channel_id=1, source_target_pairs={{0,2},{1,3},{2,0},{3,1},{4,6},{5,7},{6,4},{7,5},{8,10},{9,11},{10,... | collective-permute-start | bytes 1769480 | tf_op jit(solution)/shard_map/ppermute | solution.py:487
  (25 other events, 154.8 us)

commit v4 on v3

--- a/solution.py
+++ b/solution.py
@@ -46,7 +46,7 @@
         out_shape=[(pltpu.HBM if i in far_out or i in hand_out else pltpu.VMEM)(o.shape, o.dtype) for i, o in enumerate(outs)],
         scratch_shapes=list(scratch),
         input_output_aliases={first + k: v for k, v in (aliases or {}).items()},
-        cost_estimate=pl.CostEstimate(flops=cost * 2 * 10**8, bytes_accessed=0, transcendentals=0),
+        cost_estimate=pl.CostEstimate(flops=cost * 10**8, bytes_accessed=0, transcendentals=0),
         compiler_params=pltpu.CompilerParams(vmem_limit_bytes=limit * MIB),
     )(*([] if bits is None else [bits]), *ins, *after)
 
@@ -88,6 +88,20 @@
 
 def join_heads(rows, first):
     return jnp.where(first, rows[:SEQ], rows[SEQ:])
+
+
+def heads_product(left, right, cols, first):
+    zero = jnp.zeros_like(right[0][:, cols[0]])
+    out = ([], [])
+    for c in cols:
+        both = jnp.concatenate([left[0][:, c], left[1][:, c]], axis=0)
+        apart = jnp.concatenate(
+            [jnp.concatenate([right[0][:, c], zero], axis=1), jnp.concatenate([zero, right[1][:, c]], axis=1)], axis=0
+        )
+        rows = trans_left(both, apart)
+        for i in range(2):
+            out[i].append(join_heads(rows[:, i * 128 : (i + 1) * 128], first))
+    return [jnp.concatenate(o, axis=1) for o in out]
 
 
 def attention_forward(bits, x, w_qkv, b_qv, w_out, b_out, gain, bias, later):
@@ -105,45 +119,47 @@
         x_ref, wq_ref, bqv_ref, wo_ref, bo_ref, g_ref, b_ref = near
         pairs_of = zip(far + far_later, near + near_later)
         copies = [pltpu.make_async_copy(f, near_f, sems.at[i]) for i, (f, near_f) in enumerate(pairs_of)]
-        for copy in copies:
+        for copy in copies[:3]:
             copy.start()
         for copy in copies[:3]:
             copy.wait()
+        for copy in copies[3:]:
+            copy.start()
         first = lax.broadcasted_iota(jnp.int32, (SEQ, 128), 1) < HEAD_DIM
         cols = [slice(p * 128, (p + 1) * 128) for p in range(pairs)]
 
+        for part in range(3):
+            c = slice(part * width, (part + 1) * width)
+            value = mat_mul(x_ref[...], wq_ref[:, c])
+            if part != 1:
+                value = value + row_of(bqv_ref, (part // 2) * width, width)
+            proj_ref[:, c] = value.astype(low)
+
         @pl.loop(0, tokens // rows)
         def _(step):
-            base = pl.multiple_of(step * rows, rows)
-            block = pl.ds(base, rows)
-            x_in = x_ref[block, :]
-            for part in range(3):
-                c = slice(part * width, (part + 1) * width)
-                value = mat_mul(x_in, wq_ref[:, c])
-                if part != 1:
-                    value = value + row_of(bqv_ref, (part // 2) * width, width)
-                proj_ref[block, c] = value.astype(low)
-            for sent in range(4):
-                r = pl.ds(pl.multiple_of(base + sent * SEQ, SEQ), SEQ)
-                q = proj_ref[r, :width]
-                k = proj_ref[r, width : 2 * width]
-                v = proj_ref[r, 2 * width :]
-                scores = (
-                    jnp.concatenate([trans_right(k[:, c], split_heads(q[:, c], first)) for c in cols], axis=1) * scale
-                )
-                e = jnp.exp(scores - jnp.max(scores, axis=0, keepdims=True))
-                probs = (e * (1.0 / jnp.sum(e, axis=0, keepdims=True))).astype(low)
-                prob_ref[r, :] = probs
-                ctx_ref[r, :] = jnp.concatenate(
-                    [join_heads(trans_left(probs[:, c], v[:, c]), first) for c in cols], axis=1
-                ).astype(low)
-
-            @pl.when(step == 0)
-            def _():
-                for copy in copies[3:7]:
-                    copy.wait()
-
-            h = x_in.astype(wide) + mat_mul(ctx_ref[block, :], wo_ref[...]) + row_of(bo_ref)
+            base = step * rows
+            for two in range(2):
+                at = [pl.ds(pl.multiple_of(base + (2 * two + i) * SEQ, SEQ), SEQ) for i in range(2)]
+                probs = []
+                for r in at:
+                    q = proj_ref[r, :width]
+                    k = proj_ref[r, width : 2 * width]
+                    scores = (
+                        jnp.concatenate([trans_right(k[:, c], split_heads(q[:, c], first)) for c in cols], axis=1) * scale
+                    )
+                    e = jnp.exp(scores - jnp.max(scores, axis=0, keepdims=True))
+                    probs.append((e * (1.0 / jnp.sum(e, axis=0, keepdims=True))).astype(low))
+                    prob_ref[r, :] = probs[-1]
+                values = [proj_ref[r, 2 * width :] for r in at]
+                for r, context in zip(at, heads_product(probs, values, cols, first)):
+                    ctx_ref[r, :] = context.astype(low)
+
+        for copy in copies[3:7]:
+            copy.wait()
+
+        for start in range(0, tokens, tokens // 2):
+            block = slice(start, start + tokens // 2)
+            h = x_ref[block, :].astype(wide) + mat_mul(ctx_ref[block, :], wo_ref[...]) + row_of(bo_ref)
             normed, inv = normalize(h)
             hidden = normed * row_of(g_ref) + row_of(b_ref)
             hid_ref[block, :] = hidden
@@ -173,7 +189,7 @@
     )
 
 
-def ffn_forward_rows(hidden, wi_ref, bi_ref, wd_ref, bd_ref, store_act, store_slope):
+def ffn_forward_rows(hidden, wi_ref, bi_ref, wd_ref, bd_ref, store_act, store_gate_in):
     h_low = hidden.astype(low)
     total = hidden + row_of(bd_ref)
     for c in range(0, wi_ref.shape[1], CHUNK):
@@ -181,19 +197,21 @@
         phi = 0.5 + 0.5 * lax.erf(u * root_half)
         act = (u * phi).astype(low)
         store_act(c, act)
-        store_slope(c, (phi + u * jnp.exp(-0.5 * u * u) * gauss_norm).astype(low))
+        store_gate_in(c, u.astype(low), phi.astype(low))
         total = total + mat_mul(act, wd_ref[c : c + CHUNK, :])
     return normalize(total)
 
 
-def ffn_backward_rows(grad_block, normed, inv, gain, wd_ref, slope_of, store_gate, small_ref, bin_ref):
+def ffn_backward_rows(grad_block, normed, inv, gain, wd_ref, gate_in, store_gate, small_ref, bin_ref):
     grad_two = norm_input_grad(grad_block * gain, normed, inv)
     small_ref[0:1, :] += jnp.sum(grad_block * normed, axis=0, keepdims=True)
     small_ref[1:2, :] += jnp.sum(grad_block, axis=0, keepdims=True)
     small_ref[2:3, :] += jnp.sum(grad_two, axis=0, keepdims=True)
     grad_low = grad_two.astype(low)
     for c in range(0, wd_ref.shape[0], CHUNK):
-        gate = trans_right(grad_low, wd_ref[c : c + CHUNK, :]) * slope_of(c).astype(wide)
+        u, phi = gate_in(c)
+        slope = phi + u * jnp.exp(u * u * low(-0.5)) * low(gauss_norm)
+        gate = trans_right(grad_low, wd_ref[c : c + CHUNK, :]) * slope.astype(wide)
         bin_ref[:, c : c + CHUNK] += jnp.sum(gate, axis=0, keepdims=True)
         store_gate(c, gate.astype(low))
     return grad_low
@@ -208,22 +226,23 @@
     first = index == 0
     second = index == 1
 
-    def stores(act_ref, slope_ref):
+    def stores(act_ref, u_ref, phi_ref):
         def store_act(c, v):
             act_ref[:, at, c : c + CHUNK] = v.reshape(sents, GROUP, CHUNK)
 
-        def store_slope(c, v):
-            slope_ref[:, c : c + CHUNK] = v
-
-        return store_act, store_slope
-
-    def forward(h_ref, wi_ref, bi_ref, wd_ref, bd_ref, act_ref, slope_ref):
+        def store_gate_in(c, u, phi):
+            u_ref[:, c : c + CHUNK] = u
+            phi_ref[:, c : c + CHUNK] = phi
+
+        return store_act, store_gate_in
+
+    def forward(h_ref, wi_ref, bi_ref, wd_ref, bd_ref, act_ref, u_ref, phi_ref):
         return ffn_forward_rows(
-            h_ref[:, at, :].reshape(rows, width), wi_ref, bi_ref, wd_ref, bd_ref, *stores(act_ref, slope_ref)
+            h_ref[:, at, :].reshape(rows, width), wi_ref, bi_ref, wd_ref, bd_ref, *stores(act_ref, u_ref, phi_ref)
         )
 
-    def body_first(h_ref, wi_ref, bi_ref, wd_ref, bd_ref, g_ref, b_ref, enc_hbm, act_ref, slope_ref, n_ref, inv_ref, first_ref, enc_ref, sem):
-        normed, inv = forward(h_ref, wi_ref, bi_ref, wd_ref, bd_ref, act_ref, slope_ref)
+    def body_first(h_ref, wi_ref, bi_ref, wd_ref, bd_ref, g_ref, b_ref, enc_hbm, act_ref, u_ref, phi_ref, n_ref, inv_ref, first_ref, enc_ref, sem):
+        normed, inv = forward(h_ref, wi_ref, bi_ref, wd_ref, bd_ref, act_ref, u_ref, phi_ref)
         n_ref[...] = normed
         inv_ref[...] = inv
         block = (normed * row_of(g_ref) + row_of(b_ref)).reshape(sents, GROUP, width)
@@ -244,6 +263,7 @@
                 enc_shape,
                 act_shape,
                 struct((rows, ffn), low),
+                struct((rows, ffn), low),
                 struct((rows, width), wide),
                 struct((rows, 1), wide),
                 struct((sents, width), low),
@@ -257,21 +277,22 @@
         if not second:
             sin_ref, bin_in_ref = refs[:2]
             refs = refs[2:]
-        enc_hbm, act_ref, gate_ref, two_ref, small_ref, bin_ref, slope_ref, enc_ref, sem = refs
+        enc_hbm, act_ref, gate_ref, two_ref, small_ref, bin_ref, u_ref, phi_ref, enc_ref, sem = refs
         small_ref[...] = jnp.zeros_like(small_ref) if second else sin_ref[...]
         bin_ref[...] = jnp.zeros_like(bin_ref) if second else bin_in_ref[...]
 
         def store_gate(c, v):
             gate_ref[:, at, c : c + CHUNK] = v.reshape(sents, GROUP, CHUNK)
 
-        normed, inv = forward(h_ref, wi_ref, bi_ref, wd_ref, bd_ref, act_ref, slope_ref)
+        normed, inv = forward(h_ref, wi_ref, bi_ref, wd_ref, bd_ref, act_ref, u_ref, phi_ref)
         gain_row = row_of(g_ref)
         enc_ref[...] = (normed * gain_row + row_of(b_ref)).astype(low).reshape(sents, GROUP, width)
         copy = pltpu.make_async_copy(enc_ref, enc_hbm.at[:, pl.ds(index * GROUP, GROUP), :], sem)
         copy.start()
         grad_block = cot_ref[:, at, :].reshape(rows, width).astype(wide)
         got = ffn_backward_rows(
-            grad_block, normed, inv, gain_row, wd_ref, lambda c: slope_ref[:, c : c + CHUNK], store_gate, small_ref, bin_ref
+            grad_block, normed, inv, gain_row, wd_ref, lambda c: (u_ref[:, c : c + CHUNK], phi_ref[:, c : c + CHUNK]),
+            store_gate, small_ref, bin_ref,
         )
         two_ref[:, at, :] = got.reshape(sents, GROUP, width)
         copy.wait()
@@ -283,7 +304,7 @@
         body,
         [hidden, cot, w_in, b_in, w_down, b_down, gain, bias] + list(state),
         [enc_shape, act_shape, act_shape, enc_shape, struct((8, width), wide), struct((1, ffn), wide)],
-        scratch=[pltpu.VMEM((rows, ffn), low)] + enc_scratch,
+        scratch=[pltpu.VMEM((rows, ffn), low)] * 2 + enc_scratch,
         aliases=aliases,
         after=after,
         far=[8],
@@ -291,13 +312,13 @@
     )
 
 
-def ffn_first_back(cot, grad_first, normed, inv, slope, gain, w_down, gate, two, small, bin_sum):
+def ffn_first_back(cot, grad_first, normed, inv, gate_in, phi, gain, w_down, gate, two, small, bin_sum):
     sents, _, width = cot.shape
     ffn = w_down.shape[0]
     rows = sents * GROUP
     at = slice(0, GROUP)
 
-    def body(cot_ref, first_ref, n_ref, inv_ref, slope_ref, g_ref, wd_ref, sin_ref, bin_in_ref, _g, _t, gate_ref, two_ref, small_ref, bin_ref):
+    def body(cot_ref, first_ref, n_ref, inv_ref, u_ref, phi_ref, g_ref, wd_ref, sin_ref, bin_in_ref, _g, _t, gate_ref, two_ref, small_ref, bin_ref):
         small_ref[...] = sin_ref[...]
         bin_ref[...] = bin_in_ref[...]
         position = lax.broadcasted_iota(jnp.int32, (sents, GROUP, width), 1)
@@ -309,15 +330,15 @@
 
         got = ffn_backward_rows(
             grad_block.reshape(rows, width), n_ref[...], inv_ref[...], row_of(g_ref), wd_ref,
-            lambda c: slope_ref[:, c : c + CHUNK], store_gate, small_ref, bin_ref,
+            lambda c: (u_ref[:, c : c + CHUNK], phi_ref[:, c : c + CHUNK]), store_gate, small_ref, bin_ref,
         )
         two_ref[:, at, :] = got.reshape(sents, GROUP, width)
 
     return call(
         body,
-        [cot, grad_first, normed, inv, slope, gain, w_down, small, bin_sum, gate, two],
+        [cot, grad_first, normed, inv, gate_in, phi, gain, w_down, small, bin_sum, gate, two],
         [struct((sents, SEQ, ffn), low), struct((sents, SEQ, width), low), struct((8, width), wide), struct((1, ffn), wide)],
-        aliases={9: 0, 10: 1},
+        aliases={10: 0, 11: 1},
     )
 
 
@@ -340,45 +361,47 @@
         first = lax.broadcasted_iota(jnp.int32, (SEQ, 128), 1) < HEAD_DIM
         cols = [slice(p * 128, (p + 1) * 128) for p in range(pairs)]
 
+        block = slice(part * steps * rows, (part + 1) * steps * rows)
+        gain_row = row_of(g_ref)
+        grad_hidden = two_ref[block, :].astype(wide) + trans_right(gate_ref[block, :], wi_ref[...])
+        normed = (hid_ref[block, :] - row_of(b_ref)) * (1.0 / gain_row)
+        small_ref[0:1, :] += jnp.sum(grad_hidden * normed, axis=0, keepdims=True)
+        small_ref[1:2, :] += jnp.sum(grad_hidden, axis=0, keepdims=True)
+        grad_one = norm_input_grad(grad_hidden * gain_row, normed, inv_ref[block, :])
+        small_ref[2:3, :] += jnp.sum(grad_one, axis=0, keepdims=True)
+        one_ref[block, :] = grad_one.astype(low)
+        ctx_ref[...] = trans_right(one_ref[block, :], wo_ref[...]).astype(low)
+
         @pl.loop(0, steps)
         def _(step):
-            base = pl.multiple_of((step + part * steps) * rows, rows)
-            block = pl.ds(base, rows)
-            gain_row = row_of(g_ref)
-            grad_hidden = two_ref[block, :].astype(wide) + trans_right(gate_ref[block, :], wi_ref[...])
-            normed = (hid_ref[block, :] - row_of(b_ref)) * (1.0 / gain_row)
-            small_ref[0:1, :] += jnp.sum(grad_hidden * normed, axis=0, keepdims=True)
-            small_ref[1:2, :] += jnp.sum(grad_hidden, axis=0, keepdims=True)
-            grad_one = norm_input_grad(grad_hidden * gain_row, normed, inv_ref[block, :])
-            small_ref[2:3, :] += jnp.sum(grad_one, axis=0, keepdims=True)
-            one_low = grad_one.astype(low)
-            one_ref[block, :] = one_low
-            ctx_ref[...] = trans_right(one_low, wo_ref[...]).astype(low)
+            base = step * rows + part * steps * rows
             sum_q = jnp.zeros((1, width), wide)
             sum_v = jnp.zeros((1, width), wide)
-            for sent in range(4):
-                r = pl.ds(pl.multiple_of(base + sent * SEQ, SEQ), SEQ)
-                q_all = proj_ref[r, :width]
-                k = proj_ref[r, width : 2 * width]
-                v = proj_ref[r, 2 * width :]
-                d_all = ctx_ref[sent * SEQ : (sent + 1) * SEQ, :]
-                p_low = prob_ref[r, :]
-                q = [split_heads(q_all[:, c], first) for c in cols]
-                d = [split_heads(d_all[:, c], first) for c in cols]
-                p = p_low.astype(wide)
-                grad_p = jnp.concatenate([trans_right(v[:, c], dd) for c, dd in zip(cols, d)], axis=1)
-                grad_v = jnp.concatenate([mat_mul(p_low[:, c], dd) for c, dd in zip(cols, d)], axis=1)
-                gp = grad_p * p
-                grad_s = (gp - p * jnp.sum(gp, axis=0, keepdims=True)).astype(low)
-                grad_k = jnp.concatenate([mat_mul(grad_s[:, c], qq) for c, qq in zip(cols, q)], axis=1) * scale
-                grad_q = (
-                    jnp.concatenate([join_heads(trans_left(grad_s[:, c], k[:, c]), first) for c in cols], axis=1) * scale
-                )
-                sum_q += jnp.sum(grad_q, axis=0, keepdims=True)
-                sum_v += jnp.sum(grad_v, axis=0, keepdims=True)
-                gp_ref[r, :width] = grad_q.astype(low)
-                gp_ref[r, width : 2 * width] = grad_k.astype(low)
-                gp_ref[r, 2 * width :] = grad_v.astype(low)
+            for two in range(2):
+                at = [pl.ds(pl.multiple_of(base + (2 * two + i) * SEQ, SEQ), SEQ) for i in range(2)]
+                grads = []
+                for i, r in enumerate(at):
+                    q_all = proj_ref[r, :width]
+                    v = proj_ref[r, 2 * width :]
+                    d_all = ctx_ref[pl.ds(pl.multiple_of(step * rows + (2 * two + i) * SEQ, SEQ), SEQ), :]
+                    p_low = prob_ref[r, :]
+                    q = [split_heads(q_all[:, c], first) for c in cols]
+                    d = [split_heads(d_all[:, c], first) for c in cols]
+                    p = p_low.astype(wide)
+                    grad_p = jnp.concatenate([trans_right(v[:, c], dd) for c, dd in zip(cols, d)], axis=1)
+                    grad_v = jnp.concatenate([mat_mul(p_low[:, c], dd) for c, dd in zip(cols, d)], axis=1)
+                    gp = grad_p * p
+                    grad_s = (gp - p * jnp.sum(gp, axis=0, keepdims=True)).astype(low)
+                    grad_k = jnp.concatenate([mat_mul(grad_s[:, c], qq) for c, qq in zip(cols, q)], axis=1) * scale
+                    sum_v += jnp.sum(grad_v, axis=0, keepdims=True)
+                    gp_ref[r, width : 2 * width] = grad_k.astype(low)
+                    gp_ref[r, 2 * width :] = grad_v.astype(low)
+                    grads.append(grad_s)
+                keys = [proj_ref[r, width : 2 * width] for r in at]
+                for r, product in zip(at, heads_product(grads, keys, cols, first)):
+                    grad_q = product * scale
+                    sum_q += jnp.sum(grad_q, axis=0, keepdims=True)
+                    gp_ref[r, :width] = grad_q.astype(low)
             bqv_ref[0:1, :] += sum_q
             bqv_ref[1:2, :] += sum_v
 
@@ -386,7 +409,7 @@
         body,
         [two, gate, hidden, inv, proj, probs, w_in, w_out, gain, bias] + ([] if fresh else list(before)),
         [struct((tokens, width), low), struct((tokens, 3 * width), low), struct((8, width), wide), struct((8, width), wide)],
-        scratch=[pltpu.VMEM((rows, width), low)],
+        scratch=[pltpu.VMEM((rows * steps, width), low)],
         aliases=None if fresh else {10: 0, 11: 1},
         after=after,
     )
@@ -394,14 +417,13 @@
 
 def input_gradient(grad_proj, w_qkv, grad_one, after=()):
     tokens, width = grad_one.shape
-    rows = 4 * SEQ
+    rows = tokens // 2
 
     def body(gp_ref, w_ref, one_ref, out_ref, token):
         token[...] = jnp.zeros_like(token)
 
-        @pl.loop(0, tokens // rows)
-        def _(step):
-            block = pl.ds(pl.multiple_of(step * rows, rows), rows)
+        for start in range(0, tokens, rows):
+            block = slice(start, start + rows)
             out_ref[block, :] = (one_ref[block, :].astype(wide) + trans_right(gp_ref[block, :], w_ref[...])).astype(low)
 
     return call(
@@ -409,7 +431,7 @@
     )
 
 
-def pooler_gradients(flat, id_column, id_row, w_pool, b_pool):
+def pooler_gradients(flat, id_row, w_pool, b_pool):
     total = flat.shape[0] // 2
     pooled = jnp.tanh(mat_mul(flat, w_pool) + b_pool)
     inv_len = lax.rsqrt(jnp.sum(pooled * pooled, axis=-1, keepdims=True) + epsilon)
@@ -419,6 +441,7 @@
     square = (total, total)
     eye = (lax.broadcasted_iota(jnp.int32, square, 0) == lax.broadcasted_iota(jnp.int32, square, 1)).astype(wide)
     logits = score_scale * trans_right(zero, one) - margin_shift * eye
+    id_column = jnp.sum(jnp.where(eye > 0, id_row, 0), axis=1, keepdims=True)
     masked = jnp.where(id_column == id_row, logits, -jnp.inf)
 
     def soft(axis):
@@ -436,18 +459,18 @@
     return pre_low, trans_left(flat, pre_low), jnp.sum(grad_pre, axis=0, keepdims=True)
 
 
-def contrastive(own, got, bits, sents, id_column, id_row, w_pool, b_pool, after):
+def contrastive(own, got, bits, sents, ids, w_pool, b_pool, after):
     total, width = own.shape
     if total > 512:
         start = bits[CORE] * total + bits[PLACE] * sents
         flat = jnp.where(bits[CORE] == 0, jnp.concatenate([own, got]), jnp.concatenate([got, own]))
-        pre_low, grad_w, grad_b = pooler_gradients(flat, id_column, id_row, w_pool, b_pool.reshape(1, -1))
+        pre_low, grad_w, grad_b = pooler_gradients(flat, ids.reshape(1, -1), w_pool, b_pool.reshape(1, -1))
         return trans_right(lax.dynamic_slice_in_dim(pre_low, start, sents), w_pool), grad_w, grad_b.reshape(-1)
 
-    def body(b, own_ref, got_ref, col_ref, row_ref, w_ref, b_ref, first_ref, gw_ref, gb_ref, flat_ref, pre_ref):
+    def body(b, own_ref, got_ref, ids_ref, w_ref, b_ref, first_ref, gw_ref, gb_ref, flat_ref, pre_ref):
         flat_ref[pl.ds(pl.multiple_of(b[CORE] * total, total), total), :] = own_ref[...]
         flat_ref[pl.ds(pl.multiple_of((1 - b[CORE]) * total, total), total), :] = got_ref[...]
-        pre_low, grad_w, grad_b = pooler_gradients(flat_ref[...], col_ref[...], row_ref[...], w_ref[...], row_of(b_ref))
+        pre_low, grad_w, grad_b = pooler_gradients(flat_ref[...], row_of(ids_ref), w_ref[...], row_of(b_ref))
         pre_ref[...] = pre_low
         gw_ref[...] = grad_w
         gb_ref[...] = grad_b.reshape(-1)
@@ -455,7 +478,7 @@
 
     return call(
         body,
-        [own, got, id_column, id_row, w_pool, b_pool],
+        [own, got, ids, w_pool, b_pool],
         [struct((sents, width), wide), struct((width, width), wide), struct((width,), wide)],
         bits=bits,
         scratch=[pltpu.VMEM((2 * total, width), low)] * 2,
@@ -767,16 +790,16 @@
     stream, place_dp = lax.axis_index("stream"), lax.axis_index("dp")
     bits = jnp.stack([stream, place_dp & 1, (place_dp >> 1) & 1, (place_dp >> 2) & 1, place_dp]).astype(jnp.int32)
     later = [
-        w_in, w_down, seq_cotangent[0], w_pool, b_in, b_down, ln2_gain, ln2_bias, b_pool, pair_ids[:, None], pair_ids[None, :]
+        w_in, w_down, seq_cotangent[0], w_pool, b_in, b_down, ln2_gain, ln2_bias, b_pool, pair_ids
     ]
     proj, probs, context, hidden, hidden_low, inv_one, *later = attention_forward(
         bits, x, w_qkv, b_qv, w_out, b_out, ln1_gain, ln1_bias, later
     )
-    w_in, w_down, cotangent, w_pool, b_in, b_down, ln2_gain, ln2_bias, b_pool, id_column, id_row = later
+    w_in, w_down, cotangent, w_pool, b_in, b_down, ln2_gain, ln2_bias, b_pool, ids = later
     hid3 = hidden.reshape(sents, SEQ, width)
     cot3 = cotangent.reshape(sents, SEQ, width)
     upper = (w_in, b_in, w_down, b_down, ln2_gain, ln2_bias)
-    enc, act, slope, normed_two, inv_two, first_low = ffn_group(0, hid3, cot3, upper, ())
+    enc, act, gate_in, phi, normed_two, inv_two, first_low = ffn_group(0, hid3, cot3, upper, ())
     masks = [1 << i for i in range(dp.bit_length() - 1)]
     state = [enc, act]
     gathered = first_low
@@ -798,10 +821,10 @@
         order = [state[-1]]
     enc, act, gate, two, small_up, bin_sum = state
     grad_first, grad_w_pool, grad_b_pool = contrastive(
-        gathered, other, bits, sents, id_column, id_row, w_pool, b_pool, order
+        gathered, other, bits, sents, ids, w_pool, b_pool, order
     )
     gate, two, small_up, bin_sum = ffn_first_back(
-        cot3, grad_first, normed_two, inv_two, slope, ln2_gain, w_down, gate, two, small_up, bin_sum
+        cot3, grad_first, normed_two, inv_two, gate_in, phi, ln2_gain, w_down, gate, two, small_up, bin_sum
     )
     clock = Clock(small_up)
     act, gate, two = (v.reshape(tokens, -1) for v in (act, gate, two))

time: 244 us -> 253 us (1.037)
  Pallas kernels: 131 us -> 123 us
  waiting for transfers between devices: 60.5 us -> 68.3 us
  starting transfers between devices: 44.8 us -> 49.2 us
  local copies, waits for them, and re-layouts: 3.58 us -> 6.9 us
    ppermute x46, waiting for transfers between devices: 60.5 us -> 68.3 us  [exchange(): return lax.ppermute(a, axis, [(i, i ^ mask) for i in range(size)])]
    pallas_call x45, Pallas kernels: 131 us -> 123 us  [call(): pl.pallas_call(wrapped, in_specs=[SMEM] * first + [HBM if i in far else V...]
    unnamed x22 -> x34, local copies, waits for them, and re-layouts: 2.02 us -> 6.82 us
    ppermute x46, starting transfers between devices: 44.8 us -> 49.2 us  [exchange(): return lax.ppermute(a, axis, [(i, i ^ mask) for i in range(size)])]
  transfers between devices with their start and end apart: 46 -> 46, of which waited for: 20 -> 23; matrix products, arithmetic and copies ran while one was open for 0% -> 0% of each run, Pallas kernels for 38% -> 34%
where the time goes in v4:
time: 253 us; the launch traced here: 249 us
  Pallas kernels  123 us (49%)
  waiting for transfers between devices  68.3 us (27%)
  starting transfers between devices  49.2 us (19%)
  local copies, waits for them, and re-layouts  6.9 us (3%)
    pallas_call x45, Pallas kernels, call(): pl.pallas_call(wrapped, in_specs=[SMEM] * first + [HBM if i in far else V...  123 us
    ppermute x46, waiting for transfers between devices, exchange(): return lax.ppermute(a, axis, [(i, i ^ mask) for i in range(size)])  68.3 us
    ppermute x46, starting transfers between devices, exchange(): return lax.ppermute(a, axis, [(i, i ^ mask) for i in range(size)])  49.2 us
    unnamed x34, local copies, waits for them, and re-layouts  6.82 us
  transfers between devices with their start and end apart: 46, of which 23 were waited for; matrix products, arithmetic and copies ran while one was open for 0% of the time, Pallas kernels for 34%

profile of v4, /device:TPU:0, one launch (start us, length us, event | category | flops | bytes accessed | tf_op | source)
XLA Modules:
  0.0 249.1 jit_solution(2689232311406568242)
XLA Ops:
  0.7 13.9 %shard_map.288 = (bf16[1024,2304]{1,0:T(8,128)(2,1)S(1)}, bf16[1024,768]{1,0:T(8,128)(2,1)S(1)}, bf16[1024,768]{1,0:T(8,128)(2,1)S(1)}, f32[1024,768]{1,0:T(8,12...) custom-call(s32[5]{0:T(128)S(1)} %stack.23.refs_0_, ...), custom_call_target="tpu_custom_call" | custom-call | flops 46000001024 | tf_op jit(solution)/shard_map/pallas_call | solution.py:42
  14.7 4.6 %shard_map.289 = (bf16[16,64,768]{2,1,0:T(8,128)(2,1)}, bf16[16,64,3072]{2,1,0:T(8,128)(2,1)S(1)}, bf16[256,3072]{1,0:T(8,128)(2,1)S(1)}, bf16[256,3072]{1,0:T(8...) custom-call(f32[16,64,768]{2,1,0:T(8,128)S(1)} %bitcast.23, ...), custom_call_target="tpu_custom_call" | custom-call | flops 46000001024 | tf_op jit(solution)/shard_map/pallas_call | solution.py:42
  19.3 4.0 %collective-permute-start.2 = (bf16[16,768]{1,0:T(8,128)(2,1)S(1)}, bf16[16,768]{1,0:T(8,128)(2,1)S(1)}, u32[]{:S(2)}, u32[]{:S(2)}) collective-permute-start(bf16[16,768]{1,0:T(8,128)(2,1)S(1)} %get-tuple-element.156.refs_1_), channel_id=1, source_target_pairs={{0,3},{1,2},{2,1},{3,0},{4,7},{5,6},{6,5},{7,4},{8,11},{9,10},{10,... | collective-permute-start | bytes 73736 | tf_op jit(solution)/shard_map/ppermute | solution.py:510
  26.3 5.7 %shard_map.290 = (bf16[16,64,768]{2,1,0:T(8,128)(2,1)}, bf16[16,64,3072]{2,1,0:T(8,128)(2,1)S(1)}, bf16[16,64,3072]{2,1,0:T(8,128)(2,1)S(1)}, bf16[16,64,768]{2,...) custom-call(f32[16,64,768]{2,1,0:T(8,128)S(1)} %bitcast.24, ...), custom_call_target="tpu_custom_call", output_to_operand_aliasing={{0}: (8, {}), {1}: (9, {})} | custom-call | flops 46000001024 | tf_op jit(solution)/shard_map/pallas_call | solution.py:42
  32.6 4.1 %collective-permute-start.5 = (bf16[64,768]{1,0:T(8,128)(2,1)S(1)}, bf16[64,768]{1,0:T(8,128)(2,1)S(1)}, u32[]{:S(2)}, u32[]{:S(2)}) collective-permute-start(bf16[64,768]{1,0:T(8,128)(2,1)S(1)} %shard_map.291.refs_14_.refs_1_), channel_id=1, source_target_pairs={{0,12},{1,13},{2,14},{3,15},{4,8},{5,9},{6,10},{7,11},{8,4},{9,5},... | collective-permute-start | bytes 294920 | tf_op jit(solution)/shard_map/ppermute | solution.py:510
  37.3 6.1 %shard_map.292 = (bf16[16,64,768]{2,1,0:T(8,128)(2,1)}, bf16[16,64,3072]{2,1,0:T(8,128)(2,1)S(1)}, bf16[16,64,3072]{2,1,0:T(8,128)(2,1)S(1)}, bf16[16,64,768]{2,...) custom-call(f32[16,64,768]{2,1,0:T(8,128)S(1)} %bitcast.25, ...), custom_call_target="tpu_custom_call", output_to_operand_aliasing={{0}: (8, {}), {1}: (9, {}), {2}: (10, {}), {3}: (11, {})} | custom-call | flops 46000001024 | tf_op jit(solution)/shard_map/pallas_call | solution.py:42
  44.7 5.7 %shard_map.294 = (bf16[16,64,768]{2,1,0:T(8,128)(2,1)}, bf16[16,64,3072]{2,1,0:T(8,128)(2,1)S(1)}, bf16[16,64,3072]{2,1,0:T(8,128)(2,1)S(1)}, bf16[16,64,768]{2,...) custom-call(f32[16,64,768]{2,1,0:T(8,128)S(1)} %bitcast.26, ...), custom_call_target="tpu_custom_call", output_to_operand_aliasing={{0}: (8, {}), {1}: (9, {}), {2}: (10, {}), {3}: (11, {})} | custom-call | flops 46000001024 | tf_op jit(solution)/shard_map/pallas_call | solution.py:42
  50.4 5.3 %shard_map.295 = (f32[16,768]{1,0:T(8,128)S(1)}, f32[768,768]{1,0:T(8,128)}, f32[768]{0:T(1024)}) custom-call(s32[5]{0:T(128)S(1)} %stack.23.refs_0_, bf16[256,768]{1,0:T(8,128)(2,1)S(1)} %shard_map.293.refs_14_.refs_1_, bf16[256,768]{1,0:T(8,128)(2,1)S(1)} %collective-permute-done.6.refs_2_, s32[256]{0:T(256)S(1)} %get-tuple-element.164.refs_3_, ...), custom_call_target="tpu_custom_call" | custom-call | flops 46000001024 | tf_op jit(solution)/shard_map/pallas_call | solution.py:42
  57.8 3.5 %shard_map.297.refs_3_ = bf16[1536,768]{1,0:T(8,128)(2,1)S(1)} custom-call(s32[5]{0:T(128)S(1)} %stack.23.refs_0_, bf16[1024,3072]{1,0:T(8,128)(2,1)S(1)} %bitcast.21, bf16[1024,768]{1,0:T(8,128)(2,1)S(1)} %bitcast.31, f32[8,768]{1,0:T(8,128)S(1)} %get-tuple-element.181.refs_3_.refs_5_), custom_call_target="tpu_custom_call" | custom-call | flops 46000001024 | tf_op jit(solution)/shard_map/pallas_call | solution.py:42
  61.9 4.6 %shard_map.298.refs_4_ = bf16[384,3072]{1,0:T(8,128)(2,1)} custom-call(s32[5]{0:T(128)S(1)} %stack.23.refs_0_, bf16[1024,768]{1,0:T(8,128)(2,1)S(1)} %get-tuple-element.182.refs_1_, bf16[1024,3072]{1,0:T(8,128)(2,1)S(1)} %bitcast.17, bf16[1536,768]{1,0:T(8,128)(2,1)S(1)} %shard_map.297.refs_3_), custom_call_target="tpu_custom_call" | custom-call | flops 46000001024 | tf_op jit(solution)/shard_map/pallas_call | solution.py:42
  66.6 4.5 %shard_map.299 = (bf16[768,384]{1,0:T(8,128)(2,1)S(1)}, bf16[768,384]{1,0:T(8,128)(2,1)S(1)}, bf16[768,384]{1,0:T(8,128)(2,1)S(1)}, bf16[768,384]{1,0:T(8,128)(2,1)S(1)}) custom-call(s32[5]{0:T(128)S(1)} %stack.23.refs_0_, bf16[1024,3072]{1,0:T(8,128)(2,1)S(1)} %bitcast.22, bf16[1024,768]{1,0:T(8,128)(2,1)S(1)} %bitcast.32, ...), custom_call_target="tpu_custom_call" | custom-call | flops 46000001024 | tf_op jit(solution)/shard_map/pallas_call | solution.py:42
  76.6 8.2 %shard_map.300 = (bf16[1024,768]{1,0:T(8,128)(2,1)S(1)}, bf16[1024,2304]{1,0:T(8,128)(2,1)S(1)}, f32[8,768]{1,0:T(8,128)S(1)}, f32[8,768]{1,0:T(8,128)S(1)}) custom-call(bf16[1024,768]{1,0:T(8,128)(2,1)S(1)} %bitcast.33, bf16[1024,3072]{1,0:T(8,128)(2,1)S(1)} %bitcast.18, f32[1024,768]{1,0:T(8,128)S(1)} %copy-done.6, ...), custom_call_target="tpu_custom_call" | custom-call | flops 46000001024 | tf_op jit(solution)/shard_map/pallas_call | solution.py:42
  84.8 8.0 %shard_map.301 = (bf16[1024,768]{1,0:T(8,128)(2,1)S(1)}, bf16[1024,2304]{1,0:T(8,128)(2,1)S(1)}, f32[8,768]{1,0:T(8,128)S(1)}, f32[8,768]{1,0:T(8,128)S(1)}) custom-call(bf16[1024,768]{1,0:T(8,128)(2,1)S(1)} %bitcast.34, bf16[1024,3072]{1,0:T(8,128)(2,1)S(1)} %bitcast.19, f32[1024,768]{1,0:T(8,128)S(1)} %copy-done.6, ...), custom_call_target="tpu_custom_call", output_to_operand_aliasing={{0}: (10, {}), {1}: (11, {})} | custom-call | flops 46000001024 | tf_op jit(solution)/shard_map/pallas_call | solution.py:42
  94.9 4.8 %shard_map.303 = (bf16[192,1536]{1,0:T(8,128)(2,1)S(1)}, bf16[192,1536]{1,0:T(8,128)(2,1)S(1)}, bf16[192,1536]{1,0:T(8,128)(2,1)S(1)}, bf16[192,1536]{1,0:T(8,128)(2,1)S(1)}) custom-call(s32[5]{0:T(128)S(1)} %stack.23.refs_0_, bf16[1024,768]{1,0:T(8,128)(2,1)S(1)} %get-tuple-element.182.refs_1_, bf16[1024,3072]{1,0:T(8,128)(2,1)S(1)} %bitcast.20, ...), custom_call_target="tpu_custom_call" | custom-call | flops 46000001024 | tf_op jit(solution)/shard_map/pallas_call | solution.py:42
  99.6 3.0 %collective-permute-done.10.refs_2_ = bf16[384,384]{1,0:T(8,128)(2,1)S(1)} collective-permute-done((bf16[384,384]{1,0:T(8,128)(2,1)S(1)}, bf16[384,384]{1,0:T(8,128)(2,1)S(1)}, u32[]{:S(2)}, u32[]{:S(2)}) %collective-permute-start.10) | collective-permute-done | bytes 294944 | tf_op jit(solution)/shard_map/ppermute | solution.py:510
  104.3 3.2 %shard_map.305 = (bf16[400,3072]{1,0:T(8,128)(2,1)S(1)}, bf16[16,768]{1,0:T(8,128)(2,1)S(1)}) custom-call(s32[5]{0:T(128)S(1)} %stack.23.refs_0_, bf16[1024,768]{1,0:T(8,128)(2,1)S(1)} %bitcast.15, bf16[1024,2304]{1,0:T(8,128)(2,1)S(1)} %get-tuple-element.188.refs_2_.refs_0_, bf16[1024,768]{1,0:T(8,128)(2,1)S(1)} %get-tuple-element.201.refs_3_, ...), custom_call_target="tpu_custom_call" | custom-call | flops 46000001024 | tf_op jit(solution)/shard_map/pallas_call | solution.py:42
  110.4 6.6 %collective-permute-done.13.refs_2_ = bf16[192,768]{1,0:T(8,128)(2,1)S(1)} collective-permute-done((bf16[192,768]{1,0:T(8,128)(2,1)S(1)}, bf16[192,768]{1,0:T(8,128)(2,1)S(1)}, u32[]{:S(2)}, u32[]{:S(2)}) %collective-permute-start.13) | collective-permute-done | bytes 294944 | tf_op jit(solution)/shard_map/ppermute | solution.py:510
  119.5 4.2 %collective-permute-done.15.refs_2_ = bf16[192,1536]{1,0:T(8,128)(2,1)S(1)} collective-permute-done((bf16[192,1536]{1,0:T(8,128)(2,1)S(1)}, bf16[192,1536]{1,0:T(8,128)(2,1)S(1)}, u32[]{:S(2)}, u32[]{:S(2)}) %collective-permute-start.15) | collective-permute-done | bytes 589856 | tf_op jit(solution)/shard_map/ppermute | solution.py:510
  127.9 4.5 %shard_map.308 = (bf16[208,1536]{1,0:T(8,128)(2,1)S(1)}, bf16[208,1536]{1,0:T(8,128)(2,1)S(1)}, bf16[192,1536]{1,0:T(8,128)(2,1)S(1)}, bf16[192,1536]{1,0:T(8,128)(2,1)S(1)}) custom-call(s32[5]{0:T(128)S(1)} %stack.23.refs_0_, bf16[1024,768]{1,0:T(8,128)(2,1)S(1)} %bitcast.16, bf16[1024,2304]{1,0:T(8,128)(2,1)S(1)} %get-tuple-element.188.refs_2_.refs_0_, ...), custom_call_target="tpu_custom_call" | custom-call | flops 46000001024 | tf_op jit(solution)/shard_map/pallas_call | solution.py:42
  137.2 5.0 %shard_map.311 = (bf16[1024,768]{1,0:T(8,128)(2,1)}, f32[8,128]{1,0:T(8,128)S(1)}) custom-call(bf16[1024,2304]{1,0:T(8,128)(2,1)S(1)} %get-tuple-element.188.refs_2_.refs_0_, bf16[768,2304]{1,0:T(8,128)(2,1)S(1)} %copy-done, bf16[1024,768]{1,0:T(8,128)(2,1)S(1)} %get-tuple-element.189.refs_4_.refs_2_, bf16[192,768]{1,0:T(8,128)(2,1)S(1)} %shard_map.310.refs_3_.refs_1_), custom_call_target="tpu_custom_call" | custom-call | flops 46000001024 | tf_op jit(solution)/shard_map/pallas_call | solution.py:42
  150.1 5.1 %collective-permute-done.25.refs_2_ = bf16[48,3072]{1,0:T(8,128)(2,1)S(1)} collective-permute-done((bf16[48,3072]{1,0:T(8,128)(2,1)S(1)}, bf16[48,3072]{1,0:T(8,128)(2,1)S(1)}, u32[]{:S(2)}, u32[]{:S(2)}) %collective-permute-start.25) | collective-permute-done | bytes 294944 | tf_op jit(solution)/shard_map/ppermute | solution.py:510
  161.3 2.9 %collective-permute-start.29 = (bf16[384,384]{1,0:T(8,128)(2,1)S(1)}, bf16[384,384]{1,0:T(8,128)(2,1)S(1)}, u32[]{:S(2)}, u32[]{:S(2)}) collective-permute-start(bf16[384,384]{1,0:T(8,128)(2,1)S(1)} %get-tuple-element.225.refs_5_.refs_3_), channel_id=1, source_target_pairs={{0,1},{1,0},{2,3},{3,2},{4,5},{5,4},{6,7},{7,6},{8,9},{9,8},{10,11... | collective-permute-start | bytes 884744 | tf_op jit(solution)/shard_map/ppermute | solution.py:510
  164.2 4.6 %collective-permute-done.22.refs_2_ = bf16[112,1536]{1,0:T(8,128)(2,1)S(1)} collective-permute-done((bf16[112,1536]{1,0:T(8,128)(2,1)S(1)}, bf16[112,1536]{1,0:T(8,128)(2,1)S(1)}, u32[]{:S(2)}, u32[]{:S(2)}) %collective-permute-start.22) | collective-permute-done | bytes 344096 | tf_op jit(solution)/shard_map/ppermute | solution.py:510
  177.6 5.2 %collective-permute-done.26.refs_2_ = bf16[64,3072]{1,0:T(8,128)(2,1)S(1)} collective-permute-done((bf16[64,3072]{1,0:T(8,128)(2,1)S(1)}, bf16[64,3072]{1,0:T(8,128)(2,1)S(1)}, u32[]{:S(2)}, u32[]{:S(2)}) %collective-permute-start.26) | collective-permute-done | bytes 393248 | tf_op jit(solution)/shard_map/ppermute | solution.py:510
  192.0 2.8 %shard_map.321 = (f32[3072,768]{1,0:T(8,128)}, f32[8,128]{1,0:T(8,128)S(1)}) custom-call(s32[5]{0:T(128)S(1)} %stack.23.refs_0_, bf16[1536,768]{1,0:T(8,128)(2,1)S(1)} %shard_map.320.refs_1_.refs_2_, bf16[1536,768]{1,0:T(8,128)(2,1)S(1)} %shard_map.320.refs_1_.refs_2_), custom_call_target="tpu_custom_call" | custom-call | flops 11500000256 | tf_op jit(solution)/shard_map/pallas_call | solution.py:42
  199.9 2.8 %shard_map.324 = (f32[3072,768]{1,0:T(8,128)}, f32[8,128]{1,0:T(8,128)S(1)}) custom-call(s32[5]{0:T(128)S(1)} %stack.23.refs_0_, bf16[1536,768]{1,0:T(8,128)(2,1)S(1)} %collective-permute-done.37.refs_1_, f32[3072,768]{1,0:T(8,128)} %get-tuple-element.235.refs_2_, bf16[64,3072]{1,0:T(8,128)(2,1)S(1)} %shard_map.323.refs_3_.refs_1_), custom_call_target="tpu_custom_call", output_to_operand_aliasing={{0}: (2, {})} | custom-call | flops 11500000256 | tf_op jit(solution)/shard_map/pallas_call | solution.py:42
  202.7 6.8 %collective-permute-done.36.refs_2_ = bf16[64,3072]{1,0:T(8,128)(2,1)S(1)} collective-permute-done((bf16[64,3072]{1,0:T(8,128)(2,1)S(1)}, bf16[64,3072]{1,0:T(8,128)(2,1)S(1)}, u32[]{:S(2)}, u32[]{:S(2)}) %collective-permute-start.36) | collective-permute-done | bytes 393248 | tf_op jit(solution)/shard_map/ppermute | solution.py:510
  217.3 6.0 %collective-permute-done.38.refs_2_ = bf16[96,1536]{1,0:T(8,128)(2,1)S(1)} collective-permute-done((bf16[96,1536]{1,0:T(8,128)(2,1)S(1)}, bf16[96,1536]{1,0:T(8,128)(2,1)S(1)}, u32[]{:S(2)}, u32[]{:S(2)}) %collective-permute-start.38) | collective-permute-done | bytes 294944 | tf_op jit(solution)/shard_map/ppermute | solution.py:510
  225.9 2.8 %shard_map.329 = (f32[768,3072]{1,0:T(8,128)}, f32[8,128]{1,0:T(8,128)S(1)}) custom-call(s32[5]{0:T(128)S(1)} %stack.23.refs_0_, bf16[384,3072]{1,0:T(8,128)(2,1)S(1)} %collective-permute-done.44.refs_1_, f32[768,3072]{1,0:T(8,128)} %get-tuple-element.243.refs_2_, bf16[192,1536]{1,0:T(8,128)(2,1)S(1)} %get-tuple-element.242.refs_3_), custom_call_target="tpu_custom_call", output_to_operand_aliasing={{0}: (2, {})} | custom-call | flops 11500000256 | tf_op jit(solution)/shard_map/pallas_call | solution.py:42
  228.8 10.0 %collective-permute-done.42.refs_2_ = bf16[192,1536]{1,0:T(8,128)(2,1)S(1)} collective-permute-done((bf16[192,1536]{1,0:T(8,128)(2,1)S(1)}, bf16[192,1536]{1,0:T(8,128)(2,1)S(1)}, u32[]{:S(2)}, u32[]{:S(2)}) %collective-permute-start.42) | collective-permute-done | bytes 589856 | tf_op jit(solution)/shard_map/ppermute | solution.py:510
  240.7 2.8 %shard_map.331 = (f32[768,2304]{1,0:T(8,128)}, f32[768,768]{1,0:T(8,128)}, f32[8,128]{1,0:T(8,128)S(1)}) custom-call(s32[5]{0:T(128)S(1)} %stack.23.refs_0_, bf16[384,3072]{1,0:T(8,128)(2,1)S(1)} %shard_map.330.refs_1_.refs_2_, bf16[384,3072]{1,0:T(8,128)(2,1)S(1)} %shard_map.330.refs_1_.refs_2_), custom_call_target="tpu_custom_call" | custom-call | flops 11500000256 | tf_op jit(solution)/shard_map/pallas_call | solution.py:42
  245.2 3.4 %shard_map.332 = (f32[768,2304]{1,0:T(8,128)}, f32[768,768]{1,0:T(8,128)}, f32[8,128]{1,0:T(8,128)}) custom-call(s32[5]{0:T(128)S(1)} %stack.23.refs_0_, bf16[384,3072]{1,0:T(8,128)(2,1)S(1)} %collective-permute-done.45.refs_1_, f32[768,2304]{1,0:T(8,128)} %get-tuple-element.245.refs_2_, ...), custom_call_target="tpu_custom_call", output_to_operand_aliasing={{0}: (2, {}), {1}: (3, {})} | custom-call | flops 11500000256 | tf_op jit(solution)/shard_map/pallas_call | solution.py:42
  (141 shorter events, 82.7 us)
Async XLA Ops:
  19.3 12.6 %collective-permute-start.2 = (bf16[16,768]{1,0:T(8,128)(2,1)S(1)}, bf16[16,768]{1,0:T(8,128)(2,1)S(1)}, u32[]{:S(2)}, u32[]{:S(2)}) collective-permute-start(bf16[16,768]{1,0:T(8,128)(2,1)S(1)} %get-tuple-element.156.refs_1_), channel_id=1, source_target_pairs={{0,3},{1,2},{2,1},{3,0},{4,7},{5,6},{6,5},{7,4},{8,11},{9,10},{10,... | collective-permute-start | bytes 73736 | tf_op jit(solution)/shard_map/ppermute | solution.py:510
  32.6 10.8 %collective-permute-start.5 = (bf16[64,768]{1,0:T(8,128)(2,1)S(1)}, bf16[64,768]{1,0:T(8,128)(2,1)S(1)}, u32[]{:S(2)}, u32[]{:S(2)}) collective-permute-start(bf16[64,768]{1,0:T(8,128)(2,1)S(1)} %shard_map.291.refs_14_.refs_1_), channel_id=1, source_target_pairs={{0,12},{1,13},{2,14},{3,15},{4,8},{5,9},{6,10},{7,11},{8,4},{9,5},... | collective-permute-start | bytes 294920 | tf_op jit(solution)/shard_map/ppermute | solution.py:510
  66.5 28.4 %collective-permute-start.12 = (bf16[384,3072]{1,0:T(8,128)(2,1)}, bf16[384,3072]{1,0:T(8,128)(2,1)}, u32[]{:S(2)}, u32[]{:S(2)}) collective-permute-start(bf16[384,3072]{1,0:T(8,128)(2,1)} %shard_map.298.refs_4_), channel_id=1, source_target_pairs={{0,16},{16,0},{1,17},{17,1},{2,18},{18,2},{3,19},{19,3},{4,20},{20... | collective-permute-start | bytes 7077896 | tf_op jit(solution)/shard_map/ppermute | solution.py:510
  71.2 21.7 %collective-permute-start.8 = (bf16[768,384]{1,0:T(8,128)(2,1)S(1)}, bf16[768,384]{1,0:T(8,128)(2,1)S(1)}, u32[]{:S(2)}, u32[]{:S(2)}) collective-permute-start(bf16[768,384]{1,0:T(8,128)(2,1)S(1)} %get-tuple-element.191), channel_id=1, source_target_pairs={{0,1},{1,0},{2,3},{3,2},{4,5},{5,4},{6,7},{7,6},{8,9},{9,8},{10,11... | collective-permute-start | bytes 1769480 | tf_op jit(solution)/shard_map/ppermute | solution.py:510
  72.7 20.2 %collective-permute-start.9 = (bf16[768,384]{1,0:T(8,128)(2,1)S(1)}, bf16[768,384]{1,0:T(8,128)(2,1)S(1)}, u32[]{:S(2)}, u32[]{:S(2)}) collective-permute-start(bf16[768,384]{1,0:T(8,128)(2,1)S(1)} %get-tuple-element.192), channel_id=1, source_target_pairs={{0,2},{1,3},{2,0},{3,1},{4,6},{5,7},{6,4},{7,5},{8,10},{9,11},{10,... | collective-permute-start | bytes 1769480 | tf_op jit(solution)/shard_map/ppermute | solution.py:510
  107.5 20.4 %collective-permute-start.19 = (bf16[400,3072]{1,0:T(8,128)(2,1)S(1)}, bf16[400,3072]{1,0:T(8,128)(2,1)S(1)}, u32[]{:S(2)}, u32[]{:S(2)}) collective-permute-start(bf16[400,3072]{1,0:T(8,128)(2,1)S(1)} %get-tuple-element.212), channel_id=1, source_target_pairs={{0,16},{16,0},{1,17},{17,1},{2,18},{18,2},{3,19},{19,3},{4,20},{20... | collective-permute-start | bytes 7372808 | tf_op jit(solution)/shard_map/ppermute | solution.py:510
  107.6 9.4 %collective-permute-start.13 = (bf16[192,768]{1,0:T(8,128)(2,1)S(1)}, bf16[192,768]{1,0:T(8,128)(2,1)S(1)}, u32[]{:S(2)}, u32[]{:S(2)}) collective-permute-start(bf16[192,768]{1,0:T(8,128)(2,1)S(1)} %get-tuple-element.200), channel_id=1, source_target_pairs={{0,4},{1,5},{2,6},{3,7},{4,0},{5,1},{6,2},{7,3},{8,12},{9,13},{10,... | collective-permute-start | bytes 884744 | tf_op jit(solution)/shard_map/ppermute | solution.py:510
  108.3 15.4 %collective-permute-start.15 = (bf16[192,1536]{1,0:T(8,128)(2,1)S(1)}, bf16[192,1536]{1,0:T(8,128)(2,1)S(1)}, u32[]{:S(2)}, u32[]{:S(2)}) collective-permute-start(bf16[192,1536]{1,0:T(8,128)(2,1)S(1)} %get-tuple-element.206), channel_id=1, source_target_pairs={{0,1},{1,0},{2,3},{3,2},{4,5},{5,4},{6,7},{7,6},{8,9},{9,8},{10,11... | collective-permute-start | bytes 1769480 | tf_op jit(solution)/shard_map/ppermute | solution.py:510
  108.9 15.1 %collective-permute-start.16 = (bf16[192,1536]{1,0:T(8,128)(2,1)S(1)}, bf16[192,1536]{1,0:T(8,128)(2,1)S(1)}, u32[]{:S(2)}, u32[]{:S(2)}) collective-permute-start(bf16[192,1536]{1,0:T(8,128)(2,1)S(1)} %get-tuple-element.207), channel_id=1, source_target_pairs={{0,2},{1,3},{2,0},{3,1},{4,6},{5,7},{6,4},{7,5},{8,10},{9,11},{10,... | collective-permute-start | bytes 1769480 | tf_op jit(solution)/shard_map/ppermute | solution.py:510
  117.6 17.5 %collective-permute-start.14 = (bf16[192,768]{1,0:T(8,128)(2,1)S(1)}, bf16[192,768]{1,0:T(8,128)(2,1)S(1)}, u32[]{:S(2)}, u32[]{:S(2)}) collective-permute-start(bf16[192,768]{1,0:T(8,128)(2,1)S(1)} %shard_map.306.refs_5_.refs_1_), channel_id=1, source_target_pairs={{0,8},{1,9},{2,10},{3,11},{4,12},{5,13},{6,14},{7,15},{8,0},{9,1},... | collective-permute-start | bytes 884744 | tf_op jit(solution)/shard_map/ppermute | solution.py:510
  132.4 13.8 %collective-permute-start.21 = (bf16[192,1536]{1,0:T(8,128)(2,1)S(1)}, bf16[192,1536]{1,0:T(8,128)(2,1)S(1)}, u32[]{:S(2)}, u32[]{:S(2)}) collective-permute-start(bf16[192,1536]{1,0:T(8,128)(2,1)S(1)} %get-tuple-element.218), channel_id=1, source_target_pairs={{0,2},{1,3},{2,0},{3,1},{4,6},{5,7},{6,4},{7,5},{8,10},{9,11},{10,... | collective-permute-start | bytes 1769480 | tf_op jit(solution)/shard_map/ppermute | solution.py:510
  132.9 14.9 %collective-permute-start.20 = (bf16[208,1536]{1,0:T(8,128)(2,1)S(1)}, bf16[208,1536]{1,0:T(8,128)(2,1)S(1)}, u32[]{:S(2)}, u32[]{:S(2)}) collective-permute-start(bf16[208,1536]{1,0:T(8,128)(2,1)S(1)} %get-tuple-element.217), channel_id=1, source_target_pairs={{0,1},{1,0},{2,3},{3,2},{4,5},{5,4},{6,7},{7,6},{8,9},{9,8},{10,11... | collective-permute-start | bytes 1916936 | tf_op jit(solution)/shard_map/ppermute | solution.py:510
  142.2 17.5 %collective-permute-start.24 = (bf16[192,768]{1,0:T(8,128)(2,1)S(1)}, bf16[192,768]{1,0:T(8,128)(2,1)S(1)}, u32[]{:S(2)}, u32[]{:S(2)}) collective-permute-start(bf16[192,768]{1,0:T(8,128)(2,1)S(1)} %shard_map.310.refs_3_.refs_1_), channel_id=1, source_target_pairs={{0,4},{1,5},{2,6},{3,7},{4,0},{5,1},{6,2},{7,3},{8,12},{9,13},{10,... | collective-permute-start | bytes 884744 | tf_op jit(solution)/shard_map/ppermute | solution.py:510
  143.5 11.8 %collective-permute-start.25 = (bf16[48,3072]{1,0:T(8,128)(2,1)S(1)}, bf16[48,3072]{1,0:T(8,128)(2,1)S(1)}, u32[]{:S(2)}, u32[]{:S(2)}) collective-permute-start(bf16[48,3072]{1,0:T(8,128)(2,1)S(1)} %get-tuple-element.224), channel_id=1, source_target_pairs={{0,4},{1,5},{2,6},{3,7},{4,0},{5,1},{6,2},{7,3},{8,12},{9,13},{10,... | collective-permute-start | bytes 884744 | tf_op jit(solution)/shard_map/ppermute | solution.py:510
  148.7 15.6 %collective-permute-start.23 = (bf16[96,1536]{1,0:T(8,128)(2,1)S(1)}, bf16[96,1536]{1,0:T(8,128)(2,1)S(1)}, u32[]{:S(2)}, u32[]{:S(2)}) collective-permute-start(bf16[96,1536]{1,0:T(8,128)(2,1)S(1)} %get-tuple-element.223), channel_id=1, source_target_pairs={{0,1},{1,0},{2,3},{3,2},{4,5},{5,4},{6,7},{7,6},{8,9},{9,8},{10,11... | collective-permute-start | bytes 884744 | tf_op jit(solution)/shard_map/ppermute | solution.py:510
  155.9 18.5 %collective-permute-start.27 = (bf16[48,3072]{1,0:T(8,128)(2,1)S(1)}, bf16[48,3072]{1,0:T(8,128)(2,1)S(1)}, u32[]{:S(2)}, u32[]{:S(2)}) collective-permute-start(bf16[48,3072]{1,0:T(8,128)(2,1)S(1)} %shard_map.313.refs_3_.refs_1_), channel_id=1, source_target_pairs={{0,8},{1,9},{2,10},{3,11},{4,12},{5,13},{6,14},{7,15},{8,0},{9,1},... | collective-permute-start | bytes 884744 | tf_op jit(solution)/shard_map/ppermute | solution.py:510
  158.6 10.2 %collective-permute-start.22 = (bf16[112,1536]{1,0:T(8,128)(2,1)S(1)}, bf16[112,1536]{1,0:T(8,128)(2,1)S(1)}, u32[]{:S(2)}, u32[]{:S(2)}) collective-permute-start(bf16[112,1536]{1,0:T(8,128)(2,1)S(1)} %get-tuple-element.221), channel_id=1, source_target_pairs={{0,2},{1,3},{2,0},{3,1},{4,6},{5,7},{6,4},{7,5},{8,10},{9,11},{10,... | collective-permute-start | bytes 1032200 | tf_op jit(solution)/shard_map/ppermute | solution.py:510
  160.3 11.6 %collective-permute-start.28 = (bf16[384,384]{1,0:T(8,128)(2,1)S(1)}, bf16[384,384]{1,0:T(8,128)(2,1)S(1)}, u32[]{:S(2)}, u32[]{:S(2)}) collective-permute-start(bf16[384,384]{1,0:T(8,128)(2,1)S(1)} %get-tuple-element.228.refs_1_), channel_id=1, source_target_pairs={{0,2},{1,3},{2,0},{3,1},{4,6},{5,7},{6,4},{7,5},{8,10},{9,11},{10,... | collective-permute-start | bytes 884744 | tf_op jit(solution)/shard_map/ppermute | solution.py:510
  161.3 10.7 %collective-permute-start.29 = (bf16[384,384]{1,0:T(8,128)(2,1)S(1)}, bf16[384,384]{1,0:T(8,128)(2,1)S(1)}, u32[]{:S(2)}, u32[]{:S(2)}) collective-permute-start(bf16[384,384]{1,0:T(8,128)(2,1)S(1)} %get-tuple-element.225.refs_5_.refs_3_), channel_id=1, source_target_pairs={{0,1},{1,0},{2,3},{3,2},{4,5},{5,4},{6,7},{7,6},{8,9},{9,8},{10,11... | collective-permute-start | bytes 884744 | tf_op jit(solution)/shard_map/ppermute | solution.py:510
  169.5 13.3 %collective-permute-start.26 = (bf16[64,3072]{1,0:T(8,128)(2,1)S(1)}, bf16[64,3072]{1,0:T(8,128)(2,1)S(1)}, u32[]{:S(2)}, u32[]{:S(2)}) collective-permute-start(bf16[64,3072]{1,0:T(8,128)(2,1)S(1)} %get-tuple-element.227), channel_id=1, source_target_pairs={{0,4},{1,5},{2,6},{3,7},{4,0},{5,1},{6,2},{7,3},{8,12},{9,13},{10,... | collective-permute-start | bytes 1179656 | tf_op jit(solution)/shard_map/ppermute | solution.py:510
  172.6 18.5 %collective-permute-start.35 = (bf16[768,384]{1,0:T(8,128)(2,1)S(1)}, bf16[768,384]{1,0:T(8,128)(2,1)S(1)}, u32[]{:S(2)}, u32[]{:S(2)}) collective-permute-start(bf16[768,384]{1,0:T(8,128)(2,1)S(1)} %get-tuple-element.229.refs_3_), channel_id=1, source_target_pairs={{0,2},{1,3},{2,0},{3,1},{4,6},{5,7},{6,4},{7,5},{8,10},{9,11},{10,... | collective-permute-start | bytes 1769480 | tf_op jit(solution)/shard_map/ppermute | solution.py:510
  175.0 13.0 %collective-permute-start.31 = (bf16[48,3072]{1,0:T(8,128)(2,1)S(1)}, bf16[48,3072]{1,0:T(8,128)(2,1)S(1)}, u32[]{:S(2)}, u32[]{:S(2)}) collective-permute-start(bf16[48,3072]{1,0:T(8,128)(2,1)S(1)} %shard_map.317.refs_3_.refs_1_), channel_id=1, source_target_pairs={{0,4},{1,5},{2,6},{3,7},{4,0},{5,1},{6,2},{7,3},{8,12},{9,13},{10,... | collective-permute-start | bytes 884744 | tf_op jit(solution)/shard_map/ppermute | solution.py:510
  177.6 13.5 %collective-permute-start.34 = (bf16[768,384]{1,0:T(8,128)(2,1)S(1)}, bf16[768,384]{1,0:T(8,128)(2,1)S(1)}, u32[]{:S(2)}, u32[]{:S(2)}) collective-permute-start(bf16[768,384]{1,0:T(8,128)(2,1)S(1)} %get-tuple-element.232.refs_1_), channel_id=1, source_target_pairs={{0,1},{1,0},{2,3},{3,2},{4,5},{5,4},{6,7},{7,6},{8,9},{9,8},{10,11... | collective-permute-start | bytes 1769480 | tf_op jit(solution)/shard_map/ppermute | solution.py:510
  183.5 15.2 %collective-permute-start.30 = (bf16[64,3072]{1,0:T(8,128)(2,1)S(1)}, bf16[64,3072]{1,0:T(8,128)(2,1)S(1)}, u32[]{:S(2)}, u32[]{:S(2)}) collective-permute-start(bf16[64,3072]{1,0:T(8,128)(2,1)S(1)} %shard_map.318.refs_3_.refs_1_), channel_id=1, source_target_pairs={{0,8},{1,9},{2,10},{3,11},{4,12},{5,13},{6,14},{7,15},{8,0},{9,1},... | collective-permute-start | bytes 1179656 | tf_op jit(solution)/shard_map/ppermute | solution.py:510
  198.5 13.1 %collective-permute-start.40 = (bf16[192,1536]{1,0:T(8,128)(2,1)S(1)}, bf16[192,1536]{1,0:T(8,128)(2,1)S(1)}, u32[]{:S(2)}, u32[]{:S(2)}) collective-permute-start(bf16[192,1536]{1,0:T(8,128)(2,1)S(1)} %get-tuple-element.239.refs_1_), channel_id=1, source_target_pairs={{0,1},{1,0},{2,3},{3,2},{4,5},{5,4},{6,7},{7,6},{8,9},{9,8},{10,11... | collective-permute-start | bytes 1769480 | tf_op jit(solution)/shard_map/ppermute | solution.py:510
  198.5 14.4 %collective-permute-start.41 = (bf16[192,1536]{1,0:T(8,128)(2,1)S(1)}, bf16[192,1536]{1,0:T(8,128)(2,1)S(1)}, u32[]{:S(2)}, u32[]{:S(2)}) collective-permute-start(bf16[192,1536]{1,0:T(8,128)(2,1)S(1)} %get-tuple-element.234.refs_3_), channel_id=1, source_target_pairs={{0,2},{1,3},{2,0},{3,1},{4,6},{5,7},{6,4},{7,5},{8,10},{9,11},{10,... | collective-permute-start | bytes 1769480 | tf_op jit(solution)/shard_map/ppermute | solution.py:510
  199.3 10.1 %collective-permute-start.36 = (bf16[64,3072]{1,0:T(8,128)(2,1)S(1)}, bf16[64,3072]{1,0:T(8,128)(2,1)S(1)}, u32[]{:S(2)}, u32[]{:S(2)}) collective-permute-start(bf16[64,3072]{1,0:T(8,128)(2,1)S(1)} %shard_map.323.refs_3_.refs_1_), channel_id=1, source_target_pairs={{0,4},{1,5},{2,6},{3,7},{4,0},{5,1},{6,2},{7,3},{8,12},{9,13},{10,... | collective-permute-start | bytes 1179656 | tf_op jit(solution)/shard_map/ppermute | solution.py:510
  213.7 12.2 %collective-permute-start.44 = (bf16[384,3072]{1,0:T(8,128)(2,1)S(1)}, bf16[384,3072]{1,0:T(8,128)(2,1)S(1)}, u32[]{:S(2)}, u32[]{:S(2)}) collective-permute-start(bf16[384,3072]{1,0:T(8,128)(2,1)S(1)} %shard_map.326.refs_1_.refs_2_), channel_id=1, source_target_pairs={{0,16},{16,0},{1,17},{17,1},{2,18},{18,2},{3,19},{19,3},{4,20},{20... | collective-permute-start | bytes 7077896 | tf_op jit(solution)/shard_map/ppermute | solution.py:510
  213.8 9.5 %collective-permute-start.39 = (bf16[96,1536]{1,0:T(8,128)(2,1)S(1)}, bf16[96,1536]{1,0:T(8,128)(2,1)S(1)}, u32[]{:S(2)}, u32[]{:S(2)}) collective-permute-start(bf16[96,1536]{1,0:T(8,128)(2,1)S(1)} %get-tuple-element.238.refs_5_.refs_3_), channel_id=1, source_target_pairs={{0,1},{1,0},{2,3},{3,2},{4,5},{5,4},{6,7},{7,6},{8,9},{9,8},{10,11... | collective-permute-start | bytes 884744 | tf_op jit(solution)/shard_map/ppermute | solution.py:510
  214.2 9.1 %collective-permute-start.38 = (bf16[96,1536]{1,0:T(8,128)(2,1)S(1)}, bf16[96,1536]{1,0:T(8,128)(2,1)S(1)}, u32[]{:S(2)}, u32[]{:S(2)}) collective-permute-start(bf16[96,1536]{1,0:T(8,128)(2,1)S(1)} %get-tuple-element.237.refs_1_), channel_id=1, source_target_pairs={{0,2},{1,3},{2,0},{3,1},{4,6},{5,7},{6,4},{7,5},{8,10},{9,11},{10,... | collective-permute-start | bytes 884744 | tf_op jit(solution)/shard_map/ppermute | solution.py:510
  223.9 14.9 %collective-permute-start.42 = (bf16[192,1536]{1,0:T(8,128)(2,1)S(1)}, bf16[192,1536]{1,0:T(8,128)(2,1)S(1)}, u32[]{:S(2)}, u32[]{:S(2)}) collective-permute-start(bf16[192,1536]{1,0:T(8,128)(2,1)S(1)} %get-tuple-element.241.refs_1_), channel_id=1, source_target_pairs={{0,1},{1,0},{2,3},{3,2},{4,5},{5,4},{6,7},{7,6},{8,9},{9,8},{10,11... | collective-permute-start | bytes 1769480 | tf_op jit(solution)/shard_map/ppermute | solution.py:510
  225.6 14.3 %collective-permute-start.43 = (bf16[192,1536]{1,0:T(8,128)(2,1)S(1)}, bf16[192,1536]{1,0:T(8,128)(2,1)S(1)}, u32[]{:S(2)}, u32[]{:S(2)}) collective-permute-start(bf16[192,1536]{1,0:T(8,128)(2,1)S(1)} %get-tuple-element.242.refs_3_), channel_id=1, source_target_pairs={{0,2},{1,3},{2,0},{3,1},{4,6},{5,7},{6,4},{7,5},{8,10},{9,11},{10,... | collective-permute-start | bytes 1769480 | tf_op jit(solution)/shard_map/ppermute | solution.py:510
  (31 other events, 225.2 us)

commit v5 on v4

--- a/solution.py
+++ b/solution.py
@@ -46,7 +46,7 @@
         out_shape=[(pltpu.HBM if i in far_out or i in hand_out else pltpu.VMEM)(o.shape, o.dtype) for i, o in enumerate(outs)],
         scratch_shapes=list(scratch),
         input_output_aliases={first + k: v for k, v in (aliases or {}).items()},
-        cost_estimate=pl.CostEstimate(flops=cost * 10**8, bytes_accessed=0, transcendentals=0),
+        cost_estimate=pl.CostEstimate(flops=int(cost * 2 * 10**7), bytes_accessed=0, transcendentals=0),
         compiler_params=pltpu.CompilerParams(vmem_limit_bytes=limit * MIB),
     )(*([] if bits is None else [bits]), *ins, *after)
 
@@ -497,274 +497,264 @@
             refs[-1][pl.ds(at, rows), :] = ref[...]
 
     return call(
-        body, blocks, [struct((rows * len(blocks), width), low)], bits=bits, after=after, limit=8, cost=115
+        body, blocks, [struct((rows * len(blocks), width), low)], bits=bits, after=after, limit=8, cost=690
     )[0]
 
 
-CORE, BIT0, BIT1, BIT2, PLACE = range(5)
+CORE, FIRST, SECOND, THIRD, PLACE = range(5)
 SMALL = 16
-
-
-def exchange(a, axis, mask):
-    size = lax.axis_size(axis)
-    return lax.ppermute(a, axis, [(i, i ^ mask) for i in range(size)])
+MASKS = {FIRST: (1, 2), SECOND: (2, 1), THIRD: (4, 4)}
+
+
+def exchange(a, masks):
+    size = lax.axis_size("dp")
+    pairs = [(core * size + i, core * size + (i ^ masks[core])) for core in range(2) for i in range(size)]
+    return lax.ppermute(a, ("stream", "dp"), pairs)
+
+
+def cross(a):
+    return lax.ppermute(a, "stream", [(0, 1), (1, 0)])
 
 
 class Sources:
-    def __init__(self, pairs, small=None):
-        self.pairs = pairs
-        self.small = small
-        self.m = pairs[0][0].shape[1]
-        self.n = sum(g.shape[1] for _, g in pairs)
-        self.flat = [a for pair in pairs for a in pair]
-
-
-def gradient_rows(src, bits, recv, after=()):
+    def __init__(self, products, small=()):
+        self.products = products
+        self.small = list(small)
+        self.m = products[0][0].shape[1]
+        self.n = sum(hi - lo for _, _, lo, hi in products)
+        self.arrays = [a for left, right, _, _ in products for a in (left, right)]
+
+    def pieces(self, refs):
+        at = 0
+        for i, (_, _, lo, hi) in enumerate(self.products):
+            yield refs[2 * i], refs[2 * i + 1], lo, at, hi - lo
+            at += hi - lo
+
+
+def gradient_to_send(src, bits, after=()):
+    m, n = src.m, src.n
+    half = m // 2
+    count = len(src.arrays)
+    small = src.small
+
+    def body(b, *refs):
+        out = refs[count + len(small)]
+        rows = pl.ds(pl.multiple_of((1 - b[CORE]) * half, 128), half)
+        for a, g, lo, at, size in src.pieces(refs):
+            out[:half, at : at + size] = trans_left(a[:, rows], g[:, lo : lo + size]).astype(low)
+        if small:
+            up, bin_sum, down, bqv = refs[count : count + 4]
+            kept = refs[-1]
+            width = up.shape[1]
+            parts = [up[:3]] + [bin_sum[:, c : c + width] for c in range(0, bin_sum.shape[1], width)] + [down[:3], bqv[:2]]
+            parts.append(jnp.zeros((SMALL - sum(p.shape[0] for p in parts), width), wide))
+            kept[...] = jnp.concatenate(parts, axis=0).astype(low)
+            out[half:, :] = jnp.zeros((SMALL, n), low)
+            out[half:, :width] = kept[...]
+
+    shapes = [struct((half + (SMALL if small else 0), n), low)]
+    if small:
+        shapes.append(struct((SMALL, small[0].shape[1]), low))
+    return call(body, src.arrays + small, shapes, bits=bits, after=after)
+
+
+def gradient_sum(src, bits, got, kept, bit, after=()):
     m, n = src.m, src.n
     half, quarter = m // 2, m // 4
-    count = len(src.flat)
-    edge = n // 2
-
-    small = src.small or []
-    extra = SMALL if small else 0
-
-    if recv is None:
-
-        def body(b, *refs):
-            out = refs[count + len(small)]
-            rows = pl.ds(pl.multiple_of((1 - b[CORE]) * half, 128), half)
-            at = 0
-            for a, g in zip(refs[:count:2], refs[1:count:2]):
-                out[:half, at : at + g.shape[1]] = trans_left(a[:, rows], g[...]).astype(low)
-                at += g.shape[1]
-            if small:
-                up, bin_sum, down, bqv = refs[count : count + 4]
-                kept = refs[-1]
-                width = up.shape[1]
-                parts = [up[:3]] + [bin_sum[:, c : c + width] for c in range(0, bin_sum.shape[1], width)] + [down[:3], bqv[:2]]
-                parts.append(jnp.zeros((SMALL - sum(p.shape[0] for p in parts), width), wide))
-                kept[...] = jnp.concatenate(parts, axis=0).astype(low)
-                out[half:, :] = jnp.zeros((SMALL, n), low)
-                out[half:, :width] = kept[...]
-
-        shapes = [struct((half + extra, n), low)] + ([struct((SMALL, small[0].shape[1]), low)] if small else [])
-        return call(body, src.flat + small, shapes, bits=bits, after=after)
+    count = len(src.arrays)
+    extra = SMALL if src.small else 0
 
     def body(b, *refs):
-        got, left_send, left_keep, right_send, right_keep = refs[-5:]
+        got_ref, send, keep = refs[-3:]
+        if extra:
+            mine = refs[count]
+            total = (mine[...].astype(wide) + got_ref[half:, : mine.shape[1]].astype(wide)).astype(low)
+            for ref in (send, keep):
+                ref[quarter:, :] = jnp.zeros((SMALL, n), low)
+                ref[quarter:, : mine.shape[1]] = total
         rows = pl.ds(pl.multiple_of(b[CORE] * half, 128), half)
+        for a, g, lo, at, size in src.pieces(refs):
+            c = slice(at, at + size)
+            value = (trans_left(a[:, rows], g[:, lo : lo + size]) + got_ref[:half, c].astype(wide)).astype(low)
+
+            def put(kept_half, c=c, value=value):
+                keep[:quarter, c] = value[kept_half * quarter : (kept_half + 1) * quarter]
+                send[:quarter, c] = value[(1 - kept_half) * quarter : (2 - kept_half) * quarter]
+
+            pl.when(b[bit] == 0)(functools.partial(put, 0))
+            pl.when(b[bit] != 0)(functools.partial(put, 1))
+
+    return call(
+        body,
+        src.arrays + ([kept] if extra else []) + [got],
+        [struct((quarter + extra, n), low)] * 2,
+        bits=bits,
+        after=after,
+    )
+
+
+def whole_call(body, arrays, shapes, bits, after=(), **kwargs):
+    return call(body, arrays, shapes, bits=bits, after=after, limit=8, cost=690, **kwargs)
+
+
+def halve(mine, got, bit, extra, bits, after=()):
+    rows, cols = (mine.shape[0] - extra) // 2, mine.shape[1]
+
+    def body(b, m, g, send, keep):
+        for which, out in ((1 - b[bit], send), (b[bit], keep)):
+            at = pl.ds(pl.multiple_of(which * rows, rows), rows)
+            out[:rows, :] = (m[at, :].astype(wide) + g[at, :].astype(wide)).astype(low)
         if extra:
-            total = (refs[count][...].astype(wide) + got[half:, : refs[count].shape[1]].astype(wide)).astype(low)
-            for ref in (left_send, left_keep):
-                ref[quarter:, :] = jnp.zeros((SMALL, edge), low)
-                ref[quarter:, : total.shape[1]] = total
-        for side, bit, send, keep in ((0, BIT0, left_send, left_keep), (1, BIT1, right_send, right_keep)):
-            at = 0
-            for a, g in zip(refs[:count:2], refs[1:count:2]):
-                lo, hi = max(at, side * edge), min(at + g.shape[1], (side + 1) * edge)
-                if lo < hi:
-                    c = slice(lo - side * edge, hi - side * edge)
-                    value = (trans_left(a[:, rows], g[:, lo - at : hi - at]) + got[:half, lo:hi].astype(wide)).astype(low)
-
-                    def put(kept, c=c, value=value, send=send, keep=keep):
-                        keep[:quarter, c] = value[kept * quarter : (kept + 1) * quarter]
-                        send[:quarter, c] = value[(1 - kept) * quarter : (2 - kept) * quarter]
-
-                    pl.when(b[bit] == 0)(functools.partial(put, 0))
-                    pl.when(b[bit] != 0)(functools.partial(put, 1))
-                at += g.shape[1]
-
-    shapes = [struct((quarter + e, edge), low) for e in (extra, extra, 0, 0)]
-    return call(body, src.flat + ([src.kept] if small else []) + [recv], shapes, bits=bits, after=after)
-
-
-def part_rows(ref, bit, rows):
-    return ref[pl.ds(pl.multiple_of(bit * rows, rows), rows), :].astype(wide)
-
-
-def whole_call(body, arrays, shapes, bits, after=()):
-    return call(body, arrays, [struct(s, low) for s in shapes], bits=bits, after=after, limit=8, cost=115)
-
-
-def halve_sides(left, left_got, right, right_got, bits, after=()):
-    rows, cols = right.shape[0] // 2, right.shape[1]
-    extra = left.shape[0] - right.shape[0]
-
-    def body(b, l, lg, r, rg, ls, lk, rs, rk):
-        for mine, got, bit, send, keep in ((l, lg, BIT1, ls, lk), (r, rg, BIT0, rs, rk)):
-            send[:rows, :] = (part_rows(mine, 1 - b[bit], rows) + part_rows(got, 1 - b[bit], rows)).astype(low)
-            keep[:rows, :] = (part_rows(mine, b[bit], rows) + part_rows(got, b[bit], rows)).astype(low)
-        if extra:
-            total = (l[2 * rows :, :].astype(wide) + lg[2 * rows :, :].astype(wide)).astype(low)
-            ls[rows:, :] = total
-            lk[rows:, :] = total
-
-    shapes = [(rows + e, cols) for e in (extra, extra, 0, 0)]
-    return whole_call(body, [left, left_got, right, right_got], shapes, bits, after)
-
-
-def halve_both(left, left_got, right, right_got, bits, after=()):
-    rows, cols = right.shape[0] // 2, right.shape[1]
-    extra = left.shape[0] - right.shape[0]
-
-    def body(b, l, lg, r, rg, send, keep):
-        for mine, got, c in ((l, lg, slice(0, cols)), (r, rg, slice(cols, 2 * cols))):
-            send[:rows, c] = (part_rows(mine, 1 - b[BIT2], rows) + part_rows(got, 1 - b[BIT2], rows)).astype(low)
-            keep[:rows, c] = (part_rows(mine, b[BIT2], rows) + part_rows(got, b[BIT2], rows)).astype(low)
-        if extra:
-            total = (l[2 * rows :, :].astype(wide) + lg[2 * rows :, :].astype(wide)).astype(low)
-            for ref in (send, keep):
-                ref[rows:, :cols] = total
-                ref[rows:, cols:] = jnp.zeros_like(total)
-
-    return whole_call(body, [left, left_got, right, right_got], [(rows + extra, 2 * cols)] * 2, bits, after)
+            total = (m[2 * rows :, :].astype(wide) + g[2 * rows :, :].astype(wide)).astype(low)
+            send[rows:, :] = total
+            keep[rows:, :] = total
+
+    return whole_call(body, [mine, got], [struct((rows + extra, cols), low)] * 2, bits, after)
 
 
 def add_up(mine, got, bits, after=()):
     def body(b, m, g, out):
         out[...] = (m[...].astype(wide) + g[...].astype(wide)).astype(low)
 
-    return whole_call(body, [mine, got], [mine.shape], bits, after)[0]
-
-
-def place(out, mine, got, bit, cols=slice(None), rows=None):
-    rows = mine.shape[0] if rows is None else rows
-    out[pl.ds(pl.multiple_of(bit * rows, rows), rows), :] = mine[:rows, cols]
-    out[pl.ds(pl.multiple_of((1 - bit) * rows, rows), rows), :] = got[:rows, cols]
-
-
-def join_both(mine, got, rows, vectors, bits, after=()):
-    cols = mine.shape[1] // 2
-    width = vectors[1]
+    return whole_call(body, [mine, got], [struct(mine.shape, low)], bits, after)
+
+
+def add_last(mine, got, lengths, width, bits, after=()):
+    rows = mine.shape[0] - SMALL
 
     def body(b, m, g, *refs):
-        *outs, left, right = refs
-        place(left, m, g, b[BIT2], slice(0, cols), rows)
-        place(right, m, g, b[BIT2], slice(cols, 2 * cols), rows)
-        at = rows
-        for out in outs:
-            for c in range(0, out.shape[0], width):
-                out[pl.ds(c, width)] = m[at : at + 1, :width].astype(wide).reshape(-1)
+        *vectors, out = refs
+        out[...] = (m[:rows, :].astype(wide) + g[:rows, :].astype(wide)).astype(low)
+        total = (m[rows:, :width].astype(wide) + g[rows:, :width].astype(wide)).astype(low).astype(wide)
+        at = 0
+        for vector in vectors:
+            for c in range(0, vector.shape[0], width):
+                vector[pl.ds(c, width)] = total[at : at + 1].reshape(-1)
                 at += 1
 
-    shapes = [struct((v,), wide) for v in vectors[0]] + [struct((2 * rows, cols), low)] * 2
-    return call(body, [mine, got], shapes, bits=bits, after=after, limit=8, cost=115, far_out=range(len(vectors[0])))
-
-
-def join_sides(left, left_got, right, right_got, bits, after=()):
-    rows, cols = left.shape
-
-    def body(b, l, lg, r, rg, lo, ro):
-        place(lo, l, lg, b[BIT1])
-        place(ro, r, rg, b[BIT0])
-
-    return whole_call(body, [left, left_got, right, right_got], [(2 * rows, cols)] * 2, bits, after)
-
-
-def join_half(left, left_got, right, right_got, bits, after=()):
-    rows, cols = left.shape
-
-    def body(b, l, lg, r, rg, out):
-        place(out.at[:, pl.ds(0, cols)], l, lg, b[BIT0])
-        place(out.at[:, pl.ds(cols, cols)], r, rg, b[BIT1])
-
-    return whole_call(body, [left, left_got, right, right_got], [(2 * rows, 2 * cols)], bits, after)[0]
-
-
-def widen(source, which, before, widths, bits, after=()):
-    half, n = source.shape
+    shapes = [struct((v,), wide) for v in lengths] + [struct((rows, mine.shape[1]), low)]
+    return whole_call(body, [mine, got], shapes, bits, after, far_out=range(len(lengths)))
+
+
+def join(mine, got, bit, bits, after=()):
+    rows, cols = mine.shape
+
+    def body(b, m, g, out):
+        out[pl.ds(pl.multiple_of(b[bit] * rows, rows), rows), :] = m[...]
+        out[pl.ds(pl.multiple_of((1 - b[bit]) * rows, rows), rows), :] = g[...]
+
+    return whole_call(body, [mine, got], [struct((2 * rows, cols), low)], bits, after)
+
+
+def widen(source, which, targets, before, bits, after=()):
+    half = source.shape[0]
     parts = 4
     tile = half // parts
+    old = [(i, a) for i, a in enumerate(before) if a is not None]
 
     def body(b, src, *refs):
-        refs = refs[0 if before is None else len(before) :]
-        outs, token, bufs, sems = refs[: len(widths)], refs[len(widths)], refs[len(widths) + 1 : -1], refs[-1]
+        refs = refs[len(old) :]
+        n = len(targets)
+        outs, token, bufs, sems = refs[:n], refs[n], refs[n + 1 : -1], refs[-1]
         token[...] = jnp.zeros_like(token)
         start = (1 - b[CORE] if which else b[CORE]) * half
         copies = []
         for t in range(parts):
             at = 0
-            for out, buf, w in zip(outs, bufs, widths):
-                buf[t] = src[t * tile : (t + 1) * tile, at : at + w].astype(wide)
+            for out, buf, (_, first, size) in zip(outs, bufs, targets):
+                buf[t] = src[t * tile : (t + 1) * tile, at : at + size].astype(wide)
                 rows = pl.ds(pl.multiple_of(start + t * tile, tile), tile)
-                copies.append(pltpu.make_async_copy(buf.at[t], out.at[rows, :], sems.at[len(copies)]))
+                copies.append(pltpu.make_async_copy(buf.at[t], out.at[rows, pl.ds(first, size)], sems.at[len(copies)]))
                 copies[-1].start()
-                at += w
+                at += size
         for copy in copies:
             copy.wait()
 
     return call(
         body,
-        [source] + list(before or []),
-        [struct((2 * half, w), wide) for w in widths] + [struct((8, 128), wide)],
+        [source] + [a for _, a in old],
+        [struct(shape, wide) for shape, _, _ in targets] + [struct((8, 128), wide)],
         bits=bits,
-        scratch=[pltpu.VMEM((parts, tile, w), wide) for w in widths] + [pltpu.SemaphoreType.DMA((parts * len(widths),))],
-        aliases={1 + i: i for i in range(len(widths))} if before else None,
+        scratch=[pltpu.VMEM((parts, tile, size), wide) for _, _, size in targets]
+        + [pltpu.SemaphoreType.DMA((parts * len(targets),))],
+        aliases={1 + k: i for k, (i, _) in enumerate(old)},
         after=after,
-        far=range(1, 1 + len(widths)) if before else (),
-        hand_out=range(len(widths)),
+        far=range(1, 1 + len(old)),
+        hand_out=range(len(targets)),
         limit=12,
-        cost=115,
+        cost=690,
     )
 
 
 class Reduction:
-    def __init__(self, src, widths, bits, clock, tail, vectors=()):
-        self.vectors = vectors
-        self.src, self.widths, self.bits, self.clock, self.tail = src, widths, bits, clock, tail
+    def __init__(self, src, order, targets, outs, bits, clock, tail, lengths=()):
+        self.src, self.order, self.targets, self.outs = src, order, targets, outs
+        self.bits, self.clock, self.tail, self.lengths = bits, clock, tail, lengths
+        self.extra = SMALL if src.small else 0
 
     def step(self, fn, *args):
-        out = fn(*args, after=self.clock.now())
-        self.clock.set(out[-1] if isinstance(out, (list, tuple)) else out)
+        out = fn(*args, self.bits, after=self.clock.now())
+        self.clock.set(out[-1])
         return out
 
     def core_send(self):
-        send, *kept = self.step(gradient_rows, self.src, self.bits, None)
-        if kept:
-            self.src.kept = kept[0]
-        self.got = exchange(send, "stream", 1)
+        send, *self.kept = self.step(gradient_to_send, self.src)
+        self.got = cross(send)
 
     def core_sum(self):
-        ls, self.l, rs, self.r = self.step(gradient_rows, self.src, self.bits, self.got)
-        self.gl, self.gr = exchange(ls, "dp", 1), exchange(rs, "dp", 2)
+        out = gradient_sum(
+            self.src, self.bits, self.got, self.kept[0] if self.kept else None, self.order[0], after=self.clock.now()
+        )
+        self.clock.set(out[-1])
+        self.v = out[1]
+        self.got = exchange(out[0], MASKS[self.order[0]])
+
+    def halve(self, i):
+        send, self.v = self.step(halve, self.v, self.got, self.order[i], self.extra)
+        self.got = exchange(send, MASKS[self.order[i]])
 
     def first_sum(self):
-        ls, self.l, rs, self.r = self.step(halve_sides, self.l, self.gl, self.r, self.gr, self.bits)
-        self.gl, self.gr = exchange(ls, "dp", 2), exchange(rs, "dp", 1)
+        self.halve(1)
 
     def second_sum(self):
-        send, self.v = self.step(halve_both, self.l, self.gl, self.r, self.gr, self.bits)
-        self.got = exchange(send, "dp", 4)
+        self.halve(2)
 
     def third_sum(self):
-        self.v = self.step(add_up, self.v, self.got, self.bits)
-        self.got = exchange(self.v, "dp", self.tail[0])
+        for mask in self.tail:
+            (self.v,) = self.step(add_up, self.v, self.got)
+            self.got = exchange(self.v, (mask, mask))
 
     def last_sum(self):
-        for mask in self.tail[1:]:
-            self.v = self.step(add_up, self.v, self.got, self.bits)
-            self.got = exchange(self.v, "dp", mask)
-        self.v = self.step(add_up, self.v, self.got, self.bits)
-        self.got = exchange(self.v, "dp", 4)
+        if self.extra:
+            *self.sums, self.v = self.step(add_last, self.v, self.got, self.lengths, self.src.small[0].shape[1])
+        else:
+            (self.v,) = self.step(add_up, self.v, self.got)
+        self.got = exchange(self.v, MASKS[self.order[2]])
+
+    def join(self, i):
+        (self.v,) = self.step(join, self.v, self.got, self.order[i])
+        self.got = exchange(self.v, MASKS[self.order[i - 1]]) if i else cross(self.v)
 
     def third_back(self):
-        vectors = self.vectors, self.src.small[0].shape[1] if self.src.small else None
-        *self.sums, self.l, self.r = self.step(join_both, self.v, self.got, self.src.m // 16, vectors, self.bits)
-        self.gl, self.gr = exchange(self.l, "dp", 2), exchange(self.r, "dp", 1)
+        self.join(2)
 
     def second_back(self):
-        self.l, self.r = self.step(join_sides, self.l, self.gl, self.r, self.gr, self.bits)
-        self.gl, self.gr = exchange(self.l, "dp", 1), exchange(self.r, "dp", 2)
+        self.join(1)
 
     def first_back(self):
-        self.v = self.step(join_half, self.l, self.gl, self.r, self.gr, self.bits)
-        self.got = exchange(self.v, "stream", 1)
+        self.join(0)
+
+    def write(self, which, source):
+        before = [self.outs.get(name) for name, *_ in self.targets]
+        *arrays, _ = self.step(widen, source, which, [t[1:] for t in self.targets], before)
+        for (name, *_), array in zip(self.targets, arrays):
+            self.outs[name] = array
 
     def finish_own(self):
-        self.out = self.step(widen, self.v, 0, None, self.widths, self.bits)[:-1]
+        self.write(0, self.v)
 
     def finish(self):
-        return self.step(widen, self.got, 1, self.out, self.widths, self.bits)[:-1]
+        self.write(1, self.got)
 
 
 class Clock:
@@ -788,7 +778,8 @@
     ffn = w_in.shape[1]
     dp = lax.axis_size("dp")
     stream, place_dp = lax.axis_index("stream"), lax.axis_index("dp")
-    bits = jnp.stack([stream, place_dp & 1, (place_dp >> 1) & 1, (place_dp >> 2) & 1, place_dp]).astype(jnp.int32)
+    first, second = (place_dp >> stream) & 1, (place_dp >> (1 - stream)) & 1
+    bits = jnp.stack([stream, first, second, (place_dp >> 2) & 1, place_dp]).astype(jnp.int32)
     later = [
         w_in, w_down, seq_cotangent[0], w_pool, b_in, b_down, ln2_gain, ln2_bias, b_pool, pair_ids
     ]
@@ -807,14 +798,14 @@
     order = [inv_two]
     for low_bit in range(0, len(masks), 2):
         span = 4 if low_bit + 1 < len(masks) else 2
-        blocks = [gathered] + [exchange(gathered, "dp", i << low_bit) for i in range(1, span)]
+        blocks = [gathered] + [exchange(gathered, (i << low_bit,) * 2) for i in range(1, span)]
         if group < SEQ // GROUP:
             state = ffn_group(group, hid3, cot3, upper, state, after=order)
             group += 1
             order = [state[-1]]
         gathered = put_in_order(blocks, bits, low_bit, order)
         order = [gathered]
-    other = exchange(gathered, "stream", 1)
+    other = cross(gathered)
     while group < SEQ // GROUP:
         state = ffn_group(group, hid3, cot3, upper, state, after=order)
         group += 1
@@ -829,70 +820,93 @@
     clock = Clock(small_up)
     act, gate, two = (v.reshape(tokens, -1) for v in (act, gate, two))
     tail = masks[3:]
-    down = Reduction(Sources([(act, two)]), [width], bits, clock, tail)
-    into = Reduction(Sources([(hidden_low, gate)]), [ffn], bits, clock, tail)
+    outs = {}
+    shape_of = {"down": (ffn, width), "into": (width, ffn), "qkv": (width, 3 * width), "out": (width, width)}
+
+    def target(name, first, size):
+        return name, shape_of[name], first, size
+
+    plain, third_first = (FIRST, SECOND, THIRD), (THIRD, FIRST, SECOND)
+    rest = (outs, bits, clock, tail)
+    down = Reduction(Sources([(act, two, 0, width)]), plain, [target("down", 0, width)], *rest)
+    into = Reduction(Sources([(hidden_low, gate, 0, ffn)]), third_first, [target("into", 0, ffn)], *rest)
+    lower = (two, gate, hidden, inv_one, proj, probs, w_in, w_out, ln1_gain, ln1_bias)
+
+    def lower_reductions(grad_one, grad_proj, small_low, bqv):
+        edge, end = 2 * width, 3 * width
+        lengths = (width, width, width, ffn, width, width, width, 2 * width)
+        part_a = Sources([(x, grad_proj, 0, edge)], [small_up, bin_sum, small_low, bqv])
+        part_b = Sources([(x, grad_proj, edge, end), (context, grad_one, 0, width)])
+        return (
+            Reduction(part_a, plain, [target("qkv", 0, edge)], *rest, lengths),
+            Reduction(part_b, plain, [target("qkv", edge, end - edge), target("out", 0, width)], *rest),
+        )
+
+    into.core_send()
     down.core_send()
-    into.core_send()
+    into.core_sum()
     down.core_sum()
-    lower = (two, gate, hidden, inv_one, proj, probs, w_in, w_out, ln1_gain, ln1_bias)
     state = lower_backward(0, 2, *lower, after=clock.now())
     clock.set(state[-1])
     state = lower_backward(1, 2, *lower, before=state, after=clock.now())
     grad_one, grad_proj, small_low, bqv = state
     clock.set(bqv)
+    lower_a, lower_b = lower_reductions(grad_one, grad_proj, small_low, bqv)
     down.first_sum()
-    into.core_sum()
-    low_part = Reduction(
-        Sources([(x, grad_proj), (context, grad_one)], [small_up, bin_sum, small_low, bqv]),
-        [3 * width, width],
-        bits,
-        clock,
-        tail,
-        (width, width, width, ffn, width, width, width, 2 * width),
-    )
+    lower_a.core_send()
+    into.first_sum()
     down.second_sum()
-    low_part.core_send()
+    lower_a.core_sum()
+    into.second_sum()
     down.third_sum()
-    into.first_sum()
-    low_part.core_sum()
-    into.second_sum()
-    down.last_sum()
+    lower_b.core_send()
+    lower_a.first_sum()
+    lower_b.core_sum()
+    into.third_sum()
+    lower_a.second_sum()
     grad_input, token = input_gradient(grad_proj, w_qkv, grad_one, after=clock.now())
     clock.set(token)
-    low_part.first_sum()
-    into.third_sum()
+    down.last_sum()
+    lower_b.first_sum()
+    lower_a.third_sum()
+    into.last_sum()
     down.third_back()
-    low_part.second_sum()
+    lower_b.second_sum()
+    into.third_back()
+    lower_b.third_sum()
     down.second_back()
-    into.last_sum()
-    low_part.third_sum()
-    into.third_back()
+    lower_a.last_sum()
+    lower_b.last_sum()
+    into.second_back()
+    lower_a.third_back()
+    lower_b.third_back()
     down.first_back()
+    lower_a.second_back()
     down.finish_own()
-    into.second_back()
-    low_part.last_sum()
-    (out_down,) = down.finish()
-    low_part.third_back()
+    lower_b.second_back()
+    down.finish()
+    lower_a.first_back()
+    lower_a.finish_own()
+    lower_a.finish()
+    lower_b.first_back()
     into.first_back()
+    lower_b.finish_own()
     into.finish_own()
-    low_part.second_back()
-    (out_in,) = into.finish()
-    low_part.first_back()
-    low_part.finish_own()
-    out_qkv, out_out = low_part.finish()
-    g_ln2_gain, g_ln2_bias, g_b_down, g_b_in, g_ln1_gain, g_ln1_bias, g_b_out, g_b_qv = low_part.sums
+    lower_b.finish()
+    into.finish()
+    g_ln2_gain, g_ln2_bias, g_b_down, g_b_in, g_ln1_gain, g_ln1_bias, g_b_out, g_b_qv = lower_a.sums
     return (
         enc.reshape(1, tokens, width),
         grad_input[None],
-        out_qkv,
+        outs["qkv"],
         g_b_qv,
-        out_out,
+        outs["out"],
         g_b_out,
         g_ln1_gain,
         g_ln1_bias,
-        out_in,
+        outs["into"],
         g_b_in,
-        out_down,
+        outs["down"],
         g_b_down,
         g_ln2_gain,
         g_ln2_bias,

time: 253 us -> 232 us (0.917)
  waiting for transfers between devices: 68.3 us -> 54.4 us
  local copies, waits for them, and re-layouts: 6.9 us -> 0.16 us
  Pallas kernels: 123 us -> 129 us
  starting transfers between devices: 49.2 us -> 43.2 us
    ppermute x46 -> x43, waiting for transfers between devices: 68.3 us -> 54.4 us  [the longest x34 51.2 us: exchange(): return lax.ppermute(a, ('stream', 'dp'), pairs)]
    unnamed x34 -> x30, local copies, waits for them, and re-layouts: 6.82 us -> 0.07 us
    ppermute x46 -> x43, starting transfers between devices: 49.2 us -> 43.2 us  [the longest x34 41.6 us: exchange(): return lax.ppermute(a, ('stream', 'dp'), pairs)]
    pallas_call x45 -> x56, Pallas kernels: 123 us -> 129 us  [call(): pl.pallas_call(wrapped, in_specs=[SMEM] * first + [HBM if i in far else V...]
  transfers between devices with their start and end apart: 46 -> 43, of which waited for: 23 -> 21; matrix products, arithmetic and copies ran while one was open for 0% -> 0% of each run, Pallas kernels for 34% -> 40%
where the time goes in v5:
time: 232 us; the launch traced here: 228 us
  Pallas kernels  129 us (56%)
  waiting for transfers between devices  54.4 us (23%)
  starting transfers between devices  43.2 us (19%)
    pallas_call x56, Pallas kernels, call(): pl.pallas_call(wrapped, in_specs=[SMEM] * first + [HBM if i in far else V...  129 us
    ppermute x34, waiting for transfers between devices, exchange(): return lax.ppermute(a, ('stream', 'dp'), pairs)  51.2 us
    ppermute x34, starting transfers between devices, exchange(): return lax.ppermute(a, ('stream', 'dp'), pairs)  41.6 us
  transfers between devices with their start and end apart: 43, of which 21 were waited for; matrix products, arithmetic and copies ran while one was open for 0% of the time, Pallas kernels for 40%

profile of v5, /device:TPU:0, one launch (start us, length us, event | category | flops | bytes accessed | tf_op | source)
XLA Modules:
  0.0 228.4 jit_solution(17215564385598095216)
XLA Ops:
  0.7 13.9 %shard_map.288 = (bf16[1024,2304]{1,0:T(8,128)(2,1)S(1)}, bf16[1024,768]{1,0:T(8,128)(2,1)S(1)}, bf16[1024,768]{1,0:T(8,128)(2,1)S(1)}, f32[1024,768]{1,0:T(8,12...) custom-call(s32[5]{0:T(128)S(1)} %stack.23.refs_0_, ...), custom_call_target="tpu_custom_call" | custom-call | flops 9200000000 | tf_op jit(solution)/shard_map/pallas_call | solution.py:42
  14.7 4.6 %shard_map.289 = (bf16[16,64,768]{2,1,0:T(8,128)(2,1)}, bf16[16,64,3072]{2,1,0:T(8,128)(2,1)S(1)}, bf16[256,3072]{1,0:T(8,128)(2,1)S(1)}, bf16[256,3072]{1,0:T(8...) custom-call(f32[16,64,768]{2,1,0:T(8,128)S(1)} %bitcast.25, ...), custom_call_target="tpu_custom_call" | custom-call | flops 9200000000 | tf_op jit(solution)/shard_map/pallas_call | solution.py:42
  19.3 4.0 %collective-permute-start.2 = (bf16[16,768]{1,0:T(8,128)(2,1)S(1)}, bf16[16,768]{1,0:T(8,128)(2,1)S(1)}, u32[]{:S(2)}, u32[]{:S(2)}) collective-permute-start(bf16[16,768]{1,0:T(8,128)(2,1)S(1)} %get-tuple-element.143.refs_1_), channel_id=1, source_target_pairs={{0,3},{1,2},{2,1},{3,0},{4,7},{5,6},{6,5},{7,4},{8,11},{9,10},{10,... | collective-permute-start | bytes 73736 | tf_op jit(solution)/shard_map/ppermute | solution.py:512
  23.9 5.7 %shard_map.290 = (bf16[16,64,768]{2,1,0:T(8,128)(2,1)}, bf16[16,64,3072]{2,1,0:T(8,128)(2,1)S(1)}, bf16[16,64,3072]{2,1,0:T(8,128)(2,1)S(1)}, bf16[16,64,768]{2,...) custom-call(f32[16,64,768]{2,1,0:T(8,128)S(1)} %bitcast.26, ...), custom_call_target="tpu_custom_call", output_to_operand_aliasing={{0}: (8, {}), {1}: (9, {})} | custom-call | flops 9200000000 | tf_op jit(solution)/shard_map/pallas_call | solution.py:42
  30.2 4.1 %collective-permute-start.5 = (bf16[64,768]{1,0:T(8,128)(2,1)S(1)}, bf16[64,768]{1,0:T(8,128)(2,1)S(1)}, u32[]{:S(2)}, u32[]{:S(2)}) collective-permute-start(bf16[64,768]{1,0:T(8,128)(2,1)S(1)} %shard_map.291.refs_14_.refs_1_), channel_id=1, source_target_pairs={{0,12},{1,13},{2,14},{3,15},{4,8},{5,9},{6,10},{7,11},{8,4},{9,5},... | collective-permute-start | bytes 294920 | tf_op jit(solution)/shard_map/ppermute | solution.py:512
  34.9 6.1 %shard_map.292 = (bf16[16,64,768]{2,1,0:T(8,128)(2,1)}, bf16[16,64,3072]{2,1,0:T(8,128)(2,1)S(1)}, bf16[16,64,3072]{2,1,0:T(8,128)(2,1)S(1)}, bf16[16,64,768]{2,...) custom-call(f32[16,64,768]{2,1,0:T(8,128)S(1)} %bitcast.27, ...), custom_call_target="tpu_custom_call", output_to_operand_aliasing={{0}: (8, {}), {1}: (9, {}), {2}: (10, {}), {3}: (11, {})} | custom-call | flops 9200000000 | tf_op jit(solution)/shard_map/pallas_call | solution.py:42
  42.4 5.7 %shard_map.294 = (bf16[16,64,768]{2,1,0:T(8,128)(2,1)}, bf16[16,64,3072]{2,1,0:T(8,128)(2,1)S(1)}, bf16[16,64,3072]{2,1,0:T(8,128)(2,1)S(1)}, bf16[16,64,768]{2,...) custom-call(f32[16,64,768]{2,1,0:T(8,128)S(1)} %bitcast.28, ...), custom_call_target="tpu_custom_call", output_to_operand_aliasing={{0}: (8, {}), {1}: (9, {}), {2}: (10, {}), {3}: (11, {})} | custom-call | flops 9200000000 | tf_op jit(solution)/shard_map/pallas_call | solution.py:42
  48.1 5.3 %shard_map.295 = (f32[16,768]{1,0:T(8,128)S(1)}, f32[768,768]{1,0:T(8,128)}, f32[768]{0:T(1024)}) custom-call(s32[5]{0:T(128)S(1)} %stack.23.refs_0_, bf16[256,768]{1,0:T(8,128)(2,1)S(1)} %shard_map.293.refs_14_.refs_1_, bf16[256,768]{1,0:T(8,128)(2,1)S(1)} %collective-permute-done.6.refs_2_, s32[256]{0:T(256)S(1)} %get-tuple-element.151.refs_3_, ...), custom_call_target="tpu_custom_call" | custom-call | flops 9200000000 | tf_op jit(solution)/shard_map/pallas_call | solution.py:42
  53.4 2.1 shard_map.296
  55.4 3.4 %shard_map.297.refs_3_ = bf16[384,3072]{1,0:T(8,128)(2,1)S(1)} custom-call(s32[5]{0:T(128)S(1)} %stack.23.refs_0_, bf16[1024,768]{1,0:T(8,128)(2,1)S(1)} %get-tuple-element.168.refs_1_, bf16[1024,3072]{1,0:T(8,128)(2,1)S(1)} %bitcast.19, f32[8,768]{1,0:T(8,128)S(1)} %get-tuple-element.169.refs_3_), custom_call_target="tpu_custom_call" | custom-call | flops 9200000000 | tf_op jit(solution)/shard_map/pallas_call | solution.py:42
  59.4 3.3 %shard_map.298.refs_4_ = bf16[1536,768]{1,0:T(8,128)(2,1)S(1)} custom-call(s32[5]{0:T(128)S(1)} %stack.23.refs_0_, bf16[1024,3072]{1,0:T(8,128)(2,1)S(1)} %bitcast.23, bf16[1024,768]{1,0:T(8,128)(2,1)S(1)} %bitcast.33, bf16[384,3072]{1,0:T(8,128)(2,1)S(1)} %shard_map.297.refs_3_), custom_call_target="tpu_custom_call" | custom-call | flops 9200000000 | tf_op jit(solution)/shard_map/pallas_call | solution.py:42
  63.5 3.5 %shard_map.299 = (bf16[192,3072]{1,0:T(8,128)(2,1)S(1)}, bf16[192,3072]{1,0:T(8,128)(2,1)S(1)}) custom-call(s32[5]{0:T(128)S(1)} %stack.23.refs_0_, bf16[1024,768]{1,0:T(8,128)(2,1)S(1)} %copy-done.10, bf16[1024,3072]{1,0:T(8,128)(2,1)S(1)} %bitcast.20, bf16[384,3072]{1,0:T(8,128)(2,1)S(1)} %collective-permute-done.8.refs_3_, ...), custom_call_target="tpu_custom_call" | custom-call | flops 9200000000 | tf_op jit(solution)/shard_map/pallas_call | solution.py:42
  67.3 3.6 %shard_map.300 = (bf16[768,768]{1,0:T(8,128)(2,1)S(1)}, bf16[768,768]{1,0:T(8,128)(2,1)S(1)}) custom-call(s32[5]{0:T(128)S(1)} %stack.23.refs_0_, bf16[1024,3072]{1,0:T(8,128)(2,1)S(1)} %bitcast.24, bf16[1024,768]{1,0:T(8,128)(2,1)S(1)} %bitcast.34, bf16[1536,768]{1,0:T(8,128)(2,1)S(1)} %collective-permute-done.7.refs_3_, ...), custom_call_target="tpu_custom_call" | custom-call | flops 9200000000 | tf_op jit(solution)/shard_map/pallas_call | solution.py:42
  73.3 8.2 %shard_map.301 = (bf16[1024,768]{1,0:T(8,128)(2,1)S(1)}, bf16[1024,2304]{1,0:T(8,128)(2,1)S(1)}, f32[8,768]{1,0:T(8,128)S(1)}, f32[8,768]{1,0:T(8,128)S(1)}) custom-call(bf16[1024,768]{1,0:T(8,128)(2,1)S(1)} %bitcast.35, bf16[1024,3072]{1,0:T(8,128)(2,1)S(1)} %bitcast.21, f32[1024,768]{1,0:T(8,128)S(1)} %get-tuple-element.126.refs_2_, ...), custom_call_target="tpu_custom_call" | custom-call | flops 9200000000 | tf_op jit(solution)/shard_map/pallas_call | solution.py:42
  81.5 8.0 %shard_map.302 = (bf16[1024,768]{1,0:T(8,128)(2,1)S(1)}, bf16[1024,2304]{1,0:T(8,128)(2,1)S(1)}, f32[8,768]{1,0:T(8,128)S(1)}, f32[8,768]{1,0:T(8,128)S(1)}) custom-call(bf16[1024,768]{1,0:T(8,128)(2,1)S(1)} %bitcast.36, bf16[1024,3072]{1,0:T(8,128)(2,1)S(1)} %bitcast.22, ...), custom_call_target="tpu_custom_call", output_to_operand_aliasing={{0}: (10, {}), {1}: (11, {})} | custom-call | flops 9200000000 | tf_op jit(solution)/shard_map/pallas_call | solution.py:42
  94.0 6.2 %collective-permute-done.12.refs_2_ = bf16[192,3072]{1,0:T(8,128)(2,1)S(1)} collective-permute-done((bf16[192,3072]{1,0:T(8,128)(2,1)S(1)}, bf16[192,3072]{1,0:T(8,128)(2,1)S(1)}, u32[]{:S(2)}, u32[]{:S(2)}) %collective-permute-start.12) | collective-permute-done | bytes 1179680 | tf_op jit(solution)/shard_map/ppermute | solution.py:512
  105.6 2.1 shard_map.307
  107.6 3.4 %collective-permute-done.15.refs_2_ = bf16[96,3072]{1,0:T(8,128)(2,1)S(1)} collective-permute-done((bf16[96,3072]{1,0:T(8,128)(2,1)S(1)}, bf16[96,3072]{1,0:T(8,128)(2,1)S(1)}, u32[]{:S(2)}, u32[]{:S(2)}) %collective-permute-start.15) | collective-permute-done | bytes 589856 | tf_op jit(solution)/shard_map/ppermute | solution.py:512
  118.5 7.4 %collective-permute-done.13.refs_2_ = bf16[208,1536]{1,0:T(8,128)(2,1)S(1)} collective-permute-done((bf16[208,1536]{1,0:T(8,128)(2,1)S(1)}, bf16[208,1536]{1,0:T(8,128)(2,1)S(1)}, u32[]{:S(2)}, u32[]{:S(2)}) %collective-permute-start.13) | collective-permute-done | bytes 639008 | tf_op jit(solution)/shard_map/ppermute | solution.py:512
  127.6 2.9 %shard_map.312 = (bf16[192,1536]{1,0:T(8,128)(2,1)S(1)}, bf16[192,1536]{1,0:T(8,128)(2,1)S(1)}) custom-call(s32[5]{0:T(128)S(1)} %stack.23.refs_0_, bf16[1024,768]{1,0:T(8,128)(2,1)S(1)} %bitcast.18, bf16[1024,2304]{1,0:T(8,128)(2,1)S(1)} %get-tuple-element.176.refs_2_.refs_0_, bf16[1024,768]{1,0:T(8,128)(2,1)S(1)} %copy-done.8, ...), custom_call_target="tpu_custom_call" | custom-call | flops 9200000000 | tf_op jit(solution)/shard_map/pallas_call | solution.py:42
  134.5 5.0 %shard_map.315 = (bf16[1024,768]{1,0:T(8,128)(2,1)}, f32[8,128]{1,0:T(8,128)S(1)}) custom-call(bf16[1024,2304]{1,0:T(8,128)(2,1)S(1)} %get-tuple-element.176.refs_2_.refs_0_, bf16[768,2304]{1,0:T(8,128)(2,1)S(1)} %copy-done, bf16[1024,768]{1,0:T(8,128)(2,1)S(1)} %get-tuple-element.177.refs_4_.refs_2_, bf16[64,1536]{1,0:T(8,128)(2,1)S(1)} %get-tuple-element.199.refs_3_.refs_1_), custom_call_target="tpu_custom_call" | custom-call | flops 9200000000 | tf_op jit(solution)/shard_map/pallas_call | solution.py:42
  143.2 7.9 %collective-permute-done.19.refs_2_ = bf16[192,1536]{1,0:T(8,128)(2,1)S(1)} collective-permute-done((bf16[192,1536]{1,0:T(8,128)(2,1)S(1)}, bf16[192,1536]{1,0:T(8,128)(2,1)S(1)}, u32[]{:S(2)}, u32[]{:S(2)}) %collective-permute-start.19) | collective-permute-done | bytes 589856 | tf_op jit(solution)/shard_map/ppermute | solution.py:512
  155.5 2.5 %collective-permute-done.22.refs_2_ = bf16[192,768]{1,0:T(8,128)(2,1)S(1)} collective-permute-done((bf16[192,768]{1,0:T(8,128)(2,1)S(1)}, bf16[192,768]{1,0:T(8,128)(2,1)S(1)}, u32[]{:S(2)}, u32[]{:S(2)}) %collective-permute-start.22) | collective-permute-done | bytes 294944 | tf_op jit(solution)/shard_map/ppermute | solution.py:512
  160.2 2.3 %collective-permute-start.25 = (bf16[48,1536]{1,0:T(8,128)(2,1)S(1)}, bf16[48,1536]{1,0:T(8,128)(2,1)S(1)}, u32[]{:S(2)}, u32[]{:S(2)}) collective-permute-start(bf16[48,1536]{1,0:T(8,128)(2,1)S(1)} %get-tuple-element.207), channel_id=1, source_target_pairs={{0,4},{1,5},{2,6},{3,7},{4,0},{5,1},{6,2},{7,3},{8,12},{9,13},{10,... | collective-permute-start | bytes 442376 | tf_op jit(solution)/shard_map/ppermute | solution.py:512
  168.6 4.8 %collective-permute-done.29.refs_2_ = bf16[384,768]{1,0:T(8,128)(2,1)S(1)} collective-permute-done((bf16[384,768]{1,0:T(8,128)(2,1)S(1)}, bf16[384,768]{1,0:T(8,128)(2,1)S(1)}, u32[]{:S(2)}, u32[]{:S(2)}) %collective-permute-start.29) | collective-permute-done | bytes 589856 | tf_op jit(solution)/shard_map/ppermute | solution.py:512
  174.1 2.3 collective-permute-start.34
  188.8 8.1 %collective-permute-done.34.refs_2_ = bf16[768,768]{1,0:T(8,128)(2,1)S(1)} collective-permute-done((bf16[768,768]{1,0:T(8,128)(2,1)S(1)}, bf16[768,768]{1,0:T(8,128)(2,1)S(1)}, u32[]{:S(2)}, u32[]{:S(2)}) %collective-permute-start.34) | collective-permute-done | bytes 1179680 | tf_op jit(solution)/shard_map/ppermute | solution.py:512
  198.3 2.1 collective-permute-start.37
  200.3 2.8 %shard_map.332 = (f32[3072,768]{1,0:T(8,128)}, f32[8,128]{1,0:T(8,128)S(1)}) custom-call(s32[5]{0:T(128)S(1)} %stack.23.refs_0_, bf16[1536,768]{1,0:T(8,128)(2,1)S(1)} %shard_map.330.refs_3_.refs_1_, bf16[192,1536]{1,0:T(8,128)(2,1)S(1)} %shard_map.331.refs_2_.refs_1_), custom_call_target="tpu_custom_call" | custom-call | flops 13799999488 | tf_op jit(solution)/shard_map/pallas_call | solution.py:42
  203.9 2.8 %shard_map.334 = (f32[3072,768]{1,0:T(8,128)}, f32[8,128]{1,0:T(8,128)S(1)}) custom-call(s32[5]{0:T(128)S(1)} %stack.23.refs_0_, bf16[1536,768]{1,0:T(8,128)(2,1)S(1)} %collective-permute-done.38.refs_1_, f32[3072,768]{1,0:T(8,128)} %get-tuple-element.210.refs_2_, bf16[192,1536]{1,0:T(8,128)(2,1)S(1)} %shard_map.333.refs_3_.refs_1_), custom_call_target="tpu_custom_call", output_to_operand_aliasing={{0}: (2, {})} | custom-call | flops 13799999488 | tf_op jit(solution)/shard_map/pallas_call | solution.py:42
  219.6 2.8 %shard_map.341 = (f32[768,3072]{1,0:T(8,128)}, f32[8,128]{1,0:T(8,128)S(1)}) custom-call(s32[5]{0:T(128)S(1)} %stack.23.refs_0_, bf16[384,3072]{1,0:T(8,128)(2,1)S(1)} %shard_map.339.refs_3_.refs_1_, f32[8,128]{1,0:T(8,128)S(1)} %get-tuple-element.218.refs_2_), custom_call_target="tpu_custom_call" | custom-call | flops 13799999488 | tf_op jit(solution)/shard_map/pallas_call | solution.py:42
  224.5 3.4 %shard_map.343 = (f32[768,3072]{1,0:T(8,128)}, f32[8,128]{1,0:T(8,128)}) custom-call(s32[5]{0:T(128)S(1)} %stack.23.refs_0_, bf16[384,3072]{1,0:T(8,128)(2,1)S(1)} %collective-permute-done.42.refs_1_, f32[768,3072]{1,0:T(8,128)} %get-tuple-element.226.refs_2_, f32[8,128]{1,0:T(8,128)S(1)} %get-tuple-element.227.refs_3_), custom_call_target="tpu_custom_call", output_to_operand_aliasing={{0}: (2, {})} | custom-call | flops 13799999488 | tf_op jit(solution)/shard_map/pallas_call | solution.py:42
  (143 shorter events, 76.4 us)
Async XLA Ops:
  19.3 10.3 %collective-permute-start.2 = (bf16[16,768]{1,0:T(8,128)(2,1)S(1)}, bf16[16,768]{1,0:T(8,128)(2,1)S(1)}, u32[]{:S(2)}, u32[]{:S(2)}) collective-permute-start(bf16[16,768]{1,0:T(8,128)(2,1)S(1)} %get-tuple-element.143.refs_1_), channel_id=1, source_target_pairs={{0,3},{1,2},{2,1},{3,0},{4,7},{5,6},{6,5},{7,4},{8,11},{9,10},{10,... | collective-permute-start | bytes 73736 | tf_op jit(solution)/shard_map/ppermute | solution.py:512
  30.2 10.9 %collective-permute-start.5 = (bf16[64,768]{1,0:T(8,128)(2,1)S(1)}, bf16[64,768]{1,0:T(8,128)(2,1)S(1)}, u32[]{:S(2)}, u32[]{:S(2)}) collective-permute-start(bf16[64,768]{1,0:T(8,128)(2,1)S(1)} %shard_map.291.refs_14_.refs_1_), channel_id=1, source_target_pairs={{0,12},{1,13},{2,14},{3,15},{4,8},{5,9},{6,10},{7,11},{8,4},{9,5},... | collective-permute-start | bytes 294920 | tf_op jit(solution)/shard_map/ppermute | solution.py:512
  34.3 7.4 %collective-permute-start.4 = (bf16[64,768]{1,0:T(8,128)(2,1)S(1)}, bf16[64,768]{1,0:T(8,128)(2,1)S(1)}, u32[]{:S(2)}, u32[]{:S(2)}) collective-permute-start(bf16[64,768]{1,0:T(8,128)(2,1)S(1)} %shard_map.291.refs_14_.refs_1_), channel_id=1, source_target_pairs={{0,8},{1,9},{2,10},{3,11},{4,12},{5,13},{6,14},{7,15},{8,0},{9,1},... | collective-permute-start | bytes 294920 | tf_op jit(solution)/shard_map/ppermute | solution.py:512
  34.3 7.4 %collective-permute-start.3 = (bf16[64,768]{1,0:T(8,128)(2,1)S(1)}, bf16[64,768]{1,0:T(8,128)(2,1)S(1)}, u32[]{:S(2)}, u32[]{:S(2)}) collective-permute-start(bf16[64,768]{1,0:T(8,128)(2,1)S(1)} %shard_map.291.refs_14_.refs_1_), channel_id=1, source_target_pairs={{0,4},{1,5},{2,6},{3,7},{4,0},{5,1},{6,2},{7,3},{8,12},{9,13},{10,... | collective-permute-start | bytes 294920 | tf_op jit(solution)/shard_map/ppermute | solution.py:512
  70.9 18.6 %collective-permute-start.9 = (bf16[768,768]{1,0:T(8,128)(2,1)S(1)}, bf16[768,768]{1,0:T(8,128)(2,1)S(1)}, u32[]{:S(2)}, u32[]{:S(2)}) collective-permute-start(bf16[768,768]{1,0:T(8,128)(2,1)S(1)} %get-tuple-element.181), channel_id=1, source_target_pairs={{0,1},{1,0},{2,3},{3,2},{4,5},{5,4},{6,7},{7,6},{8,9},{9,8},{10,11... | collective-permute-start | bytes 3538952 | tf_op jit(solution)/shard_map/ppermute | solution.py:512
  72.5 27.7 %collective-permute-start.12 = (bf16[192,3072]{1,0:T(8,128)(2,1)S(1)}, bf16[192,3072]{1,0:T(8,128)(2,1)S(1)}, u32[]{:S(2)}, u32[]{:S(2)}) collective-permute-start(bf16[192,3072]{1,0:T(8,128)(2,1)S(1)} %get-tuple-element.186), channel_id=1, source_target_pairs={{0,4},{1,5},{2,6},{3,7},{4,0},{5,1},{6,2},{7,3},{8,12},{9,13},{10,... | collective-permute-start | bytes 3538952 | tf_op jit(solution)/shard_map/ppermute | solution.py:512
  90.4 12.2 %collective-permute-start.11 = (bf16[384,768]{1,0:T(8,128)(2,1)S(1)}, bf16[384,768]{1,0:T(8,128)(2,1)S(1)}, u32[]{:S(2)}, u32[]{:S(2)}) collective-permute-start(bf16[384,768]{1,0:T(8,128)(2,1)S(1)} %get-tuple-element.185), channel_id=1, source_target_pairs={{0,2},{1,3},{2,0},{3,1},{4,6},{5,7},{6,4},{7,5},{8,10},{9,11},{10,... | collective-permute-start | bytes 1769480 | tf_op jit(solution)/shard_map/ppermute | solution.py:512
  101.1 9.9 %collective-permute-start.15 = (bf16[96,3072]{1,0:T(8,128)(2,1)S(1)}, bf16[96,3072]{1,0:T(8,128)(2,1)S(1)}, u32[]{:S(2)}, u32[]{:S(2)}) collective-permute-start(bf16[96,3072]{1,0:T(8,128)(2,1)S(1)} %get-tuple-element.193), channel_id=1, source_target_pairs={{0,1},{1,0},{2,3},{3,2},{4,5},{5,4},{6,7},{7,6},{8,9},{9,8},{10,11... | collective-permute-start | bytes 1769480 | tf_op jit(solution)/shard_map/ppermute | solution.py:512
  103.3 9.5 %collective-permute-start.14 = (bf16[192,768]{1,0:T(8,128)(2,1)S(1)}, bf16[192,768]{1,0:T(8,128)(2,1)S(1)}, u32[]{:S(2)}, u32[]{:S(2)}) collective-permute-start(bf16[192,768]{1,0:T(8,128)(2,1)S(1)} %get-tuple-element.192), channel_id=1, source_target_pairs={{0,4},{1,5},{2,6},{3,7},{4,0},{5,1},{6,2},{7,3},{8,12},{9,13},{10,... | collective-permute-start | bytes 884744 | tf_op jit(solution)/shard_map/ppermute | solution.py:512
  111.7 18.8 %collective-permute-start.17 = (bf16[48,3072]{1,0:T(8,128)(2,1)S(1)}, bf16[48,3072]{1,0:T(8,128)(2,1)S(1)}, u32[]{:S(2)}, u32[]{:S(2)}) collective-permute-start(bf16[48,3072]{1,0:T(8,128)(2,1)S(1)} %get-tuple-element.197), channel_id=1, source_target_pairs={{0,2},{1,3},{2,0},{3,1},{4,6},{5,7},{6,4},{7,5},{8,10},{9,11},{10,... | collective-permute-start | bytes 884744 | tf_op jit(solution)/shard_map/ppermute | solution.py:512
  113.4 28.8 %collective-permute-start.20 = (bf16[192,768]{1,0:T(8,128)(2,1)S(1)}, bf16[192,768]{1,0:T(8,128)(2,1)S(1)}, u32[]{:S(2)}, u32[]{:S(2)}) collective-permute-start(bf16[192,768]{1,0:T(8,128)(2,1)S(1)} %shard_map.309.refs_5_.refs_1_), channel_id=1, source_target_pairs={{0,8},{1,9},{2,10},{3,11},{4,12},{5,13},{6,14},{7,15},{8,0},{9,1},... | collective-permute-start | bytes 884744 | tf_op jit(solution)/shard_map/ppermute | solution.py:512
  115.5 10.4 %collective-permute-start.13 = (bf16[208,1536]{1,0:T(8,128)(2,1)S(1)}, bf16[208,1536]{1,0:T(8,128)(2,1)S(1)}, u32[]{:S(2)}, u32[]{:S(2)}) collective-permute-start(bf16[208,1536]{1,0:T(8,128)(2,1)S(1)} %get-tuple-element.190), channel_id=1, source_target_pairs={{0,1},{1,0},{2,3},{3,2},{4,5},{5,4},{6,7},{7,6},{8,9},{9,8},{10,11... | collective-permute-start | bytes 1916936 | tf_op jit(solution)/shard_map/ppermute | solution.py:512
  118.4 9.2 %collective-permute-start.18 = (bf16[384,1536]{1,0:T(8,128)(2,1)S(1)}, bf16[384,1536]{1,0:T(8,128)(2,1)S(1)}, u32[]{:S(2)}, u32[]{:S(2)}) collective-permute-start(bf16[384,1536]{1,0:T(8,128)(2,1)S(1)} %shard_map.310.refs_3_), channel_id=1, source_target_pairs={{0,16},{16,0},{1,17},{17,1},{2,18},{18,2},{3,19},{19,3},{4,20},{20... | collective-permute-start | bytes 3538952 | tf_op jit(solution)/shard_map/ppermute | solution.py:516
  126.6 7.3 %collective-permute-start.16 = (bf16[112,1536]{1,0:T(8,128)(2,1)S(1)}, bf16[112,1536]{1,0:T(8,128)(2,1)S(1)}, u32[]{:S(2)}, u32[]{:S(2)}) collective-permute-start(bf16[112,1536]{1,0:T(8,128)(2,1)S(1)} %get-tuple-element.196), channel_id=1, source_target_pairs={{0,2},{1,3},{2,0},{3,1},{4,6},{5,7},{6,4},{7,5},{8,10},{9,11},{10,... | collective-permute-start | bytes 1032200 | tf_op jit(solution)/shard_map/ppermute | solution.py:512
  131.2 22.7 %collective-permute-start.23 = (bf16[48,3072]{1,0:T(8,128)(2,1)S(1)}, bf16[48,3072]{1,0:T(8,128)(2,1)S(1)}, u32[]{:S(2)}, u32[]{:S(2)}) collective-permute-start(bf16[48,3072]{1,0:T(8,128)(2,1)S(1)} %shard_map.313.refs_3_.refs_1_), channel_id=1, source_target_pairs={{0,8},{1,9},{2,10},{3,11},{4,12},{5,13},{6,14},{7,15},{8,0},{9,1},... | collective-permute-start | bytes 884744 | tf_op jit(solution)/shard_map/ppermute | solution.py:512
  139.5 12.3 %collective-permute-start.24 = (bf16[64,1536]{1,0:T(8,128)(2,1)S(1)}, bf16[64,1536]{1,0:T(8,128)(2,1)S(1)}, u32[]{:S(2)}, u32[]{:S(2)}) collective-permute-start(bf16[64,1536]{1,0:T(8,128)(2,1)S(1)} %get-tuple-element.205), channel_id=1, source_target_pairs={{0,4},{1,5},{2,6},{3,7},{4,0},{5,1},{6,2},{7,3},{8,12},{9,13},{10,... | collective-permute-start | bytes 589832 | tf_op jit(solution)/shard_map/ppermute | solution.py:512
  141.3 9.9 %collective-permute-start.19 = (bf16[192,1536]{1,0:T(8,128)(2,1)S(1)}, bf16[192,1536]{1,0:T(8,128)(2,1)S(1)}, u32[]{:S(2)}, u32[]{:S(2)}) collective-permute-start(bf16[192,1536]{1,0:T(8,128)(2,1)S(1)} %get-tuple-element.201), channel_id=1, source_target_pairs={{0,1},{1,0},{2,3},{3,2},{4,5},{5,4},{6,7},{7,6},{8,9},{9,8},{10,11... | collective-permute-start | bytes 1769480 | tf_op jit(solution)/shard_map/ppermute | solution.py:512
  142.8 15.1 %collective-permute-start.22 = (bf16[192,768]{1,0:T(8,128)(2,1)S(1)}, bf16[192,768]{1,0:T(8,128)(2,1)S(1)}, u32[]{:S(2)}, u32[]{:S(2)}) collective-permute-start(bf16[192,768]{1,0:T(8,128)(2,1)S(1)} %shard_map.316.refs_3_.refs_1_), channel_id=1, source_target_pairs={{0,4},{1,5},{2,6},{3,7},{4,0},{5,1},{6,2},{7,3},{8,12},{9,13},{10,... | collective-permute-start | bytes 884744 | tf_op jit(solution)/shard_map/ppermute | solution.py:512
  152.4 23.9 %collective-permute-start.28 = (bf16[64,1536]{1,0:T(8,128)(2,1)S(1)}, bf16[64,1536]{1,0:T(8,128)(2,1)S(1)}, u32[]{:S(2)}, u32[]{:S(2)}) collective-permute-start(bf16[64,1536]{1,0:T(8,128)(2,1)S(1)} %shard_map.318.refs_3_.refs_1_), channel_id=1, source_target_pairs={{0,8},{1,9},{2,10},{3,11},{4,12},{5,13},{6,14},{7,15},{8,0},{9,1},... | collective-permute-start | bytes 589832 | tf_op jit(solution)/shard_map/ppermute | solution.py:512
  154.5 8.2 %collective-permute-start.26 = (bf16[48,3072]{1,0:T(8,128)(2,1)S(1)}, bf16[48,3072]{1,0:T(8,128)(2,1)S(1)}, u32[]{:S(2)}, u32[]{:S(2)}) collective-permute-start(bf16[48,3072]{1,0:T(8,128)(2,1)S(1)} %shard_map.319.refs_3_.refs_1_), channel_id=1, source_target_pairs={{0,2},{1,3},{2,0},{3,1},{4,6},{5,7},{6,4},{7,5},{8,10},{9,11},{10,... | collective-permute-start | bytes 884744 | tf_op jit(solution)/shard_map/ppermute | solution.py:512
  158.6 14.9 %collective-permute-start.29 = (bf16[384,768]{1,0:T(8,128)(2,1)S(1)}, bf16[384,768]{1,0:T(8,128)(2,1)S(1)}, u32[]{:S(2)}, u32[]{:S(2)}) collective-permute-start(bf16[384,768]{1,0:T(8,128)(2,1)S(1)} %shard_map.320.refs_3_.refs_1_), channel_id=1, source_target_pairs={{0,2},{1,3},{2,0},{3,1},{4,6},{5,7},{6,4},{7,5},{8,10},{9,11},{10,... | collective-permute-start | bytes 1769480 | tf_op jit(solution)/shard_map/ppermute | solution.py:512
  163.3 16.9 %collective-permute-start.32 = (bf16[96,3072]{1,0:T(8,128)(2,1)S(1)}, bf16[96,3072]{1,0:T(8,128)(2,1)S(1)}, u32[]{:S(2)}, u32[]{:S(2)}) collective-permute-start(bf16[96,3072]{1,0:T(8,128)(2,1)S(1)} %shard_map.322.refs_3_.refs_1_), channel_id=1, source_target_pairs={{0,1},{1,0},{2,3},{3,2},{4,5},{5,4},{6,7},{7,6},{8,9},{9,8},{10,11... | collective-permute-start | bytes 1769480 | tf_op jit(solution)/shard_map/ppermute | solution.py:512
  166.9 11.2 %collective-permute-start.27 = (bf16[48,1536]{1,0:T(8,128)(2,1)S(1)}, bf16[48,1536]{1,0:T(8,128)(2,1)S(1)}, u32[]{:S(2)}, u32[]{:S(2)}) collective-permute-start(bf16[48,1536]{1,0:T(8,128)(2,1)S(1)} %shard_map.323.refs_3_.refs_1_), channel_id=1, source_target_pairs={{0,8},{1,9},{2,10},{3,11},{4,12},{5,13},{6,14},{7,15},{8,0},{9,1},... | collective-permute-start | bytes 442376 | tf_op jit(solution)/shard_map/ppermute | solution.py:512
  174.1 22.8 %collective-permute-start.34 = (bf16[768,768]{1,0:T(8,128)(2,1)S(1)}, bf16[768,768]{1,0:T(8,128)(2,1)S(1)}, u32[]{:S(2)}, u32[]{:S(2)}) collective-permute-start(bf16[768,768]{1,0:T(8,128)(2,1)S(1)} %shard_map.324.refs_3_.refs_1_), channel_id=1, source_target_pairs={{0,1},{1,0},{2,3},{3,2},{4,5},{5,4},{6,7},{7,6},{8,9},{9,8},{10,11... | collective-permute-start | bytes 3538952 | tf_op jit(solution)/shard_map/ppermute | solution.py:512
  178.7 8.7 %collective-permute-start.30 = (bf16[48,1536]{1,0:T(8,128)(2,1)S(1)}, bf16[48,1536]{1,0:T(8,128)(2,1)S(1)}, u32[]{:S(2)}, u32[]{:S(2)}) collective-permute-start(bf16[48,1536]{1,0:T(8,128)(2,1)S(1)} %shard_map.326.refs_3_.refs_1_), channel_id=1, source_target_pairs={{0,4},{1,5},{2,6},{3,7},{4,0},{5,1},{6,2},{7,3},{8,12},{9,13},{10,... | collective-permute-start | bytes 442376 | tf_op jit(solution)/shard_map/ppermute | solution.py:512
  181.9 33.4 %collective-permute-start.41 = (bf16[192,3072]{1,0:T(8,128)(2,1)}, bf16[192,3072]{1,0:T(8,128)(2,1)}, u32[]{:S(2)}, u32[]{:S(2)}) collective-permute-start(bf16[192,3072]{1,0:T(8,128)(2,1)} %shard_map.327.refs_3_.refs_1_), channel_id=1, source_target_pairs={{0,4},{1,5},{2,6},{3,7},{4,0},{5,1},{6,2},{7,3},{8,12},{9,13},{10,... | collective-permute-start | bytes 3538952 | tf_op jit(solution)/shard_map/ppermute | solution.py:512
  184.8 12.8 %collective-permute-start.35 = (bf16[96,1536]{1,0:T(8,128)(2,1)S(1)}, bf16[96,1536]{1,0:T(8,128)(2,1)S(1)}, u32[]{:S(2)}, u32[]{:S(2)}) collective-permute-start(bf16[96,1536]{1,0:T(8,128)(2,1)S(1)} %shard_map.328.refs_3_.refs_1_), channel_id=1, source_target_pairs={{0,2},{1,3},{2,0},{3,1},{4,6},{5,7},{6,4},{7,5},{8,10},{9,11},{10,... | collective-permute-start | bytes 884744 | tf_op jit(solution)/shard_map/ppermute | solution.py:512
  188.0 15.2 %collective-permute-start.33 = (bf16[96,1536]{1,0:T(8,128)(2,1)S(1)}, bf16[96,1536]{1,0:T(8,128)(2,1)S(1)}, u32[]{:S(2)}, u32[]{:S(2)}) collective-permute-start(bf16[96,1536]{1,0:T(8,128)(2,1)S(1)} %shard_map.329.refs_3_.refs_1_), channel_id=1, source_target_pairs={{0,2},{1,3},{2,0},{3,1},{4,6},{5,7},{6,4},{7,5},{8,10},{9,11},{10,... | collective-permute-start | bytes 884744 | tf_op jit(solution)/shard_map/ppermute | solution.py:512
  198.3 9.9 %collective-permute-start.37 = (bf16[192,1536]{1,0:T(8,128)(2,1)S(1)}, bf16[192,1536]{1,0:T(8,128)(2,1)S(1)}, u32[]{:S(2)}, u32[]{:S(2)}) collective-permute-start(bf16[192,1536]{1,0:T(8,128)(2,1)S(1)} %shard_map.331.refs_2_.refs_1_), channel_id=1, source_target_pairs={{0,1},{1,0},{2,3},{3,2},{4,5},{5,4},{6,7},{7,6},{8,9},{9,8},{10,11... | collective-permute-start | bytes 1769480 | tf_op jit(solution)/shard_map/ppermute | solution.py:512
  203.8 10.7 %collective-permute-start.36 = (bf16[192,1536]{1,0:T(8,128)(2,1)S(1)}, bf16[192,1536]{1,0:T(8,128)(2,1)S(1)}, u32[]{:S(2)}, u32[]{:S(2)}) collective-permute-start(bf16[192,1536]{1,0:T(8,128)(2,1)S(1)} %shard_map.333.refs_3_.refs_1_), channel_id=1, source_target_pairs={{0,1},{1,0},{2,3},{3,2},{4,5},{5,4},{6,7},{7,6},{8,9},{9,8},{10,11... | collective-permute-start | bytes 1769480 | tf_op jit(solution)/shard_map/ppermute | solution.py:512
  215.2 7.3 %collective-permute-start.40 = (bf16[384,1536]{1,0:T(8,128)(2,1)S(1)}, bf16[384,1536]{1,0:T(8,128)(2,1)S(1)}, u32[]{:S(2)}, u32[]{:S(2)}) collective-permute-start(bf16[384,1536]{1,0:T(8,128)(2,1)S(1)} %shard_map.338.refs_3_.refs_1_), channel_id=1, source_target_pairs={{0,16},{16,0},{1,17},{17,1},{2,18},{18,2},{3,19},{19,3},{4,20},{20... | collective-permute-start | bytes 3538952 | tf_op jit(solution)/shard_map/ppermute | solution.py:516
  217.1 7.5 %collective-permute-start.42 = (bf16[384,3072]{1,0:T(8,128)(2,1)S(1)}, bf16[384,3072]{1,0:T(8,128)(2,1)S(1)}, u32[]{:S(2)}, u32[]{:S(2)}) collective-permute-start(bf16[384,3072]{1,0:T(8,128)(2,1)S(1)} %shard_map.339.refs_3_.refs_1_), channel_id=1, source_target_pairs={{0,16},{16,0},{1,17},{17,1},{2,18},{18,2},{3,19},{19,3},{4,20},{20... | collective-permute-start | bytes 7077896 | tf_op jit(solution)/shard_map/ppermute | solution.py:516
  (26 other events, 199.9 us)
